TPU v7x, 128 devices: a whole 4x4x4 slice. The times are simulated.
128 devices in a mesh: gx: 8 (over z_lo, x), gy: 16 (over y, z_hi, core).
Axes of the slice: x: 4, y: 4, z: 4 (z_hi: 2, z_lo: 2; z = z_hi * 2 + z_lo), core: 2. Of those that a mesh axis runs over, the one named last changes fastest.
Arguments:
- point_feats: bfloat16 [524288, 128], P(('gx', 'gy')), may hold values from -6 to 6
- top_bin: int32 [524288], P(('gx', 'gy')), may hold values from -1 to 131071, as said below
- front_bin: int32 [524288], P(('gx', 'gy')), may hold values from -1 to 16383, as said below
- side_bin: int32 [524288], P(('gx', 'gy')), may hold values from -1 to 8191, as said below
- camera_of_device: int32 [128], P(('gx', 'gy')), may hold values from 0 to 5
- camera_embed: float32 [6, 128], replicated, may hold values from -6 to 6
- w_in: bfloat16 [128, 256], replicated, may hold values from -0.5 to 0.5
- b_in: float32 [256], replicated, may hold values from -6 to 6
- w_out: bfloat16 [256, 128], replicated, may hold values from -0.375 to 0.375
- b_out: float32 [128], replicated, may hold values from -3 to 3
Outputs:
- voxels: bfloat16 [512, 256, 32, 128], P('gx', 'gy')
Inputs may be any that keep to these rules, and one draw needn't show every extreme that they name: For each point, top_bin, front_bin and side_bin are all -1, or all describe the same cell (x, y, z): top_bin = x * 256 + y, front_bin = x * 32 + z, side_bin = y * 32 + z. Of the points of one device, at most 64 lie in the block of x cells [i * 64, (i + 1) * 64) and y cells [j * 16, (j + 1) * 16) of any one pair (i, j); in every draw some such block receives exactly 64 points from every device. `front_bin`: see top_bin. `side_bin`: see top_bin.
All inputs are finite; a program needn't handle non-finite values.
Results may differ from a plain program's by a relative error of at most 0.001.
The roundings to bfloat16 on the way count: a program that leaves them out, or rounds other values in their place, can miss the bound.
Values may be sent and summed in bfloat16 or wider, within the bound.
No kernel may reach another device: no remote copies, remote signals or barrier semaphores. Data moves between devices by JAX's collectives and lax.ppermute only.
A program may use at most 64 MiB of HBM per device.

v0:
```python
import jax
import jax.numpy as jnp
from jax import lax
from jax.sharding import PartitionSpec as P

C = 128
CAMS = 6
NZ = 32
BX = 64
BY = 16
P_DEV = 4096


def per_device(
    point_feats,
    top_bin,
    front_bin,
    side_bin,
    camera_of_device,
    camera_embed,
    w_in,
    b_in,
    w_out,
    b_out,
):
    size_gx = lax.axis_size("gx")
    size_gy = lax.axis_size("gy")
    devices_all = size_gx * size_gy
    capacity = 2 * P_DEV // devices_all
    grid_y_cells = BY * size_gy
    camera_row = jnp.sum(
        jnp.where(jnp.arange(CAMS)[:, None] == camera_of_device[0], camera_embed, 0.0), axis=0
    )
    features = (point_feats.astype(jnp.float32) + camera_row).astype(jnp.bfloat16)
    live = top_bin >= 0
    grid_x = top_bin // grid_y_cells
    grid_y = top_bin % grid_y_cells
    depth = front_bin % NZ
    block_x = grid_x // BX
    block_y = grid_y // BY
    owner = jnp.where(live, block_x * size_gy + block_y, devices_all)
    local_x = grid_x - block_x * BX
    local_y = grid_y - block_y * BY
    cells = jnp.stack([local_x * BY + local_y, local_x * NZ + depth, local_y * NZ + depth], axis=0)
    marks = (owner[:, None] == jnp.arange(devices_all)[None, :]).astype(jnp.int32)
    ranks = jnp.sum((jnp.cumsum(marks, axis=0) - 1) * marks, axis=1)
    target = jnp.where(live, owner * capacity + ranks, devices_all * capacity)
    feat_slots = jnp.zeros((devices_all * capacity + 1, C), jnp.bfloat16).at[target].set(features)
    feat_slots = feat_slots[:-1].reshape(devices_all, capacity, C)
    cell_slots = jnp.full((3, devices_all * capacity + 1), -1, jnp.int32).at[:, target].set(cells)
    cell_slots = jnp.transpose(cell_slots[:, :-1].reshape(3, devices_all, capacity), (1, 0, 2))
    got_feats, got_cells = (
        lax.all_to_all(feat_slots, ("gx", "gy"), split_axis=0, concat_axis=0, tiled=True),
        lax.all_to_all(cell_slots, ("gx", "gy"), split_axis=0, concat_axis=0, tiled=True),
    )
    slots_all = devices_all * capacity
    got_feats = got_feats.reshape(slots_all, C)
    got_cells = jnp.moveaxis(got_cells, 1, 0).reshape(3, slots_all)
    block = min(1024, slots_all)
    turns = slots_all // block

    def splat(turn, planes):
        start = turn * block
        piece = lax.dynamic_slice_in_dim(got_feats, start, block, 0)
        labels = lax.dynamic_slice_in_dim(got_cells, start, block, 1)

        def pool(count, row):
            onehot = (jnp.arange(count, dtype=jnp.int32)[:, None] == row[None, :]).astype(
                jnp.bfloat16
            )
            return jnp.dot(onehot, piece, preferred_element_type=jnp.float32)

        return (
            planes[0] + pool(BX * BY, labels[0]),
            planes[1] + pool(BX * NZ, labels[1]),
            planes[2] + pool(BY * NZ, labels[2]),
        )

    empty = (
        jnp.zeros((BX * BY, C), jnp.float32),
        jnp.zeros((BX * NZ, C), jnp.float32),
        jnp.zeros((BY * NZ, C), jnp.float32),
    )
    top_part, front_part, side_part = lax.fori_loop(0, turns, splat, empty)
    top_plane = top_part.astype(jnp.bfloat16).reshape(BX, BY, C)
    front_plane = lax.psum(front_part, "gy").astype(jnp.bfloat16)
    side_plane = lax.psum(side_part, "gx").astype(jnp.bfloat16)
    front_plane = front_plane.reshape(BX, NZ, C)
    side_plane = side_plane.reshape(BY, NZ, C)

    def mix(parts):
        top_rows, front_rows = parts
        cell = (
            top_rows[:, :, None, :].astype(jnp.float32)
            + front_rows[:, None, :, :].astype(jnp.float32)
            + side_plane[None, :, :, :].astype(jnp.float32)
        ).astype(jnp.bfloat16)
        flat = cell.reshape(-1, C)
        hidden = jax.nn.gelu(
            jnp.dot(flat, w_in, preferred_element_type=jnp.float32) + b_in, approximate=False
        ).astype(jnp.bfloat16)
        result = (
            jnp.dot(hidden, w_out, preferred_element_type=jnp.float32)
            + b_out
            + flat.astype(jnp.float32)
        )
        return result.astype(jnp.bfloat16).reshape(4, BY, NZ, C)

    blocks = lax.map(
        mix, (top_plane.reshape(BX // 4, 4, BY, C), front_plane.reshape(BX // 4, 4, NZ, C))
    )
    return blocks.reshape(BX, BY, NZ, C)


def solution(mesh):
    placed = (
        P(("gx", "gy"), None),
        P(("gx", "gy")),
        P(("gx", "gy")),
        P(("gx", "gy")),
        P(("gx", "gy")),
        P(),
        P(),
        P(),
        P(),
        P(),
    )
    return jax.shard_map(
        per_device, mesh=mesh, in_specs=placed, out_specs=P("gx", "gy", None, None), check_vma=False
    )
```

profile of v0, /device:TPU:0, one launch (start us, length us, event | category | flops | bytes accessed | tf_op | source)
XLA Modules:
  0.0 348.7 jit_solution(6584000969864736604)
XLA Ops:
  1.8 1.2 copy.16
  3.1 1.4 fusion.59
  5.2 12.9 %scatter_custom_fusion = s32[3,8193]{0,1:T(8,128)} fusion(s32[4096]{0:T(1024)S(1)} %compare_select_fusion, s32[4096,3]{1,0:T(8,128)S(1)} %copy.17, s32[]{:T(128)} %constant.175.clone.1), kind=kCustom, calls=%fused_computation.78 | custom fusion | bytes 98320 | tf_op jit(solution)/shard_map/scatter | solution.py:50
  18.1 4.4 %slice.42 = s32[3,8192]{0,1:T(8,128)} slice(s32[3,8193]{0,1:T(8,128)} %scatter_custom_fusion), slice={[0:3], [0:8192]} | slice | bytes 196608 | tf_op jit(solution)/shard_map/slice | solution.py:51
  22.5 3.1 copy.18
  26.5 11.1 %all-to-all-start = ((s32[128,1,192]{2,1,0:T(1,128)}), s32[128,1,192]{2,1,0:T(1,128)S(1)}, u32[]{:S(2)}, u32[]{:S(2)}) async-start(s32[128,1,192]{2,1,0:T(1,128)} %reshape.110), calls=%async_computation | async-start | bytes 262144 | tf_op jit(solution)/shard_map/all_to_all | solution.py:54
  38.4 11.5 %scatter_custom_fusion.1 = bf16[8193,128]{1,0:T(8,128)(2,1)S(1)} fusion(s32[4096]{0:T(1024)S(1)} %compare_select_fusion, bf16[]{:T(256)} %constant.170.clone.1, bf16[4096,128]{1,0:T(8,128)(2,1)S(1)} %copy-done, f32[128]{0:T(128)S(1)} %select_reduce_fusion), kind=kCustom, calls=%fused_computation.88 | custom fusion | flops 1572864 | bytes 3146498 | tf_op jit(solution)/shard_map/scatter | solution.py:48
  49.9 1.5 slice.43
  51.4 9.9 %all-to-all-start.1 = ((bf16[128,64,128]{2,1,0:T(8,128)(2,1)}), bf16[128,64,128]{2,1,0:T(8,128)(2,1)S(1)}, u32[]{:S(2)}, u32[]{:S(2)}) async-start(bf16[128,64,128]{2,1,0:T(8,128)(2,1)} %bitcast.65), calls=%async_computation.1 | async-start | bytes 4194304 | tf_op jit(solution)/shard_map/all_to_all | solution.py:53
  63.8 1.1 reshape.81
  64.8 24.7 %all-to-all-done.1 = bf16[128,64,128]{2,1,0:T(8,128)(2,1)S(1)} async-done(((bf16[128,64,128]{2,1,0:T(8,128)(2,1)}), bf16[128,64,128]{2,1,0:T(8,128)(2,1)S(1)}, u32[]{:S(2)}, u32[]{:S(2)}) %all-to-all-start.1) | async-done | bytes 2097184 | tf_op jit(solution)/shard_map/all_to_all | solution.py:53
  89.5 45.5 %while.29 = (s32[]{:T(128)}, f32[1024,128]{1,0:T(8,128)}, f32[2048,128]{1,0:T(8,128)S(1)}, f32[512,128]{1,0:T(8,128)}, s32[3,8192]{1,0:T(4,128)S(1)}, /*index=5*...) while((s32[]{:T(128)}, f32[1024,128]{1,0:T(8,128)}, ...), condition=%wide.region_7.8_spmd.clone, body=%wide.region_6.7_spmd.clone.sunk | while | flops 944111616 | bytes 6590743 | solution.py:84
  89.6 1.8 fusion.97
  91.4 1.6 fusion.96
  94.4 1.8 fusion.97
  96.2 2.7 fusion.96
  100.2 1.8 fusion.97
  102.0 2.7 fusion.96
  106.0 1.8 fusion.97
  107.8 2.7 fusion.96
  111.8 1.8 fusion.97
  113.6 2.7 fusion.96
  117.6 1.8 fusion.97
  119.4 2.7 fusion.96
  123.5 1.8 fusion.97
  125.3 2.7 fusion.96
  129.3 1.8 fusion.97
  131.1 2.7 fusion.96
  135.0 79.3 %all-reduce.2 = bf16[2048,128]{1,0:T(8,128)(2,1)S(1)} all-reduce(f32[2048,128]{1,0:T(8,128)S(1)} %get-tuple-element.164), channel_id=1, replica_groups=mesh['gx'=8,'gy'=16] {'gy'}, use_global_device_ids=true, to_apply=%region_8.9 | all-reduce | flops 262144 | bytes 1572864 | tf_op jit(solution)/shard_map/psum | solution.py:86
  214.3 35.3 %all-reduce.3 = bf16[512,128]{1,0:T(8,128)(2,1)S(1)} all-reduce(f32[512,128]{1,0:T(8,128)} %get-tuple-element.165), channel_id=1, replica_groups=mesh['gx'=8,'gy'=16] {'gx'}, use_global_device_ids=true, to_apply=%region_9.10 | all-reduce | flops 65536 | bytes 393216 | tf_op jit(solution)/shard_map/psum | solution.py:87
  249.7 1.1 convert_element_type.81
  250.8 97.9 %while.28 = (s32[]{:T(128)}, bf16[16,4,16,32,128]{4,3,2,1,0:T(8,128)(2,1)}, bf16[16,4,16,128]{3,2,1,0:T(8,128)(2,1)S(1)}, bf16[16,4,32,128]{3,2,1,0:T(8,128)(2,1...) while((s32[]{:T(128)}, ...), condition=%wide.region_11.12_spmd, body=%wide.region_10.11_spmd.sunk | while | flops 304963584 | bytes 3655789 | solution.py:109
  251.0 5.1 %fusion.91 = bf16[2048,128]{1,0:T(8,128)(2,1)S(1)} fusion(bf16[256,128]{1,0:T(8,128)(2,1)S(1)} %get-tuple-element.389, bf16[2048,128]{1,0:T(8,128)(2,1)S(1)} %bitcast.63, f32[256]{0:T(256)S(1)} %get-tuple-element.388, bf16[128,256]{1,0:T(8,128)(2,1)S(1)} %get-tuple-element.387, f32[128]{0:T(128)S(1)} %get-tuple-element.390), kind=kOutput, calls=%fused_computation.6.clone.1 | convolution fusion | flops 304087040 | bytes 1181184 | tf_op jit(solution)/shard_map/while/body/eval_jaxpr/dot_general | solution.py:103
  257.1 5.1 %fusion.91 = bf16[2048,128]{1,0:T(8,128)(2,1)S(1)} fusion(bf16[256,128]{1,0:T(8,128)(2,1)S(1)} %get-tuple-element.389, bf16[2048,128]{1,0:T(8,128)(2,1)S(1)} %bitcast.63, f32[256]{0:T(256)S(1)} %get-tuple-element.388, bf16[128,256]{1,0:T(8,128)(2,1)S(1)} %get-tuple-element.387, f32[128]{0:T(128)S(1)} %get-tuple-element.390), kind=kOutput, calls=%fused_computation.6.clone.1 | convolution fusion | flops 304087040 | bytes 1181184 | tf_op jit(solution)/shard_map/while/body/eval_jaxpr/dot_general | solution.py:103
  263.2 5.1 %fusion.91 = bf16[2048,128]{1,0:T(8,128)(2,1)S(1)} fusion(bf16[256,128]{1,0:T(8,128)(2,1)S(1)} %get-tuple-element.389, bf16[2048,128]{1,0:T(8,128)(2,1)S(1)} %bitcast.63, f32[256]{0:T(256)S(1)} %get-tuple-element.388, bf16[128,256]{1,0:T(8,128)(2,1)S(1)} %get-tuple-element.387, f32[128]{0:T(128)S(1)} %get-tuple-element.390), kind=kOutput, calls=%fused_computation.6.clone.1 | convolution fusion | flops 304087040 | bytes 1181184 | tf_op jit(solution)/shard_map/while/body/eval_jaxpr/dot_general | solution.py:103
  269.3 5.1 %fusion.91 = bf16[2048,128]{1,0:T(8,128)(2,1)S(1)} fusion(bf16[256,128]{1,0:T(8,128)(2,1)S(1)} %get-tuple-element.389, bf16[2048,128]{1,0:T(8,128)(2,1)S(1)} %bitcast.63, f32[256]{0:T(256)S(1)} %get-tuple-element.388, bf16[128,256]{1,0:T(8,128)(2,1)S(1)} %get-tuple-element.387, f32[128]{0:T(128)S(1)} %get-tuple-element.390), kind=kOutput, calls=%fused_computation.6.clone.1 | convolution fusion | flops 304087040 | bytes 1181184 | tf_op jit(solution)/shard_map/while/body/eval_jaxpr/dot_general | solution.py:103
  275.5 5.1 %fusion.91 = bf16[2048,128]{1,0:T(8,128)(2,1)S(1)} fusion(bf16[256,128]{1,0:T(8,128)(2,1)S(1)} %get-tuple-element.389, bf16[2048,128]{1,0:T(8,128)(2,1)S(1)} %bitcast.63, f32[256]{0:T(256)S(1)} %get-tuple-element.388, bf16[128,256]{1,0:T(8,128)(2,1)S(1)} %get-tuple-element.387, f32[128]{0:T(128)S(1)} %get-tuple-element.390), kind=kOutput, calls=%fused_computation.6.clone.1 | convolution fusion | flops 304087040 | bytes 1181184 | tf_op jit(solution)/shard_map/while/body/eval_jaxpr/dot_general | solution.py:103
  281.6 5.1 %fusion.91 = bf16[2048,128]{1,0:T(8,128)(2,1)S(1)} fusion(bf16[256,128]{1,0:T(8,128)(2,1)S(1)} %get-tuple-element.389, bf16[2048,128]{1,0:T(8,128)(2,1)S(1)} %bitcast.63, f32[256]{0:T(256)S(1)} %get-tuple-element.388, bf16[128,256]{1,0:T(8,128)(2,1)S(1)} %get-tuple-element.387, f32[128]{0:T(128)S(1)} %get-tuple-element.390), kind=kOutput, calls=%fused_computation.6.clone.1 | convolution fusion | flops 304087040 | bytes 1181184 | tf_op jit(solution)/shard_map/while/body/eval_jaxpr/dot_general | solution.py:103
  287.7 5.1 %fusion.91 = bf16[2048,128]{1,0:T(8,128)(2,1)S(1)} fusion(bf16[256,128]{1,0:T(8,128)(2,1)S(1)} %get-tuple-element.389, bf16[2048,128]{1,0:T(8,128)(2,1)S(1)} %bitcast.63, f32[256]{0:T(256)S(1)} %get-tuple-element.388, bf16[128,256]{1,0:T(8,128)(2,1)S(1)} %get-tuple-element.387, f32[128]{0:T(128)S(1)} %get-tuple-element.390), kind=kOutput, calls=%fused_computation.6.clone.1 | convolution fusion | flops 304087040 | bytes 1181184 | tf_op jit(solution)/shard_map/while/body/eval_jaxpr/dot_general | solution.py:103
  293.8 5.1 %fusion.91 = bf16[2048,128]{1,0:T(8,128)(2,1)S(1)} fusion(bf16[256,128]{1,0:T(8,128)(2,1)S(1)} %get-tuple-element.389, bf16[2048,128]{1,0:T(8,128)(2,1)S(1)} %bitcast.63, f32[256]{0:T(256)S(1)} %get-tuple-element.388, bf16[128,256]{1,0:T(8,128)(2,1)S(1)} %get-tuple-element.387, f32[128]{0:T(128)S(1)} %get-tuple-element.390), kind=kOutput, calls=%fused_computation.6.clone.1 | convolution fusion | flops 304087040 | bytes 1181184 | tf_op jit(solution)/shard_map/while/body/eval_jaxpr/dot_general | solution.py:103
  299.9 5.1 %fusion.91 = bf16[2048,128]{1,0:T(8,128)(2,1)S(1)} fusion(bf16[256,128]{1,0:T(8,128)(2,1)S(1)} %get-tuple-element.389, bf16[2048,128]{1,0:T(8,128)(2,1)S(1)} %bitcast.63, f32[256]{0:T(256)S(1)} %get-tuple-element.388, bf16[128,256]{1,0:T(8,128)(2,1)S(1)} %get-tuple-element.387, f32[128]{0:T(128)S(1)} %get-tuple-element.390), kind=kOutput, calls=%fused_computation.6.clone.1 | convolution fusion | flops 304087040 | bytes 1181184 | tf_op jit(solution)/shard_map/while/body/eval_jaxpr/dot_general | solution.py:103
  306.0 5.1 %fusion.91 = bf16[2048,128]{1,0:T(8,128)(2,1)S(1)} fusion(bf16[256,128]{1,0:T(8,128)(2,1)S(1)} %get-tuple-element.389, bf16[2048,128]{1,0:T(8,128)(2,1)S(1)} %bitcast.63, f32[256]{0:T(256)S(1)} %get-tuple-element.388, bf16[128,256]{1,0:T(8,128)(2,1)S(1)} %get-tuple-element.387, f32[128]{0:T(128)S(1)} %get-tuple-element.390), kind=kOutput, calls=%fused_computation.6.clone.1 | convolution fusion | flops 304087040 | bytes 1181184 | tf_op jit(solution)/shard_map/while/body/eval_jaxpr/dot_general | solution.py:103
  312.2 5.1 %fusion.91 = bf16[2048,128]{1,0:T(8,128)(2,1)S(1)} fusion(bf16[256,128]{1,0:T(8,128)(2,1)S(1)} %get-tuple-element.389, bf16[2048,128]{1,0:T(8,128)(2,1)S(1)} %bitcast.63, f32[256]{0:T(256)S(1)} %get-tuple-element.388, bf16[128,256]{1,0:T(8,128)(2,1)S(1)} %get-tuple-element.387, f32[128]{0:T(128)S(1)} %get-tuple-element.390), kind=kOutput, calls=%fused_computation.6.clone.1 | convolution fusion | flops 304087040 | bytes 1181184 | tf_op jit(solution)/shard_map/while/body/eval_jaxpr/dot_general | solution.py:103
  318.3 5.1 %fusion.91 = bf16[2048,128]{1,0:T(8,128)(2,1)S(1)} fusion(bf16[256,128]{1,0:T(8,128)(2,1)S(1)} %get-tuple-element.389, bf16[2048,128]{1,0:T(8,128)(2,1)S(1)} %bitcast.63, f32[256]{0:T(256)S(1)} %get-tuple-element.388, bf16[128,256]{1,0:T(8,128)(2,1)S(1)} %get-tuple-element.387, f32[128]{0:T(128)S(1)} %get-tuple-element.390), kind=kOutput, calls=%fused_computation.6.clone.1 | convolution fusion | flops 304087040 | bytes 1181184 | tf_op jit(solution)/shard_map/while/body/eval_jaxpr/dot_general | solution.py:103
  324.4 5.1 %fusion.91 = bf16[2048,128]{1,0:T(8,128)(2,1)S(1)} fusion(bf16[256,128]{1,0:T(8,128)(2,1)S(1)} %get-tuple-element.389, bf16[2048,128]{1,0:T(8,128)(2,1)S(1)} %bitcast.63, f32[256]{0:T(256)S(1)} %get-tuple-element.388, bf16[128,256]{1,0:T(8,128)(2,1)S(1)} %get-tuple-element.387, f32[128]{0:T(128)S(1)} %get-tuple-element.390), kind=kOutput, calls=%fused_computation.6.clone.1 | convolution fusion | flops 304087040 | bytes 1181184 | tf_op jit(solution)/shard_map/while/body/eval_jaxpr/dot_general | solution.py:103
  330.5 5.1 %fusion.91 = bf16[2048,128]{1,0:T(8,128)(2,1)S(1)} fusion(bf16[256,128]{1,0:T(8,128)(2,1)S(1)} %get-tuple-element.389, bf16[2048,128]{1,0:T(8,128)(2,1)S(1)} %bitcast.63, f32[256]{0:T(256)S(1)} %get-tuple-element.388, bf16[128,256]{1,0:T(8,128)(2,1)S(1)} %get-tuple-element.387, f32[128]{0:T(128)S(1)} %get-tuple-element.390), kind=kOutput, calls=%fused_computation.6.clone.1 | convolution fusion | flops 304087040 | bytes 1181184 | tf_op jit(solution)/shard_map/while/body/eval_jaxpr/dot_general | solution.py:103
  336.6 5.1 %fusion.91 = bf16[2048,128]{1,0:T(8,128)(2,1)S(1)} fusion(bf16[256,128]{1,0:T(8,128)(2,1)S(1)} %get-tuple-element.389, bf16[2048,128]{1,0:T(8,128)(2,1)S(1)} %bitcast.63, f32[256]{0:T(256)S(1)} %get-tuple-element.388, bf16[128,256]{1,0:T(8,128)(2,1)S(1)} %get-tuple-element.387, f32[128]{0:T(128)S(1)} %get-tuple-element.390), kind=kOutput, calls=%fused_computation.6.clone.1 | convolution fusion | flops 304087040 | bytes 1181184 | tf_op jit(solution)/shard_map/while/body/eval_jaxpr/dot_general | solution.py:103
  342.7 5.1 %fusion.91 = bf16[2048,128]{1,0:T(8,128)(2,1)S(1)} fusion(bf16[256,128]{1,0:T(8,128)(2,1)S(1)} %get-tuple-element.389, bf16[2048,128]{1,0:T(8,128)(2,1)S(1)} %bitcast.63, f32[256]{0:T(256)S(1)} %get-tuple-element.388, bf16[128,256]{1,0:T(8,128)(2,1)S(1)} %get-tuple-element.387, f32[128]{0:T(128)S(1)} %get-tuple-element.390), kind=kOutput, calls=%fused_computation.6.clone.1 | convolution fusion | flops 304087040 | bytes 1181184 | tf_op jit(solution)/shard_map/while/body/eval_jaxpr/dot_general | solution.py:103
  (162 shorter events, 32.1 us)
Async XLA Ops:
  22.5 15.8 %copy-start.3 = (f32[6,128]{1,0:T(8,128)S(1)}, f32[6,128]{1,0:T(8,128)}, u32[]{:S(2)}) copy-start(f32[6,128]{1,0:T(8,128)} %param.18) | copy-start | bytes 9220
  22.5 15.9 %copy-start = (bf16[4096,128]{1,0:T(8,128)(2,1)S(1)}, bf16[4096,128]{1,0:T(8,128)(2,1)}, u32[]{:S(2)}) copy-start(bf16[4096,128]{1,0:T(8,128)(2,1)} %param.14) | copy-start | bytes 3145732
  26.5 24.9 %all-to-all-start = ((s32[128,1,192]{2,1,0:T(1,128)}), s32[128,1,192]{2,1,0:T(1,128)S(1)}, u32[]{:S(2)}, u32[]{:S(2)}) async-start(s32[128,1,192]{2,1,0:T(1,128)} %reshape.110), calls=%async_computation | async-start | bytes 262144 | tf_op jit(solution)/shard_map/all_to_all | solution.py:54
  51.4 38.1 %all-to-all-start.1 = ((bf16[128,64,128]{2,1,0:T(8,128)(2,1)}), bf16[128,64,128]{2,1,0:T(8,128)(2,1)S(1)}, u32[]{:S(2)}, u32[]{:S(2)}) async-start(bf16[128,64,128]{2,1,0:T(8,128)(2,1)} %bitcast.65), calls=%async_computation.1 | async-start | bytes 4194304 | tf_op jit(solution)/shard_map/all_to_all | solution.py:53
  91.4 1.6 copy-start.1
  93.6 0.7 copy-start.2
  96.1 2.7 copy-start.1
  99.4 0.7 copy-start.2
  102.0 2.7 copy-start.1
  105.2 0.7 copy-start.2
  107.8 2.7 copy-start.1
  111.0 0.7 copy-start.2
  113.6 2.7 copy-start.1
  116.9 0.7 copy-start.2
  119.4 2.7 copy-start.1
  122.7 0.7 copy-start.2
  125.3 2.7 copy-start.1
  128.5 0.7 copy-start.2
  131.1 2.7 copy-start.1
  134.3 0.7 copy-start.2
  135.0 115.7 %copy-start.4 = (bf16[128,256]{1,0:T(8,128)(2,1)S(1)}, bf16[128,256]{1,0:T(8,128)(2,1)}, u32[]{:S(2)}) copy-start(bf16[128,256]{1,0:T(8,128)(2,1)} %param.19) | copy-start | bytes 196612
  135.0 115.7 %copy-start.5 = (bf16[256,128]{1,0:T(8,128)(2,1)S(1)}, bf16[256,128]{1,0:T(8,128)(2,1)}, u32[]{:S(2)}) copy-start(bf16[256,128]{1,0:T(8,128)(2,1)} %param.21) | copy-start | bytes 196612
  135.0 115.7 %copy-start.6 = (f32[256]{0:T(256)S(1)}, f32[256]{0:T(256)}, u32[]{:S(2)}) copy-start(f32[256]{0:T(256)} %param.20) | copy-start | bytes 3076
  135.0 115.7 %copy-start.7 = (f32[128]{0:T(128)S(1)}, f32[128]{0:T(128)}, u32[]{:S(2)}) copy-start(f32[128]{0:T(128)} %param.22) | copy-start | bytes 1540
where the time goes:
time: 349 us
  matrix products  121 us (35%)
  blocking collectives  115 us (33%)
  local copies, waits for them, and re-layouts  46.8 us (13%)
  waiting for transfers between devices  24.7 us (7%)
  starting transfers between devices  21.1 us (6%)
  other arithmetic  19.3 us (6%)
    dot_general x16, matrix products, mix(): jnp.dot(hidden, w_out, preferred_element_type=jnp.float32) + b_out  81.6 us
    psum x1, blocking collectives, per_device(): front_plane = lax.psum(front_part, 'gy').astype(jnp.bfloat16)  79.3 us
    dot_general x24, matrix products, pool(): return jnp.dot(onehot, piece, preferred_element_type=jnp.float32)  39 us
    psum x1, blocking collectives, per_device(): side_plane = lax.psum(side_part, 'gx').astype(jnp.bfloat16)  35.3 us
    all_to_all x1, waiting for transfers between devices, per_device(): lax.all_to_all(feat_slots, ('gx', 'gy'), split_axis=0, concat_axis=0, til...  24.7 us
    dynamic_update_slice x16, local copies, waits for them, and re-layouts, per_device(): lax.map(mix, (top_plane.reshape(BX // 4, 4, BY, C), front_plane.reshape(B...  13.4 us
    scatter x1, local copies, waits for them, and re-layouts, per_device(): jnp.full((3, devices_all * capacity + 1), -1, jnp.int32).at[:, target]  12.9 us
    scatter x1, other arithmetic, per_device(): jnp.zeros((devices_all * capacity + 1, C), jnp.bfloat16).at[target]  11.5 us
  transfers between devices with their start and end apart: 2, of which 1 were waited for; matrix products, arithmetic and copies ran while one was open for 5% of the time, Pallas kernels for 0%

commit v1 on v0

v1 whole, which is shorter than its diff:
```python
import jax
import jax.numpy as jnp
from jax import lax
from jax.experimental import pallas as pl
from jax.experimental.pallas import tpu as pltpu
from jax.sharding import PartitionSpec as P

C = 128
HID = 256
CAMS = 6
NZ = 32
BX = 64
BY = 16
P_DEV = 4096
DEVICES = 128
N_GX = 8
N_GY = 16
CAP = 64
ROWS = CAP + 8
SLOTS = DEVICES * CAP
CHUNKS = P_DEV // 128
PAIRS = DEVICES // 2

F32 = jnp.float32
BF16 = jnp.bfloat16
VMEM_LIMIT = 48 * 2**20


def iota(shape, axis):
    return lax.broadcasted_iota(jnp.int32, shape, axis)


def columns_of(row):
    diagonal = jnp.where(iota((128, 128), 0) == iota((128, 128), 1), row, 0.0).astype(BF16)
    return jnp.dot(diagonal, jnp.ones((128, 128), BF16), preferred_element_type=F32)


def split_columns(values, half):
    zero = jnp.zeros_like(values)
    return jnp.concatenate(
        [jnp.where(half < 0.5, values, zero), jnp.where(half < 0.5, zero, values)], axis=1
    )


def onehot_block(labels_ref, block, chunks):
    base = (block * 256).astype(F32) if not isinstance(block, int) else float(block * 256)
    numbers = iota((256, 128), 0).astype(F32).astype(BF16)
    one = jnp.ones((256, 128), BF16)
    zero = jnp.zeros((256, 128), BF16)
    pieces = []
    for k in range(chunks):
        label = labels_ref[pl.ds(k, 1), :] - base
        label = jnp.where((label >= 0.0) & (label < 256.0), label, -1.0)
        label = jnp.broadcast_to(label, (256, 128)).astype(BF16)
        pieces.append(jnp.where(label == numbers, one, zero))
    return jnp.concatenate(pieces, axis=1)


def pack_kernel(cam_ref, feats_ref, top_ref, front_ref, embed_ref, out_ref, rank_ref, label_ref, half_ref, rhs_ref, meta_ref):
    top = top_ref[...]
    live = top >= 0
    grid_x = top >> 8
    grid_y = top & 255
    owner = jnp.where(live, (grid_x >> 6) * N_GY + (grid_y >> 4), -1)
    local_x = (grid_x & (BX - 1)).astype(F32) + 1.0
    local_y = (grid_y & (BY - 1)).astype(F32) + 1.0
    depth = (front_ref[...] & (NZ - 1)).astype(F32) + 1.0

    before = iota((128, 256), 0) < iota((128, 256), 1)
    later = iota((128, 256), 1) >= 128
    counter = jnp.where(before | later, 1.0, 0.0).astype(BF16)
    seen = jnp.zeros((DEVICES, 128), F32)
    meta = jnp.zeros((DEVICES, 3 * 128), F32)
    slot_of_row = (iota((128, 128), 0) & (CAP - 1)).astype(F32)
    for k in range(CHUNKS):
        mine = iota((DEVICES, 128), 0) == owner[k : k + 1, :]
        marks = jnp.where(mine, 1.0, 0.0).astype(BF16)
        counts = jnp.dot(marks, counter, preferred_element_type=F32)
        rank = jnp.sum(jnp.where(mine, counts[:, :128] + seen, 0.0), axis=0, keepdims=True)
        seen = seen + counts[:, 128:]
        rank_ref[pl.ds(k, 1), :] = rank
        here = slot_of_row == rank
        values = jnp.concatenate(
            [
                jnp.where(here, local_x[k : k + 1, :], 0.0),
                jnp.where(here, local_y[k : k + 1, :], 0.0),
                jnp.where(here, depth[k : k + 1, :], 0.0),
            ],
            axis=0,
        ).astype(BF16)
        meta = meta + lax.dot_general(
            marks, values, (((1,), (1,)), ((), ())), preferred_element_type=F32
        )
    rank = rank_ref[...].astype(jnp.int32)
    label_ref[...] = jnp.where(live, owner * (CAP // 2) + (rank & (CAP // 2 - 1)), -1).astype(F32)
    half_ref[...] = (rank >> 5).astype(F32)

    for part in range(3):
        meta_ref[pl.ds(part, DEVICES, stride=8), :] = meta[:, part * 128 : (part + 1) * 128]
    for part in range(3, 8):
        meta_ref[pl.ds(part, DEVICES, stride=8), :] = jnp.zeros((DEVICES, 128), F32)
    out_ref[:, CAP:ROWS, :] = meta_ref[...].reshape(DEVICES, 8, 128).astype(BF16)

    camera = embed_ref[pl.ds(cam_ref[0], 1), :]

    @pl.loop(0, CHUNKS)
    def _(k):
        rows = pl.ds(pl.multiple_of(k * 128, 128), 128)
        features = (feats_ref[rows, :].astype(F32) + camera).astype(BF16)
        half = columns_of(half_ref[pl.ds(k, 1), :])
        rhs_ref[rows, :] = split_columns(features.astype(F32), half).astype(BF16)

    @pl.loop(0, SLOTS // 512)
    def _(block):
        picked = jnp.dot(
            onehot_block(label_ref, block, CHUNKS), rhs_ref[...], preferred_element_type=F32
        ).astype(BF16)
        devices = pl.ds(block * 8, 8)
        out_ref[devices, 0 : CAP // 2, :] = picked[:, :C].reshape(8, CAP // 2, C)
        out_ref[devices, CAP // 2 : CAP, :] = picked[:, C:].reshape(8, CAP // 2, C)


def pack(camera, point_feats, top_bin, front_bin, camera_embed):
    whole = pl.BlockSpec(memory_space=pltpu.VMEM)
    return pl.pallas_call(
        pack_kernel,
        out_shape=jax.ShapeDtypeStruct((DEVICES, ROWS, C), BF16),
        in_specs=[pl.BlockSpec(memory_space=pltpu.SMEM)] + [whole] * 4,
        out_specs=whole,
        scratch_shapes=[
            pltpu.VMEM((CHUNKS, 128), F32),
            pltpu.VMEM((CHUNKS, 128), F32),
            pltpu.VMEM((CHUNKS, 128), F32),
            pltpu.VMEM((P_DEV, 2 * C), BF16),
            pltpu.VMEM((DEVICES * 8, 128), F32),
        ],
        compiler_params=pltpu.CompilerParams(vmem_limit_bytes=VMEM_LIMIT),
        cost_estimate=pl.CostEstimate(flops=2 * 4096 * 4096 * 256, bytes_accessed=4 * 2**20, transcendentals=0),
        name="pack",
    )(camera, point_feats, top_bin.reshape(CHUNKS, 128), front_bin.reshape(CHUNKS, 128), camera_embed)


def pool_kernel(got_ref, front_ref, side_ref, top_ref, meta_ref, fl_ref, sl_ref, tl_ref, zh_ref, yh_ref, zr_ref, yr_ref):
    meta_ref[...] = got_ref[:, CAP:ROWS, :].astype(F32).reshape(DEVICES * 8, 128)
    first = iota((PAIRS, 128), 1) < CAP

    def pairs(part):
        even = meta_ref[pl.ds(part, PAIRS, stride=16), :]
        odd = meta_ref[pl.ds(part + 8, PAIRS, stride=16), :]
        return jnp.where(first, even, odd).astype(jnp.int32) - 1

    x, y, z = pairs(0), pairs(1), pairs(2)
    live = x >= 0
    fl_ref[...] = jnp.where(live, x * 16 + (z & 15), -1).astype(F32)
    sl_ref[...] = jnp.where(live, y * 16 + (z & 15), -1).astype(F32)
    tl_ref[...] = jnp.where(live, x * 8 + (y & 7), -1).astype(F32)
    zh_ref[...] = ((z >> 4) & 1).astype(F32)
    yh_ref[...] = ((y >> 3) & 1).astype(F32)

    @pl.loop(0, PAIRS)
    def _(q):
        rows = pl.ds(pl.multiple_of(q * 128, 128), 128)
        piece = got_ref[pl.ds(q * 2, 2), 0:CAP, :].reshape(128, C).astype(F32)
        zr_ref[rows, :] = split_columns(piece, columns_of(zh_ref[pl.ds(q, 1), :])).astype(BF16)
        yr_ref[rows, :] = split_columns(piece, columns_of(yh_ref[pl.ds(q, 1), :])).astype(BF16)

    @pl.loop(0, 4)
    def _(block):
        sums = jnp.dot(onehot_block(fl_ref, block, PAIRS), zr_ref[...], preferred_element_type=F32)
        xs = pl.ds(block * 16, 16)
        front_ref[xs, 0:16, :] = sums[:, :C].reshape(16, 16, C)
        front_ref[xs, 16:32, :] = sums[:, C:].reshape(16, 16, C)

    sums = jnp.dot(onehot_block(sl_ref, 0, PAIRS), zr_ref[...], preferred_element_type=F32)
    side_ref[:, 0:16, :] = sums[:, :C].reshape(16, 16, C)
    side_ref[:, 16:32, :] = sums[:, C:].reshape(16, 16, C)

    @pl.loop(0, 2)
    def _(block):
        sums = jnp.dot(onehot_block(tl_ref, block, PAIRS), yr_ref[...], preferred_element_type=F32)
        xs = pl.ds(block * 32, 32)
        top_ref[xs, 0:8, :] = sums[:, :C].reshape(32, 8, C)
        top_ref[xs, 8:16, :] = sums[:, C:].reshape(32, 8, C)


def pool(got):
    whole = pl.BlockSpec(memory_space=pltpu.VMEM)
    return pl.pallas_call(
        pool_kernel,
        out_shape=[
            jax.ShapeDtypeStruct((BX, NZ, C), F32),
            jax.ShapeDtypeStruct((BY, NZ, C), F32),
            jax.ShapeDtypeStruct((BX, BY, C), F32),
        ],
        in_specs=[whole],
        out_specs=[whole] * 3,
        scratch_shapes=[pltpu.VMEM((DEVICES * 8, 128), F32)]
        + [pltpu.VMEM((PAIRS, 128), F32)] * 5
        + [pltpu.VMEM((SLOTS, 2 * C), BF16)] * 2,
        compiler_params=pltpu.CompilerParams(vmem_limit_bytes=VMEM_LIMIT),
        cost_estimate=pl.CostEstimate(flops=2 * 8192 * 1792 * 256, bytes_accessed=4 * 2**20, transcendentals=0),
        name="pool",
    )(got)


ATANH_ERF = (
    0.7978842164012749,
    0.036334282759596444,
    -3.312947161090104e-05,
    -5.524030501873291e-05,
    3.9691284083295496e-06,
    -1.3344752372813232e-07,
    1.80564030499361e-09,
)


def gelu(x):
    square = jnp.minimum(x * x, 64.0)
    ratio = ATANH_ERF[-1] * square + ATANH_ERF[-2]
    for factor in ATANH_ERF[-3::-1]:
        ratio = ratio * square + factor
    half = 0.5 * x
    return half + half * jnp.tanh(x * ratio)


STEP = 4


def mlp_kernel(top_ref, front_ref, side_ref, w_in_ref, b_in_ref, w_out_ref, b_out_ref, out_ref):
    for i in range(STEP):
        top = top_ref[i].astype(BF16).astype(F32)
        front = front_ref[i].astype(F32)
        cell = (top[:, None, :] + front[None, :, :] + side_ref[...].astype(F32)).astype(BF16)
        cell = cell.reshape(BY * NZ, C)
        hidden = jnp.dot(cell, w_in_ref[...], preferred_element_type=F32) + b_in_ref[...]
        hidden = gelu(hidden).astype(BF16)
        result = jnp.dot(hidden, w_out_ref[...], preferred_element_type=F32)
        result = result + b_out_ref[...] + cell.astype(F32)
        out_ref[i] = result.astype(BF16).reshape(BY, NZ, C)


def mlp(top, front, side, w_in, b_in, w_out, b_out):
    def same(*shape):
        return pl.BlockSpec(shape, lambda i: (0,) * len(shape))

    return pl.pallas_call(
        mlp_kernel,
        grid=(BX // STEP,),
        in_specs=[
            pl.BlockSpec((STEP, BY, C), lambda i: (i, 0, 0)),
            pl.BlockSpec((STEP, NZ, C), lambda i: (i, 0, 0)),
            same(BY, NZ, C),
            same(C, HID),
            same(1, HID),
            same(HID, C),
            same(1, C),
        ],
        out_specs=pl.BlockSpec((STEP, BY, NZ, C), lambda i: (i, 0, 0, 0)),
        out_shape=jax.ShapeDtypeStruct((BX, BY, NZ, C), BF16),
        compiler_params=pltpu.CompilerParams(vmem_limit_bytes=VMEM_LIMIT),
        cost_estimate=pl.CostEstimate(
            flops=4 * BX * BY * NZ * C * HID, bytes_accessed=9 * 2**20, transcendentals=BX * BY * NZ * HID
        ),
        name="voxel_mlp",
    )(top, front, side, w_in, b_in.reshape(1, HID), w_out, b_out.reshape(1, C))


def plane_sum(part, axis, size):
    rows = part.shape[0] * part.shape[1] // size
    pieces = lax.all_to_all(part.reshape(size, rows, C), axis, 0, 0, tiled=True)
    share = jnp.sum(pieces, axis=0).astype(BF16)
    return lax.all_gather(share, axis, axis=0, tiled=True).reshape(part.shape)


def per_device(
    point_feats, top_bin, front_bin, side_bin, camera_of_device, camera_embed, w_in, b_in, w_out, b_out
):
    sent = pack(camera_of_device, point_feats, top_bin, front_bin, camera_embed)
    got = lax.all_to_all(sent, ("gx", "gy"), split_axis=0, concat_axis=0, tiled=True)
    front_part, side_part, top = pool(got)
    front = plane_sum(front_part, "gy", N_GY)
    side = plane_sum(side_part, "gx", N_GX)
    return mlp(top, front, side, w_in, b_in, w_out, b_out)


def solution(mesh):
    points = P(("gx", "gy"))
    placed = (P(("gx", "gy"), None), points, points, points, points, P(), P(), P(), P(), P())
    return jax.shard_map(
        per_device, mesh=mesh, in_specs=placed, out_specs=P("gx", "gy", None, None), check_vma=False
    )
```

time: 349 us -> 191 us (0.55)
  matrix products: 121 us -> 0 us
  Pallas kernels: 0 us -> 72.9 us
  local copies, waits for them, and re-layouts: 46.8 us -> 3.36 us
  waiting for transfers between devices: 24.7 us -> 0.01 us
  other arithmetic: 19.3 us -> 0.08 us
  starting transfers between devices: 21.1 us -> 4.34 us
  blocking collectives: 115 us -> 108 us
    dot_general x40 -> x0, matrix products: 121 us -> none  [the longest x16 81.6 us: mix(): jnp.dot(hidden, w_out, preferred_element_type=jnp.float32) + b_out]
    psum x2 -> x0, blocking collectives: 115 us -> none  [the longest x1 79.3 us: per_device(): front_plane = lax.psum(front_part, 'gy').astype(jnp.bfloat16)]
    pallas_call x0 -> x3, Pallas kernels: none -> 72.9 us  [the longest x1 31.3 us: mlp(): pl.pallas_call(mlp_kernel, grid=(BX // STEP,), in_specs=[pl.BlockSpec((ST...]
    all_gather x0 -> x2, blocking collectives: none -> 54.2 us  [plane_sum(): return lax.all_gather(share, axis, axis=0, tiled=True).reshape(part.shape)]
    all_to_all x0 -> x2, blocking collectives: none -> 53.4 us  [the longest x1 42.2 us: per_device(): lax.all_to_all(sent, ('gx', 'gy'), split_axis=0, concat_axis=0, tiled=True)]
    all_to_all x2 -> x1, waiting for transfers between devices: 24.7 us -> 0.01 us  [plane_sum(): pieces = lax.all_to_all(part.reshape(size, rows, C), axis, 0, 0, tiled=True)]
    all_to_all x2 -> x1, starting transfers between devices: 21.1 us -> 4.34 us  [plane_sum(): pieces = lax.all_to_all(part.reshape(size, rows, C), axis, 0, 0, tiled=True)]
    dynamic_update_slice x16 -> x0, local copies, waits for them, and re-layouts: 13.4 us -> none  [per_device(): lax.map(mix, (top_plane.reshape(BX // 4, 4, BY, C), front_plane.reshape(B...]
  transfers between devices with their start and end apart: 2 -> 1, of which waited for: 1 -> 0; matrix products, arithmetic and copies ran while one was open for 5% -> 0% of each run, Pallas kernels for 0% -> 0%
where the time goes in v1:
time: 191 us; the launch traced here: 189 us
  blocking collectives  108 us (57%)
  Pallas kernels  72.9 us (38%)
  starting transfers between devices  4.34 us (2%)
  local copies, waits for them, and re-layouts  3.36 us (2%)
    all_gather x2, blocking collectives, plane_sum(): return lax.all_gather(share, axis, axis=0, tiled=True).reshape(part.shape)  54.2 us
    all_to_all x1, blocking collectives, per_device(): lax.all_to_all(sent, ('gx', 'gy'), split_axis=0, concat_axis=0, tiled=True)  42.2 us
    pallas_call x1, Pallas kernels, mlp(): pl.pallas_call(mlp_kernel, grid=(BX // STEP,), in_specs=[pl.BlockSpec((ST...  31.3 us
    pallas_call x1, Pallas kernels, pack(): pl.pallas_call(pack_kernel, out_shape=jax.ShapeDtypeStruct((DEVICES, ROWS...  23.1 us
    pallas_call x1, Pallas kernels, pool(): pl.pallas_call(pool_kernel, out_shape=[jax.ShapeDtypeStruct((BX, NZ, C),...  18.5 us
    all_to_all x1, blocking collectives, plane_sum(): pieces = lax.all_to_all(part.reshape(size, rows, C), axis, 0, 0, tiled=True)  11.2 us
    all_to_all x1, starting transfers between devices, plane_sum(): pieces = lax.all_to_all(part.reshape(size, rows, C), axis, 0, 0, tiled=True)  4.34 us
  transfers between devices with their start and end apart: 1, of which 0 were waited for; matrix products, arithmetic and copies ran while one was open for 0% of the time, Pallas kernels for 0%

profile of v1, /device:TPU:0, one launch (start us, length us, event | category | flops | bytes accessed | tf_op | source)
XLA Modules:
  0.0 189.1 jit_solution(7187199851325924634)
XLA Ops:
  0.7 0.0 copy-start
  0.7 1.2 copy-done
  1.9 0.0 copy-start.3
  1.9 0.7 copy-done.3
  2.6 0.0 copy-start.4
  2.6 0.7 copy-done.4
  3.3 0.0 copy-start.5
  3.3 0.7 copy-done.5
  4.0 23.1 %pack.1 = bf16[128,72,128]{2,1,0:T(8,128)(2,1)S(1)} custom-call(s32[1]{0:T(128)S(6)} %copy.10.cam_ref, bf16[4096,128]{1,0:T(8,128)(2,1)S(1)} %copy-done, s32[32,128]{1,0:T(8,128)S(1)} %bitcast.11, s32[32,128]{1,0:T(8,128)S(1)} %bitcast.12, f32[6,128]{1,0:T(8,128)S(1)} %copy-done.5), custom_call_target="tpu_custom_call" | custom-call | flops 8589934592 | bytes 4194304 | tf_op jit(solution)/shard_map/pack/pallas_call | solution.py:125
  27.1 42.2 %all_to_all.15.got_ref = bf16[128,72,128]{2,1,0:T(8,128)(2,1)S(1)} all-to-all(bf16[128,72,128]{2,1,0:T(8,128)(2,1)S(1)} %pack.1), channel_id=1, replica_groups=mesh['gx'=8,'gy'=16] {'gx','gy'}, dimensions={0} | all-to-all | bytes 4718592 | tf_op jit(solution)/shard_map/all_to_all | solution.py:279
  69.3 18.5 %pool.1 = (f32[64,32,128]{2,1,0:T(8,128)}, f32[16,32,128]{2,1,0:T(8,128)S(1)}, f32[64,16,128]{2,1,0:T(8,128)S(1)}) custom-call(bf16[128,72,128]{2,1,0:T(8,128)(2,1)S(1)} %all_to_all.15.got_ref), custom_call_target="tpu_custom_call" | custom-call | flops 7516192768 | bytes 4194304 | tf_op jit(solution)/shard_map/pool/pallas_call | solution.py:188
  87.8 0.0 copy-start.1
  87.8 0.0 copy-start.2
  87.9 0.0 copy-start.6
  87.9 0.0 copy-start.7
  87.9 11.2 %all_to_all.16 = f32[8,64,128]{2,1,0:T(8,128)S(1)} all-to-all(f32[8,64,128]{2,1,0:T(8,128)S(1)} %bitcast.9), channel_id=1, replica_groups=mesh['gx'=8,'gy'=16] {'gx'}, dimensions={0} | all-to-all | bytes 524288 | tf_op jit(solution)/shard_map/all_to_all | solution.py:270
  99.1 4.3 %all-to-all-start.1 = ((f32[16,128,128]{2,1,0:T(8,128)}), f32[16,128,128]{2,1,0:T(8,128)S(1)}, u32[]{:S(2)}, u32[]{:S(2)}) async-start(f32[16,128,128]{2,1,0:T(8,128)} %bitcast.2), calls=%async_computation.1 | async-start | bytes 2097152 | tf_op jit(solution)/shard_map/all_to_all | solution.py:270
  103.5 28.6 %all_gather.7 = bf16[512,128]{1,0:T(8,128)(2,1)S(1)} all-gather(bf16[64,128]{1,0:T(8,128)(2,1)S(1)} %reduce_sum.19), channel_id=1, replica_groups=mesh['gx'=8,'gy'=16] {'gx'}, dimensions={0}, use_global_device_ids=true | all-gather | bytes 147456 | tf_op jit(solution)/shard_map/all_gather | solution.py:272
  132.1 0.0 all-to-all-done.1
  132.1 0.1 reduce_sum.18
  132.2 25.6 %all_gather.6 = bf16[2048,128]{1,0:T(8,128)(2,1)S(1)} all-gather(bf16[128,128]{1,0:T(8,128)(2,1)S(1)} %reduce_sum.18), channel_id=1, replica_groups=mesh['gx'=8,'gy'=16] {'gy'}, dimensions={0}, use_global_device_ids=true | all-gather | bytes 557056 | tf_op jit(solution)/shard_map/all_gather | solution.py:272
  157.8 0.0 copy-done.1
  157.8 0.0 copy-done.2
  157.8 0.0 copy-done.6
  157.8 0.0 copy-done.7
  157.8 31.3 %voxel_mlp.1 = bf16[64,16,32,128]{3,2,1,0:T(8,128)(2,1)} custom-call(f32[64,16,128]{2,1,0:T(8,128)S(1)} %get-tuple-element.8.top_ref, bf16[64,32,128]{2,1,0:T(8,128)(2,1)S(1)} %bitcast.8, bf16[16,32,128]{2,1,0:T(8,128)(2,1)S(1)} %bitcast.10, bf16[128,256]{1,0:T(8,128)(2,1)S(1)} %copy-done.1, f32[1,256]{1,0:T(1,128)S(1)} %bitcast.13, ...), custom_call_target="tpu_custom_call" | custom-call | flops 4294967296 | bytes 9437184 | tf_op jit(solution)/shard_map/voxel_mlp/pallas_call | solution.py:246
  (1 shorter events, 0.0 us)
Async XLA Ops:
  0.7 1.2 copy-start
  1.9 0.7 copy-start.3
  2.6 0.7 copy-start.4
  3.3 0.7 copy-start.5
  87.8 69.9 %copy-start.1 = (bf16[128,256]{1,0:T(8,128)(2,1)S(1)}, bf16[128,256]{1,0:T(8,128)(2,1)}, u32[]{:S(2)}) copy-start(bf16[128,256]{1,0:T(8,128)(2,1)} %w_in_ref.1) | copy-start | bytes 196612
  87.8 69.9 %copy-start.2 = (bf16[256,128]{1,0:T(8,128)(2,1)S(1)}, bf16[256,128]{1,0:T(8,128)(2,1)}, u32[]{:S(2)}) copy-start(bf16[256,128]{1,0:T(8,128)(2,1)} %w_out_ref.1) | copy-start | bytes 196612
  87.9 69.9 %copy-start.6 = (f32[256]{0:T(256)S(1)}, f32[256]{0:T(256)}, u32[]{:S(2)}) copy-start(f32[256]{0:T(256)} %param.16) | copy-start | bytes 3076
  87.9 69.9 %copy-start.7 = (f32[128]{0:T(128)S(1)}, f32[128]{0:T(128)}, u32[]{:S(2)}) copy-start(f32[128]{0:T(128)} %param.18) | copy-start | bytes 1540
  99.1 33.0 %all-to-all-start.1 = ((f32[16,128,128]{2,1,0:T(8,128)}), f32[16,128,128]{2,1,0:T(8,128)S(1)}, u32[]{:S(2)}, u32[]{:S(2)}) async-start(f32[16,128,128]{2,1,0:T(8,128)} %bitcast.2), calls=%async_computation.1 | async-start | bytes 2097152 | tf_op jit(solution)/shard_map/all_to_all | solution.py:270

commit v2 on v1

v2 whole, which is shorter than its diff:
```python
import jax
import jax.numpy as jnp
from jax import lax
from jax.experimental import pallas as pl
from jax.experimental.pallas import tpu as pltpu
from jax.sharding import PartitionSpec as P

C = 128
HID = 256
CAMS = 6
NZ = 32
BX = 64
BY = 16
P_DEV = 4096
DEVICES = 128
N_GX = 8
N_GY = 16
CAP = 64
ROWS = CAP + 8
SLOTS = DEVICES * CAP
CHUNKS = P_DEV // 128
PAIRS = DEVICES // 2

F32 = jnp.float32
BF16 = jnp.bfloat16
VMEM_LIMIT = 48 * 2**20


def iota(shape, axis):
    return lax.broadcasted_iota(jnp.int32, shape, axis)


def columns_of(row):
    diagonal = jnp.where(iota((128, 128), 0) == iota((128, 128), 1), row, 0.0).astype(BF16)
    return jnp.dot(diagonal, jnp.ones((128, 128), BF16), preferred_element_type=F32).astype(BF16)


def split_columns(values, half):
    zero = jnp.zeros_like(values)
    left = half == jnp.zeros_like(half)
    return jnp.concatenate([jnp.where(left, values, zero), jnp.where(left, zero, values)], axis=1)


def onehot_rows(label, base, rows):
    return jnp.where(iota((rows, 128), 0) + base == label, 1.0, 0.0).astype(BF16)


def onehot(labels_ref, base, rows, chunks):
    return jnp.concatenate(
        [onehot_rows(labels_ref[pl.ds(k, 1), :], base, rows) for k in range(chunks)], axis=1
    )


def pack_kernel(
    cam_ref, feats_ref, top_ref, front_ref, embed_ref, out_ref,
    marks_ref, rank_ref, place_ref, half_ref, rhs_ref, values_ref, sorted_ref, meta_ref, start_ref, start_smem, sem,
):
    top = top_ref[...]
    live = top >= 0
    grid_x = top >> 8
    grid_y = top & 255
    owner = jnp.where(live, (grid_x >> 6) * N_GY + (grid_y >> 4), -1)
    cells = (
        (grid_x & (BX - 1)) + 1,
        (grid_y & (BY - 1)) + 1,
        (front_ref[...] & (NZ - 1)) + 1,
    )
    cells = [cell.astype(F32) for cell in cells]

    for k in range(CHUNKS):
        marks_ref[:, k * 128 : (k + 1) * 128] = onehot_rows(owner[k : k + 1, :], 0, DEVICES)
    totals = jnp.dot(marks_ref[...], jnp.ones((P_DEV, 128), BF16), preferred_element_type=F32)
    below = jnp.where(iota((128, 128), 1) < iota((128, 128), 0), 1.0, 0.0).astype(BF16)
    starts = jnp.dot(below, totals.astype(BF16), preferred_element_type=F32)
    start_row = jnp.sum(
        jnp.where(iota((128, 128), 0) == iota((128, 128), 1), starts, 0.0), axis=0, keepdims=True
    )
    start_ref[...] = start_row.astype(jnp.int32)
    copy = pltpu.make_async_copy(start_ref, start_smem, sem)
    copy.start()

    before = iota((128, 256), 0) < iota((128, 256), 1)
    later = iota((128, 256), 1) >= 128
    counter = jnp.where(before | later, 1.0, 0.0).astype(BF16)
    seen = jnp.zeros((DEVICES, 128), F32)
    slot = iota((128, 128), 0) & (CAP - 1)
    for k in range(CHUNKS):
        columns = slice(k * 128, (k + 1) * 128)
        mine = iota((DEVICES, 128), 0) == owner[k : k + 1, :]
        counts = jnp.dot(marks_ref[:, columns], counter, preferred_element_type=F32)
        rank = jnp.sum(jnp.where(mine, counts[:, :128] + seen, 0.0), axis=0, keepdims=True)
        start = jnp.sum(jnp.where(mine, starts, 0.0), axis=0, keepdims=True)
        seen = seen + counts[:, 128:]
        place_ref[pl.ds(k, 1), :] = rank + start
        here = slot == rank.astype(jnp.int32)
        for part in range(3):
            values_ref[part * 128 : (part + 1) * 128, columns] = jnp.where(
                here, cells[part][k : k + 1, :], 0.0
            ).astype(BF16)
    place = place_ref[...].astype(jnp.int32)
    half_ref[...] = (place >> 11).astype(F32)
    place_ref[...] = jnp.where(live, place & 2047, -1).astype(F32)

    camera = embed_ref[pl.ds(cam_ref[0], 1), :]
    for k in range(CHUNKS):
        rows = slice(k * 128, (k + 1) * 128)
        features = (feats_ref[rows, :].astype(F32) + camera).astype(BF16)
        rhs_ref[rows, :] = split_columns(features, columns_of(half_ref[pl.ds(k, 1), :]))

    rank_ref[...] = place_ref[...].astype(jnp.int32)
    for block in range(8):
        base = block * 256
        picked = jnp.dot(onehot(rank_ref, base, 256, CHUNKS), rhs_ref[...], preferred_element_type=F32)
        sorted_ref[base : base + 256, :] = picked[:, :C]
        sorted_ref[2048 + base : 2304 + base, :] = picked[:, C:]
    sorted_ref[P_DEV : P_DEV + CAP, :] = jnp.zeros((CAP, C), F32)

    meta = lax.dot_general(
        values_ref[...], marks_ref[...], (((1,), (1,)), ((), ())), preferred_element_type=F32
    )
    for part in range(3):
        meta_ref[pl.ds(part, DEVICES, stride=8), :] = meta[part * 128 : (part + 1) * 128, :].T
    for part in range(3, 8):
        meta_ref[pl.ds(part, DEVICES, stride=8), :] = jnp.zeros((DEVICES, 128), F32)
    out_ref[:, CAP:ROWS, :] = meta_ref[...].reshape(DEVICES, 8, 128).astype(BF16)

    copy.wait()

    @pl.loop(0, DEVICES, unroll=8)
    def _(device):
        out_ref[device, 0:CAP, :] = sorted_ref[pl.ds(start_smem[0, device], CAP), :].astype(BF16)


def pack(camera, point_feats, top_bin, front_bin, camera_embed):
    whole = pl.BlockSpec(memory_space=pltpu.VMEM)
    return pl.pallas_call(
        pack_kernel,
        out_shape=jax.ShapeDtypeStruct((DEVICES, ROWS, C), BF16),
        in_specs=[pl.BlockSpec(memory_space=pltpu.SMEM)] + [whole] * 4,
        out_specs=whole,
        scratch_shapes=[
            pltpu.VMEM((DEVICES, P_DEV), BF16),
            pltpu.VMEM((CHUNKS, 128), jnp.int32),
            pltpu.VMEM((CHUNKS, 128), F32),
            pltpu.VMEM((CHUNKS, 128), F32),
            pltpu.VMEM((P_DEV, 2 * C), BF16),
            pltpu.VMEM((3 * 128, P_DEV), BF16),
            pltpu.VMEM((P_DEV + CAP, C), F32),
            pltpu.VMEM((DEVICES * 8, 128), F32),
            pltpu.VMEM((1, DEVICES), jnp.int32),
            pltpu.SMEM((1, DEVICES), jnp.int32),
            pltpu.SemaphoreType.DMA,
        ],
        compiler_params=pltpu.CompilerParams(vmem_limit_bytes=VMEM_LIMIT),
        cost_estimate=pl.CostEstimate(flops=2 * 4096 * 4096 * 256, bytes_accessed=4 * 2**20, transcendentals=0),
        name="pack",
    )(camera, point_feats, top_bin.reshape(CHUNKS, 128), front_bin.reshape(CHUNKS, 128), camera_embed)


def pool_side_kernel(half_ref, got_ref, side_ref, labels_ref, meta_ref):
    meta_ref[...] = got_ref[:, CAP:ROWS, :].astype(F32).reshape(DEVICES * 8, 128)
    first = iota((PAIRS, 128), 1) < CAP

    def pairs(part):
        even = meta_ref[pl.ds(part, PAIRS, stride=16), :]
        odd = meta_ref[pl.ds(part + 8, PAIRS, stride=16), :]
        return jnp.where(first, even, odd).astype(jnp.int32) - 1

    x, y, z = pairs(0), pairs(1), pairs(2)
    live = x >= 0
    x = x ^ (half_ref[0] * (BX // 2))
    labels_ref[0] = jnp.where(live, x * 16 + (z & 15), -1)
    labels_ref[1] = jnp.where(live, x * 8 + (y & 7), -1)
    labels_ref[2] = jnp.where(live, y * 32 + z, -1)
    labels_ref[3] = (y >> 3) & 1
    labels_ref[4] = (z >> 4) & 1

    points = got_ref[:, 0:CAP, :].reshape(SLOTS, C)
    for block in range(2):
        sums = jnp.dot(onehot(labels_ref.at[2], block * 256, 256, PAIRS), points, preferred_element_type=F32)
        side_ref[block * 8 : block * 8 + 8] = sums.reshape(8, NZ, C)


def split_points(got_ref, half_ref, rhs_ref):
    for q in range(PAIRS):
        piece = got_ref[q * 2 : q * 2 + 2, 0:CAP, :].reshape(128, C)
        half = columns_of(half_ref[pl.ds(q, 1), :].astype(F32))
        rhs_ref[q * 128 : (q + 1) * 128, :] = split_columns(piece, half)


def pool_front_kernel(got_ref, labels_ref, mine_ref, other_ref, rhs_ref):
    split_points(got_ref, labels_ref.at[4], rhs_ref)
    for block in range(4):
        sums = jnp.dot(onehot(labels_ref.at[0], block * 256, 256, PAIRS), rhs_ref[...], preferred_element_type=F32)
        out = (mine_ref, other_ref)[block // 2]
        xs = pl.ds(block % 2 * 16, 16)
        out[xs, 0:16, :] = sums[:, :C].reshape(16, 16, C)
        out[xs, 16:32, :] = sums[:, C:].reshape(16, 16, C)


def pool_top_kernel(got_ref, labels_ref, top_ref, rhs_ref):
    split_points(got_ref, labels_ref.at[3], rhs_ref)
    for block in range(2):
        sums = jnp.dot(onehot(labels_ref.at[1], block * 256, 256, PAIRS), rhs_ref[...], preferred_element_type=F32)
        xs = pl.ds(block * 32, 32)
        top_ref[xs, 0:8, :] = sums[:, :C].reshape(32, 8, C)
        top_ref[xs, 8:16, :] = sums[:, C:].reshape(32, 8, C)


def call(kernel, ins, outs, scratch, flops, name):
    whole = pl.BlockSpec(memory_space=pltpu.VMEM)
    small = pl.BlockSpec(memory_space=pltpu.SMEM)
    return pl.pallas_call(
        kernel,
        out_shape=outs,
        in_specs=[small if i.dtype == jnp.int32 and i.size == 1 else whole for i in ins],
        out_specs=[whole] * len(outs),
        scratch_shapes=scratch,
        compiler_params=pltpu.CompilerParams(vmem_limit_bytes=VMEM_LIMIT),
        cost_estimate=pl.CostEstimate(flops=flops, bytes_accessed=4 * 2**20, transcendentals=0),
        name=name,
    )(*ins)


def pool_side(half, got):
    return call(
        pool_side_kernel,
        [half, got],
        [jax.ShapeDtypeStruct((BY, NZ, C), F32), jax.ShapeDtypeStruct((5, PAIRS, 128), jnp.int32)],
        [pltpu.VMEM((DEVICES * 8, 128), F32)],
        2 * 8192 * 512 * 256,
        "pool_side",
    )


def pool_front(got, labels):
    shape = jax.ShapeDtypeStruct((BX // 2, NZ, C), F32)
    scratch = [pltpu.VMEM((SLOTS, 2 * C), BF16)]
    return call(pool_front_kernel, [got, labels], [shape, shape], scratch, 2 * 8192 * 1024 * 256 * 2, "pool_front")


def pool_top(got, labels):
    return call(
        pool_top_kernel,
        [got, labels],
        [jax.ShapeDtypeStruct((BX, BY, C), F32)],
        [pltpu.VMEM((SLOTS, 2 * C), BF16)],
        2 * 8192 * 768 * 256 * 2,
        "pool_top",
    )[0]


def gelu(x):
    half = 0.5 * x
    return half + half * lax.erf(x * 0.7071067811865476)


STEP = 4


def mlp_kernel(half_ref, top_ref, mine_ref, other_ref, side_ref, w_in_ref, b_in_ref, w_out_ref, b_out_ref, out_ref):
    def work(front_ref):
        for i in range(STEP):
            top = top_ref[i].astype(BF16).astype(F32)
            front = front_ref[i].astype(F32)
            cell = (top[:, None, :] + front[None, :, :] + side_ref[...].astype(F32)).astype(BF16)
            cell = cell.reshape(BY * NZ, C)
            hidden = jnp.dot(cell, w_in_ref[...], preferred_element_type=F32) + b_in_ref[...]
            hidden = gelu(hidden).astype(BF16)
            result = jnp.dot(hidden, w_out_ref[...], preferred_element_type=F32)
            result = result + b_out_ref[...] + cell.astype(F32)
            out_ref[i] = result.astype(BF16).reshape(BY, NZ, C)

    mine = pl.program_id(0) < HALF_STEPS
    pl.when(mine)(lambda: work(mine_ref))
    pl.when(jnp.logical_not(mine))(lambda: work(other_ref))


HALF_STEPS = BX // STEP // 2


def mlp(half, top, mine, other, side, w_in, b_in, w_out, b_out):
    def same(*shape):
        return pl.BlockSpec(shape, lambda i, h: (0,) * len(shape))

    return pl.pallas_call(
        mlp_kernel,
        grid_spec=pltpu.PrefetchScalarGridSpec(
            num_scalar_prefetch=1,
            grid=(BX // STEP,),
            in_specs=[
                pl.BlockSpec((STEP, BY, C), lambda i, h: (i, 0, 0)),
                pl.BlockSpec((STEP, NZ, C), lambda i, h: (jnp.minimum(i, HALF_STEPS - 1), 0, 0)),
                pl.BlockSpec((STEP, NZ, C), lambda i, h: (jnp.maximum(i - HALF_STEPS, 0), 0, 0)),
                same(BY, NZ, C),
                same(C, HID),
                same(1, HID),
                same(HID, C),
                same(1, C),
            ],
            out_specs=pl.BlockSpec((STEP, BY, NZ, C), lambda i, h: (i ^ (h[0] * HALF_STEPS), 0, 0, 0)),
        ),
        out_shape=jax.ShapeDtypeStruct((BX, BY, NZ, C), BF16),
        compiler_params=pltpu.CompilerParams(vmem_limit_bytes=VMEM_LIMIT),
        cost_estimate=pl.CostEstimate(
            flops=4 * BX * BY * NZ * C * HID, bytes_accessed=9 * 2**20, transcendentals=BX * BY * NZ * HID
        ),
        name="voxel_mlp",
    )(half, top, mine, other, side, w_in, b_in.reshape(1, HID), w_out, b_out.reshape(1, C))


SAME_CORE = [list(range(core, N_GY, 2)) for core in range(2)]
OTHER_CORE = [(i, i ^ 1) for i in range(N_GY)]


def plane_sum(part, axis, groups=None):
    rows = part.shape[0] * part.shape[1] // 8
    pieces = lax.all_to_all(part.reshape(8, rows, C), axis, 0, 0, tiled=True, axis_index_groups=groups)
    share = jnp.sum(pieces, axis=0).astype(BF16)
    copies = jnp.broadcast_to(share[None], (8, rows, C))
    whole = lax.all_to_all(copies, axis, 0, 0, tiled=True, axis_index_groups=groups)
    return whole.reshape(part.shape)


def per_device(
    point_feats, top_bin, front_bin, side_bin, camera_of_device, camera_embed, w_in, b_in, w_out, b_out
):
    half = (lax.axis_index("gy") & 1).astype(jnp.int32).reshape(1)
    sent = pack(camera_of_device, point_feats, top_bin, front_bin, camera_embed)
    got = lax.all_to_all(sent, ("gx", "gy"), split_axis=0, concat_axis=0, tiled=True)
    side_part, labels = pool_side(half, got)
    side = plane_sum(side_part, "gx")
    mine, other = pool_front(got, labels)
    mine = mine + lax.ppermute(other, "gy", OTHER_CORE)
    top = pool_top(got, labels)
    mine, top, side = lax.optimization_barrier((mine, top, side))
    mine = plane_sum(mine, "gy", SAME_CORE)
    other = lax.ppermute(mine, "gy", OTHER_CORE)
    return mlp(half, top, mine, other, side, w_in, b_in, w_out, b_out)


def solution(mesh):
    points = P(("gx", "gy"))
    placed = (P(("gx", "gy"), None), points, points, points, points, P(), P(), P(), P(), P())
    return jax.shard_map(
        per_device, mesh=mesh, in_specs=placed, out_specs=P("gx", "gy", None, None), check_vma=False
    )
```

time: 191 us -> 129 us (0.68)
  blocking collectives: 108 us -> 25.8 us
  Pallas kernels: 72.9 us -> 34.9 us
  waiting for transfers between devices: 0.01 us -> 35 us
  starting transfers between devices: 4.34 us -> 20 us
  local copies, waits for them, and re-layouts: 3.36 us -> 8.73 us
  other arithmetic: 0.08 us -> 2.19 us
    all_gather x2 -> x0, blocking collectives: 54.2 us -> none  [plane_sum(): return lax.all_gather(share, axis, axis=0, tiled=True).reshape(part.shape)]
    all_to_all x1 -> x3, waiting for transfers between devices: 0.01 us -> 33.5 us  [the longest x1 31.2 us: per_device(): lax.all_to_all(sent, ('gx', 'gy'), split_axis=0, concat_axis=0, tiled=True)]
    all_to_all x2, blocking collectives: 53.4 us -> 25.8 us  [the longest x1 14.5 us: plane_sum(): lax.all_to_all(part.reshape(8, rows, C), axis, 0, 0, tiled=True, axis_ind...]
    pallas_call x2 -> x4, Pallas kernels: 49.8 us -> 27.1 us  [the longest x1 16.1 us: mlp(): pl.pallas_call(mlp_kernel, grid_spec=pltpu.PrefetchScalarGridSpec(num_sca...]
    pallas_call x1, Pallas kernels: 23.1 us -> 7.8 us  [pack(): pl.pallas_call(pack_kernel, out_shape=jax.ShapeDtypeStruct((DEVICES, ROWS...]
    all_to_all x1 -> x3, starting transfers between devices: 4.34 us -> 19 us  [the longest x1 11.1 us: per_device(): lax.all_to_all(sent, ('gx', 'gy'), split_axis=0, concat_axis=0, tiled=True)]
    unnamed x16 -> x28, local copies, waits for them, and re-layouts: 3.36 us -> 8.03 us
  transfers between devices with their start and end apart: 1 -> 5, of which waited for: 0 -> 4; matrix products, arithmetic and copies ran while one was open for 0% -> 2% of each run, Pallas kernels for 0% -> 6%
where the time goes in v2:
time: 129 us; the launch traced here: 127 us
  waiting for transfers between devices  35 us (27%)
  Pallas kernels  34.9 us (27%)
  blocking collectives  25.8 us (20%)
  starting transfers between devices  20 us (16%)
  local copies, waits for them, and re-layouts  8.73 us (7%)
  other arithmetic  2.19 us (2%)
    all_to_all x1, waiting for transfers between devices, per_device(): lax.all_to_all(sent, ('gx', 'gy'), split_axis=0, concat_axis=0, tiled=True)  31.2 us
    pallas_call x1, Pallas kernels, mlp(): pl.pallas_call(mlp_kernel, grid_spec=pltpu.PrefetchScalarGridSpec(num_sca...  16.1 us
    all_to_all x1, blocking collectives, plane_sum(): lax.all_to_all(part.reshape(8, rows, C), axis, 0, 0, tiled=True, axis_ind...  14.5 us
    all_to_all x1, blocking collectives, plane_sum(): lax.all_to_all(copies, axis, 0, 0, tiled=True, axis_index_groups=groups)  11.3 us
    all_to_all x1, starting transfers between devices, per_device(): lax.all_to_all(sent, ('gx', 'gy'), split_axis=0, concat_axis=0, tiled=True)  11.1 us
    pallas_call x3, Pallas kernels, call(): pl.pallas_call(kernel, out_shape=outs, in_specs=[small if i.dtype == jnp....  11 us
    unnamed x28, local copies, waits for them, and re-layouts  8.03 us
    pallas_call x1, Pallas kernels, pack(): pl.pallas_call(pack_kernel, out_shape=jax.ShapeDtypeStruct((DEVICES, ROWS...  7.8 us
  transfers between devices with their start and end apart: 5, of which 4 were waited for; matrix products, arithmetic and copies ran while one was open for 2% of the time, Pallas kernels for 6%

profile of v2, /device:TPU:0, one launch (start us, length us, event | category | flops | bytes accessed | tf_op | source)
XLA Modules:
  0.0 127.5 jit_solution(14202881235889539321)
XLA Ops:
  0.7 0.0 copy-start.1
  0.7 1.2 copy-done.1
  1.9 0.0 copy-start.4
  1.9 0.7 copy-done.4
  2.6 0.0 copy-start.5
  2.6 0.7 copy-done.5
  3.3 0.0 copy-start.6
  3.3 0.7 copy-done.6
  4.0 7.8 %pack.1 = bf16[128,72,128]{2,1,0:T(8,128)(2,1)S(1)} custom-call(s32[1]{0:T(128)S(6)} %copy.10.cam_ref, bf16[4096,128]{1,0:T(8,128)(2,1)S(1)} %copy-done.1, s32[32,128]{1,0:T(8,128)S(1)} %bitcast.12, s32[32,128]{1,0:T(8,128)S(1)} %bitcast.13, f32[6,128]{1,0:T(8,128)S(1)} %copy-done.6), custom_call_target="tpu_custom_call" | custom-call | flops 8589934592 | bytes 4194304 | tf_op jit(solution)/shard_map/pack/pallas_call | solution.py:136
  11.8 0.0 copy-start
  11.8 1.4 %copy-done = bf16[128,72,128]{2,1,0:T(8,128)(2,1)} copy-done((bf16[128,72,128]{2,1,0:T(8,128)(2,1)}, bf16[128,72,128]{2,1,0:T(8,128)(2,1)S(1)}, u32[]{:S(2)}) %copy-start) | copy-done | bytes 2359320
  13.2 11.1 %all-to-all-start = ((bf16[128,72,128]{2,1,0:T(8,128)(2,1)}), bf16[128,72,128]{2,1,0:T(8,128)(2,1)S(1)}, u32[]{:S(2)}, u32[]{:S(2)}) async-start(bf16[128,72,128]{2,1,0:T(8,128)(2,1)} %copy-done), calls=%async_computation | async-start | bytes 4718592 | tf_op jit(solution)/shard_map/all_to_all | solution.py:330
  24.4 31.2 %all-to-all-done.got_ref = bf16[128,72,128]{2,1,0:T(8,128)(2,1)S(1)} async-done(((bf16[128,72,128]{2,1,0:T(8,128)(2,1)}), bf16[128,72,128]{2,1,0:T(8,128)(2,1)S(1)}, u32[]{:S(2)}, u32[]{:S(2)}) %all-to-all-start) | async-done | bytes 2359328 | tf_op jit(solution)/shard_map/all_to_all | solution.py:330
  55.6 3.1 %pool_side.1 = (f32[16,32,128]{2,1,0:T(8,128)}, s32[5,64,128]{2,1,0:T(8,128)S(1)}) custom-call(s32[1]{0:T(128)} %bitcast.half_ref, bf16[128,72,128]{2,1,0:T(8,128)(2,1)S(1)} %all-to-all-done.got_ref), custom_call_target="tpu_custom_call" | custom-call | flops 2147483648 | bytes 4194304 | tf_op jit(solution)/shard_map/pool_side/pallas_call | solution.py:213
  58.7 0.0 copy-start.11
  58.7 0.7 copy-done.11
  59.3 4.2 %all-to-all-start.1 = ((f32[8,64,128]{2,1,0:T(8,128)}), f32[8,64,128]{2,1,0:T(8,128)}, u32[]{:S(2)}, u32[]{:S(2)}) async-start(f32[8,64,128]{2,1,0:T(8,128)} %bitcast.3), calls=%async_computation.1 | async-start | bytes 524288 | tf_op jit(solution)/shard_map/all_to_all | solution.py:318
  63.6 0.0 copy-start.12
  63.6 0.9 copy-done.12
  64.5 5.1 %pool_front.1 = (f32[32,32,128]{2,1,0:T(8,128)S(1)}, f32[32,32,128]{2,1,0:T(8,128)S(1)}) custom-call(bf16[128,72,128]{2,1,0:T(8,128)(2,1)S(1)} %all-to-all-done.got_ref, s32[5,64,128]{2,1,0:T(8,128)S(1)} %copy-done.12), custom_call_target="tpu_custom_call" | custom-call | flops 8589934592 | bytes 4194304 | tf_op jit(solution)/shard_map/pool_front/pallas_call | solution.py:213
  69.6 1.0 collective-permute-start
  70.5 1.5 %all-to-all-done.1 = f32[8,64,128]{2,1,0:T(8,128)} async-done(((f32[8,64,128]{2,1,0:T(8,128)}), f32[8,64,128]{2,1,0:T(8,128)}, u32[]{:S(2)}, u32[]{:S(2)}) %all-to-all-start.1) | async-done | bytes 262176 | tf_op jit(solution)/shard_map/all_to_all | solution.py:318
  72.0 1.0 reduce_sum.18
  73.0 0.7 broadcast_in_dim.4
  73.7 3.7 %all-to-all-start.2 = ((bf16[8,64,128]{2,1,0:T(8,128)(2,1)}), bf16[8,64,128]{2,1,0:T(8,128)(2,1)S(1)}, u32[]{:S(2)}, u32[]{:S(2)}) async-start(bf16[8,64,128]{2,1,0:T(8,128)(2,1)} %broadcast_in_dim.4), calls=%async_computation.2 | async-start | bytes 262144 | tf_op jit(solution)/shard_map/all_to_all | solution.py:321
  77.3 0.0 copy-start.13
  77.3 0.9 copy-done.13
  78.2 2.9 %pool_top.1.top_ref = f32[64,16,128]{2,1,0:T(8,128)S(1)} custom-call(bf16[128,72,128]{2,1,0:T(8,128)(2,1)S(1)} %all-to-all-done.got_ref, s32[5,64,128]{2,1,0:T(8,128)S(1)} %copy-done.13), custom_call_target="tpu_custom_call" | custom-call | flops 6442450944 | bytes 4194304 | tf_op jit(solution)/shard_map/pool_top/pallas_call | solution.py:213
  81.1 0.0 copy-start.9
  81.1 0.8 copy-done.9
  81.9 0.0 copy-start.2
  81.9 0.0 copy-start.3
  81.9 0.0 copy-start.7
  81.9 0.0 copy-start.8
  81.9 0.0 collective-permute-done
  81.9 0.0 copy-start.10
  82.0 1.2 add.3
  83.2 0.7 all-to-all-done.2
  83.9 14.5 %all_to_all.25 = f32[8,128,128]{2,1,0:T(8,128)S(1)} all-to-all(f32[8,128,128]{2,1,0:T(8,128)S(1)} %bitcast.16), channel_id=1, replica_groups={{0,2,4,6,8,10,12,14},{1,3,5,7,9,11,13,15},{16,18,20,22,24,26,28,30},{17..., dimensions={0} | all-to-all | bytes 1048576 | tf_op jit(solution)/shard_map/all_to_all | solution.py:318
  98.5 11.3 %all_to_all.26 = bf16[8,128,128]{2,1,0:T(8,128)(2,1)S(1)} all-to-all(bf16[8,128,128]{2,1,0:T(8,128)(2,1)S(1)} %broadcast_in_dim.5), channel_id=1, replica_groups={{0,2,4,6,8,10,12,14},{1,3,5,7,9,11,13,15},{16,18,20,22,24,26,28,30},{17..., dimensions={0} | all-to-all | bytes 524288 | tf_op jit(solution)/shard_map/all_to_all | solution.py:321
  109.8 0.0 collective-permute-start.1
  109.8 1.5 %collective-permute-done.1.other_ref = bf16[32,32,128]{2,1,0:T(8,128)(2,1)S(1)} collective-permute-done((bf16[32,32,128]{2,1,0:T(8,128)(2,1)S(1)}, bf16[32,32,128]{2,1,0:T(8,128)(2,1)S(1)}, u32[]{:S(2)}, u32[]{:S(2)}) %collective-permute-start.1) | collective-permute-done | bytes 262176 | tf_op jit(solution)/shard_map/ppermute | solution.py:338
  111.3 0.0 copy-done.2
  111.3 0.0 copy-done.3
  111.3 0.0 copy-done.7
  111.4 0.0 copy-done.8
  111.4 0.0 copy-done.10
  111.4 16.1 %voxel_mlp.1 = bf16[64,16,32,128]{3,2,1,0:T(8,128)(2,1)} custom-call(s32[1]{0:T(128)} %bitcast.half_ref, f32[64,16,128]{2,1,0:T(8,128)S(1)} %copy-done.10, bf16[32,32,128]{2,1,0:T(8,128)(2,1)S(1)} %bitcast.10, bf16[32,32,128]{2,1,0:T(8,128)(2,1)S(1)} %collective-permute-done.1.other_ref, bf16[16,32,128]{2,1,0:T(8,128)(2,1)S(1)} %bitcast.11, ...), custom_call_target="tpu_custom_call" | custom-call | flops 4294967296 | bytes 9437184 | tf_op jit(solution)/shard_map/voxel_mlp/pallas_call | solution.py:286
  (2 shorter events, 0.1 us)
Async XLA Ops:
  0.7 1.2 copy-start.1
  1.9 0.7 copy-start.4
  2.6 0.7 copy-start.5
  3.3 0.7 copy-start.6
  11.8 1.4 %copy-start = (bf16[128,72,128]{2,1,0:T(8,128)(2,1)}, bf16[128,72,128]{2,1,0:T(8,128)(2,1)S(1)}, u32[]{:S(2)}) copy-start(bf16[128,72,128]{2,1,0:T(8,128)(2,1)S(1)} %pack.1) | copy-start | bytes 7077892
  13.2 42.4 %all-to-all-start = ((bf16[128,72,128]{2,1,0:T(8,128)(2,1)}), bf16[128,72,128]{2,1,0:T(8,128)(2,1)S(1)}, u32[]{:S(2)}, u32[]{:S(2)}) async-start(bf16[128,72,128]{2,1,0:T(8,128)(2,1)} %copy-done), calls=%async_computation | async-start | bytes 4718592 | tf_op jit(solution)/shard_map/all_to_all | solution.py:330
  58.7 0.7 copy-start.11
  59.3 12.7 %all-to-all-start.1 = ((f32[8,64,128]{2,1,0:T(8,128)}), f32[8,64,128]{2,1,0:T(8,128)}, u32[]{:S(2)}, u32[]{:S(2)}) async-start(f32[8,64,128]{2,1,0:T(8,128)} %bitcast.3), calls=%async_computation.1 | async-start | bytes 524288 | tf_op jit(solution)/shard_map/all_to_all | solution.py:318
  63.6 0.9 copy-start.12
  69.6 12.4 %collective-permute-start = (f32[32,32,128]{2,1,0:T(8,128)S(1)}, f32[32,32,128]{2,1,0:T(8,128)}, u32[]{:S(2)}, u32[]{:S(2)}) collective-permute-start(f32[32,32,128]{2,1,0:T(8,128)S(1)} %get-tuple-element.14), channel_id=1, source_target_pairs={{0,1},{1,0},{2,3},{3,2},{4,5},{5,4},{6,7},{7,6},{8,9},{9,8},{10,11... | collective-permute-start | bytes 1572872 | tf_op jit(solution)/shard_map/ppermute | solution.py:334
  73.7 10.2 %all-to-all-start.2 = ((bf16[8,64,128]{2,1,0:T(8,128)(2,1)}), bf16[8,64,128]{2,1,0:T(8,128)(2,1)S(1)}, u32[]{:S(2)}, u32[]{:S(2)}) async-start(bf16[8,64,128]{2,1,0:T(8,128)(2,1)} %broadcast_in_dim.4), calls=%async_computation.2 | async-start | bytes 262144 | tf_op jit(solution)/shard_map/all_to_all | solution.py:321
  77.3 0.9 copy-start.13
  81.1 0.8 copy-start.9
  81.9 29.4 %copy-start.2 = (bf16[128,256]{1,0:T(8,128)(2,1)S(1)}, bf16[128,256]{1,0:T(8,128)(2,1)}, u32[]{:S(2)}) copy-start(bf16[128,256]{1,0:T(8,128)(2,1)} %w_in_ref.1) | copy-start | bytes 196612
  81.9 29.4 %copy-start.3 = (bf16[256,128]{1,0:T(8,128)(2,1)S(1)}, bf16[256,128]{1,0:T(8,128)(2,1)}, u32[]{:S(2)}) copy-start(bf16[256,128]{1,0:T(8,128)(2,1)} %w_out_ref.1) | copy-start | bytes 196612
  81.9 29.4 %copy-start.7 = (f32[256]{0:T(256)S(1)}, f32[256]{0:T(256)}, u32[]{:S(2)}) copy-start(f32[256]{0:T(256)} %param.16) | copy-start | bytes 3076
  81.9 29.4 %copy-start.8 = (f32[128]{0:T(128)S(1)}, f32[128]{0:T(128)}, u32[]{:S(2)}) copy-start(f32[128]{0:T(128)} %param.18) | copy-start | bytes 1540
  81.9 29.4 %copy-start.10 = (f32[64,16,128]{2,1,0:T(8,128)S(1)}, f32[64,16,128]{2,1,0:T(8,128)}, u32[]{:S(2)}) copy-start(f32[64,16,128]{2,1,0:T(8,128)} %copy-done.9) | copy-start | bytes 1572868
  109.8 1.5 %collective-permute-start.1 = (bf16[32,32,128]{2,1,0:T(8,128)(2,1)S(1)}, bf16[32,32,128]{2,1,0:T(8,128)(2,1)S(1)}, u32[]{:S(2)}, u32[]{:S(2)}) collective-permute-start(bf16[32,32,128]{2,1,0:T(8,128)(2,1)S(1)} %bitcast.9), channel_id=1, source_target_pairs={{0,1},{1,0},{2,3},{3,2},{4,5},{5,4},{6,7},{7,6},{8,9},{9,8},{10,11... | collective-permute-start | bytes 786440 | tf_op jit(solution)/shard_map/ppermute | solution.py:338

commit v3 on v2

--- a/solution.py
+++ b/solution.py
@@ -23,7 +23,8 @@
 
 F32 = jnp.float32
 BF16 = jnp.bfloat16
-VMEM_LIMIT = 48 * 2**20
+VMEM_LIMIT = 24 * 2**20
+PACK_LIMIT = 60 * 2**20
 
 
 def iota(shape, axis):
@@ -52,9 +53,20 @@
 
 
 def pack_kernel(
-    cam_ref, feats_ref, top_ref, front_ref, embed_ref, out_ref,
-    marks_ref, rank_ref, place_ref, half_ref, rhs_ref, values_ref, sorted_ref, meta_ref, start_ref, start_smem, sem,
+    cam_ref, feats_hbm, top_hbm, front_hbm, embed_hbm, out_hbm,
+    feats_ref, top_ref, front_ref, embed_ref, out_ref,
+    marks_ref, rank_ref, place_ref, half_ref, rhs_ref, values_ref, sorted_ref, meta_ref, start_ref, start_smem, sems,
 ):
+    loads = [
+        pltpu.make_async_copy(source, target, sems.at[i])
+        for i, (source, target) in enumerate(
+            [(top_hbm, top_ref), (front_hbm, front_ref), (embed_hbm, embed_ref), (feats_hbm, feats_ref)]
+        )
+    ]
+    for load in loads:
+        load.start()
+    loads[0].wait()
+    loads[1].wait()
     top = top_ref[...]
     live = top >= 0
     grid_x = top >> 8
@@ -76,7 +88,7 @@
         jnp.where(iota((128, 128), 0) == iota((128, 128), 1), starts, 0.0), axis=0, keepdims=True
     )
     start_ref[...] = start_row.astype(jnp.int32)
-    copy = pltpu.make_async_copy(start_ref, start_smem, sem)
+    copy = pltpu.make_async_copy(start_ref, start_smem, sems.at[4])
     copy.start()
 
     before = iota((128, 256), 0) < iota((128, 256), 1)
@@ -101,6 +113,8 @@
     half_ref[...] = (place >> 11).astype(F32)
     place_ref[...] = jnp.where(live, place & 2047, -1).astype(F32)
 
+    loads[2].wait()
+    loads[3].wait()
     camera = embed_ref[pl.ds(cam_ref[0], 1), :]
     for k in range(CHUNKS):
         rows = slice(k * 128, (k + 1) * 128)
@@ -126,19 +140,34 @@
 
     copy.wait()
 
-    @pl.loop(0, DEVICES, unroll=8)
-    def _(device):
-        out_ref[device, 0:CAP, :] = sorted_ref[pl.ds(start_smem[0, device], CAP), :].astype(BF16)
+    stores = []
+    for part in range(4):
+
+        @pl.loop(0, DEVICES // 4, unroll=8)
+        def _(i):
+            device = part * (DEVICES // 4) + i
+            out_ref[device, 0:CAP, :] = sorted_ref[pl.ds(start_smem[0, device], CAP), :].astype(BF16)
+
+        here = pl.ds(part * (DEVICES // 4), DEVICES // 4)
+        stores.append(pltpu.make_async_copy(out_ref.at[here], out_hbm.at[here], sems.at[5 + part]))
+        stores[-1].start()
+    for store in stores:
+        store.wait()
 
 
 def pack(camera, point_feats, top_bin, front_bin, camera_embed):
-    whole = pl.BlockSpec(memory_space=pltpu.VMEM)
+    whole = pl.BlockSpec(memory_space=pltpu.HBM)
     return pl.pallas_call(
         pack_kernel,
         out_shape=jax.ShapeDtypeStruct((DEVICES, ROWS, C), BF16),
         in_specs=[pl.BlockSpec(memory_space=pltpu.SMEM)] + [whole] * 4,
         out_specs=whole,
         scratch_shapes=[
+            pltpu.VMEM((P_DEV, C), BF16),
+            pltpu.VMEM((CHUNKS, 128), jnp.int32),
+            pltpu.VMEM((CHUNKS, 128), jnp.int32),
+            pltpu.VMEM((CAMS, C), F32),
+            pltpu.VMEM((DEVICES, ROWS, C), BF16),
             pltpu.VMEM((DEVICES, P_DEV), BF16),
             pltpu.VMEM((CHUNKS, 128), jnp.int32),
             pltpu.VMEM((CHUNKS, 128), F32),
@@ -149,36 +178,12 @@
             pltpu.VMEM((DEVICES * 8, 128), F32),
             pltpu.VMEM((1, DEVICES), jnp.int32),
             pltpu.SMEM((1, DEVICES), jnp.int32),
-            pltpu.SemaphoreType.DMA,
+            pltpu.SemaphoreType.DMA((9,)),
         ],
-        compiler_params=pltpu.CompilerParams(vmem_limit_bytes=VMEM_LIMIT),
+        compiler_params=pltpu.CompilerParams(vmem_limit_bytes=PACK_LIMIT),
         cost_estimate=pl.CostEstimate(flops=2 * 4096 * 4096 * 256, bytes_accessed=4 * 2**20, transcendentals=0),
         name="pack",
     )(camera, point_feats, top_bin.reshape(CHUNKS, 128), front_bin.reshape(CHUNKS, 128), camera_embed)
-
-
-def pool_side_kernel(half_ref, got_ref, side_ref, labels_ref, meta_ref):
-    meta_ref[...] = got_ref[:, CAP:ROWS, :].astype(F32).reshape(DEVICES * 8, 128)
-    first = iota((PAIRS, 128), 1) < CAP
-
-    def pairs(part):
-        even = meta_ref[pl.ds(part, PAIRS, stride=16), :]
-        odd = meta_ref[pl.ds(part + 8, PAIRS, stride=16), :]
-        return jnp.where(first, even, odd).astype(jnp.int32) - 1
-
-    x, y, z = pairs(0), pairs(1), pairs(2)
-    live = x >= 0
-    x = x ^ (half_ref[0] * (BX // 2))
-    labels_ref[0] = jnp.where(live, x * 16 + (z & 15), -1)
-    labels_ref[1] = jnp.where(live, x * 8 + (y & 7), -1)
-    labels_ref[2] = jnp.where(live, y * 32 + z, -1)
-    labels_ref[3] = (y >> 3) & 1
-    labels_ref[4] = (z >> 4) & 1
-
-    points = got_ref[:, 0:CAP, :].reshape(SLOTS, C)
-    for block in range(2):
-        sums = jnp.dot(onehot(labels_ref.at[2], block * 256, 256, PAIRS), points, preferred_element_type=F32)
-        side_ref[block * 8 : block * 8 + 8] = sums.reshape(8, NZ, C)
 
 
 def split_points(got_ref, half_ref, rhs_ref):
@@ -188,7 +193,23 @@
         rhs_ref[q * 128 : (q + 1) * 128, :] = split_columns(piece, half)
 
 
-def pool_front_kernel(got_ref, labels_ref, mine_ref, other_ref, rhs_ref):
+def pool_front_kernel(place_ref, got_ref, mine_ref, other_ref, labels_ref, meta_ref, rhs_ref):
+    meta_ref[...] = got_ref[:, CAP:ROWS, :].astype(F32).reshape(DEVICES * 8, 128)
+    first = iota((PAIRS, 128), 1) < CAP
+
+    def pairs(part):
+        even = meta_ref[pl.ds(part, PAIRS, stride=16), :]
+        odd = meta_ref[pl.ds(part + 8, PAIRS, stride=16), :]
+        return jnp.where(first, even, odd).astype(jnp.int32) - 1
+
+    x, y, z = pairs(0), pairs(1), pairs(2)
+    live = x >= 0
+    x = x ^ (place_ref[0] * (BX // 2))
+    labels_ref[0] = jnp.where(live, x * 16 + (z & 15), -1)
+    labels_ref[1] = jnp.where(live, x * 8 + (y & 7), -1)
+    labels_ref[2] = jnp.where(live, (y ^ place_ref[1]) * 32 + z, -1)
+    labels_ref[3] = (y >> 3) & 1
+    labels_ref[4] = (z >> 4) & 1
     split_points(got_ref, labels_ref.at[4], rhs_ref)
     for block in range(4):
         sums = jnp.dot(onehot(labels_ref.at[0], block * 256, 256, PAIRS), rhs_ref[...], preferred_element_type=F32)
@@ -198,6 +219,13 @@
         out[xs, 16:32, :] = sums[:, C:].reshape(16, 16, C)
 
 
+def pool_side_kernel(got_ref, labels_ref, keep_ref, send_ref):
+    points = got_ref[:, 0:CAP, :].reshape(SLOTS, C)
+    for block, out in enumerate((keep_ref, send_ref)):
+        sums = jnp.dot(onehot(labels_ref.at[2], block * 256, 256, PAIRS), points, preferred_element_type=F32)
+        out[...] = sums.reshape(BY // 2, NZ, C)
+
+
 def pool_top_kernel(got_ref, labels_ref, top_ref, rhs_ref):
     split_points(got_ref, labels_ref.at[3], rhs_ref)
     for block in range(2):
@@ -213,7 +241,7 @@
     return pl.pallas_call(
         kernel,
         out_shape=outs,
-        in_specs=[small if i.dtype == jnp.int32 and i.size == 1 else whole for i in ins],
+        in_specs=[small if i.dtype == jnp.int32 and i.size == 2 else whole for i in ins],
         out_specs=[whole] * len(outs),
         scratch_shapes=scratch,
         compiler_params=pltpu.CompilerParams(vmem_limit_bytes=VMEM_LIMIT),
@@ -222,21 +250,32 @@
     )(*ins)
 
 
-def pool_side(half, got):
+def pool_front(place, got):
+    shape = jax.ShapeDtypeStruct((BX // 2, NZ, C), F32)
     return call(
-        pool_side_kernel,
-        [half, got],
-        [jax.ShapeDtypeStruct((BY, NZ, C), F32), jax.ShapeDtypeStruct((5, PAIRS, 128), jnp.int32)],
-        [pltpu.VMEM((DEVICES * 8, 128), F32)],
-        2 * 8192 * 512 * 256,
-        "pool_side",
-    )
-
-
-def pool_front(got, labels):
-    shape = jax.ShapeDtypeStruct((BX // 2, NZ, C), F32)
-    scratch = [pltpu.VMEM((SLOTS, 2 * C), BF16)]
-    return call(pool_front_kernel, [got, labels], [shape, shape], scratch, 2 * 8192 * 1024 * 256 * 2, "pool_front")
+        pool_front_kernel,
+        [place, got],
+        [shape, shape, jax.ShapeDtypeStruct((5, PAIRS, 128), jnp.int32)],
+        [pltpu.VMEM((DEVICES * 8, 128), F32), pltpu.VMEM((SLOTS, 2 * C), BF16)],
+        2 * 8192 * 1024 * 256 * 2,
+        "pool_front",
+    )
+
+
+def pool_side(got, labels):
+    shape = jax.ShapeDtypeStruct((BY // 2, NZ, C), F32)
+    return call(pool_side_kernel, [got, labels], [shape, shape], [], 2 * 8192 * 512 * 256, "pool_side")
+
+
+def fold_kernel(keep_ref, got_ref, *out_refs):
+    for k, out in enumerate(out_refs):
+        rows = pl.ds(k * 2, 2)
+        out[...] = keep_ref[rows] + got_ref[rows]
+
+
+def fold(keep, got):
+    shape = jax.ShapeDtypeStruct((2, NZ, C), F32)
+    return call(fold_kernel, [keep, got], [shape] * 4, [], 1024, "fold")
 
 
 def pool_top(got, labels):
@@ -258,7 +297,15 @@
 STEP = 4
 
 
-def mlp_kernel(half_ref, top_ref, mine_ref, other_ref, side_ref, w_in_ref, b_in_ref, w_out_ref, b_out_ref, out_ref):
+def mlp_kernel(
+    place_ref, top_ref, mine_ref, other_ref, near_ref, far_ref, w_in_ref, b_in_ref, w_out_ref, b_out_ref, out_ref, side_ref
+):
+    @pl.when(pl.program_id(0) == 0)
+    def _():
+        for y in range(BY // 2):
+            side_ref[y ^ place_ref[1]] = near_ref[y]
+            side_ref[(y + BY // 2) ^ place_ref[1]] = far_ref[y]
+
     def work(front_ref):
         for i in range(STEP):
             top = top_ref[i].astype(BF16).astype(F32)
@@ -279,7 +326,7 @@
 HALF_STEPS = BX // STEP // 2
 
 
-def mlp(half, top, mine, other, side, w_in, b_in, w_out, b_out):
+def mlp(place, top, mine, other, near, far, w_in, b_in, w_out, b_out):
     def same(*shape):
         return pl.BlockSpec(shape, lambda i, h: (0,) * len(shape))
 
@@ -292,13 +339,15 @@
                 pl.BlockSpec((STEP, BY, C), lambda i, h: (i, 0, 0)),
                 pl.BlockSpec((STEP, NZ, C), lambda i, h: (jnp.minimum(i, HALF_STEPS - 1), 0, 0)),
                 pl.BlockSpec((STEP, NZ, C), lambda i, h: (jnp.maximum(i - HALF_STEPS, 0), 0, 0)),
-                same(BY, NZ, C),
+                same(BY // 2, NZ, C),
+                same(BY // 2, NZ, C),
                 same(C, HID),
                 same(1, HID),
                 same(HID, C),
                 same(1, C),
             ],
             out_specs=pl.BlockSpec((STEP, BY, NZ, C), lambda i, h: (i ^ (h[0] * HALF_STEPS), 0, 0, 0)),
+            scratch_shapes=[pltpu.VMEM((BY, NZ, C), BF16)],
         ),
         out_shape=jax.ShapeDtypeStruct((BX, BY, NZ, C), BF16),
         compiler_params=pltpu.CompilerParams(vmem_limit_bytes=VMEM_LIMIT),
@@ -306,37 +355,60 @@
             flops=4 * BX * BY * NZ * C * HID, bytes_accessed=9 * 2**20, transcendentals=BX * BY * NZ * HID
         ),
         name="voxel_mlp",
-    )(half, top, mine, other, side, w_in, b_in.reshape(1, HID), w_out, b_out.reshape(1, C))
+    )(place, top, mine, other, near, far, w_in, b_in.reshape(1, HID), w_out, b_out.reshape(1, C))
 
 
 SAME_CORE = [list(range(core, N_GY, 2)) for core in range(2)]
-OTHER_CORE = [(i, i ^ 1) for i in range(N_GY)]
-
-
-def plane_sum(part, axis, groups=None):
-    rows = part.shape[0] * part.shape[1] // 8
-    pieces = lax.all_to_all(part.reshape(8, rows, C), axis, 0, 0, tiled=True, axis_index_groups=groups)
-    share = jnp.sum(pieces, axis=0).astype(BF16)
-    copies = jnp.broadcast_to(share[None], (8, rows, C))
-    whole = lax.all_to_all(copies, axis, 0, 0, tiled=True, axis_index_groups=groups)
-    return whole.reshape(part.shape)
+
+
+def swap(array, axis, size, bit):
+    return lax.ppermute(array, axis, [(i, i ^ bit) for i in range(size)])
+
+
+def front_share(mine):
+    pieces = mine.reshape(8, mine.shape[0] * mine.shape[1] // 8, C)
+    pieces = lax.all_to_all(pieces, "gy", 0, 0, tiled=True, axis_index_groups=SAME_CORE)
+    return jnp.sum(pieces, axis=0).astype(BF16)
+
+
+def front_gather(share):
+    copies = jnp.broadcast_to(share[None], (8,) + share.shape)
+    whole = lax.all_to_all(copies, "gy", 0, 0, tiled=True, axis_index_groups=SAME_CORE)
+    return whole.reshape(BX // 2, NZ, C)
+
+
+def side_share(keep, send):
+    parts = fold(keep, swap(send, "gx", N_GX, 4))
+    return (
+        parts[0] + swap(parts[1], "gx", N_GX, 2) + swap(parts[2], "gx", N_GX, 1) + swap(parts[3], "gx", N_GX, 3)
+    ).astype(BF16)
+
+
+def side_gather(share):
+    near = jnp.concatenate([share] + [swap(share, "gx", N_GX, bit) for bit in (2, 1, 3)], axis=0)
+    return near, swap(near, "gx", N_GX, 4)
 
 
 def per_device(
     point_feats, top_bin, front_bin, side_bin, camera_of_device, camera_embed, w_in, b_in, w_out, b_out
 ):
-    half = (lax.axis_index("gy") & 1).astype(jnp.int32).reshape(1)
+    row = lax.axis_index("gx")
+    place = jnp.stack(
+        [lax.axis_index("gy") & 1, (row >> 2 & 1) * 8 + (row & 1) * 4 + (row >> 1 & 1) * 2]
+    ).astype(jnp.int32)
     sent = pack(camera_of_device, point_feats, top_bin, front_bin, camera_embed)
     got = lax.all_to_all(sent, ("gx", "gy"), split_axis=0, concat_axis=0, tiled=True)
-    side_part, labels = pool_side(half, got)
-    side = plane_sum(side_part, "gx")
-    mine, other = pool_front(got, labels)
-    mine = mine + lax.ppermute(other, "gy", OTHER_CORE)
+    mine, other, labels = pool_front(place, got)
+    keep, send = pool_side(got, labels)
+    mine = mine + swap(other, "gy", N_GY, 1)
+    mine, keep, send = lax.optimization_barrier((mine, keep, send))
     top = pool_top(got, labels)
-    mine, top, side = lax.optimization_barrier((mine, top, side))
-    mine = plane_sum(mine, "gy", SAME_CORE)
-    other = lax.ppermute(mine, "gy", OTHER_CORE)
-    return mlp(half, top, mine, other, side, w_in, b_in, w_out, b_out)
+    shares = (front_share(mine), side_share(keep, send), top)
+    front, side, top = lax.optimization_barrier(shares)
+    mine = front_gather(front)
+    near, far = side_gather(side)
+    other = swap(mine, "gy", N_GY, 1)
+    return mlp(place, top, mine, other, near, far, w_in, b_in, w_out, b_out)
 
 
 def solution(mesh):

time: 129 us -> 116 us (0.90)
  blocking collectives: 25.8 us -> 0 us
  starting transfers between devices: 20 us -> 31.2 us
  local copies, waits for them, and re-layouts: 8.73 us -> 0.78 us
  waiting for transfers between devices: 35 us -> 42.2 us
  Pallas kernels: 34.9 us -> 38.4 us
    all_to_all x2 -> x0, blocking collectives: 25.8 us -> none  [the longest x1 14.5 us: plane_sum(): lax.all_to_all(part.reshape(8, rows, C), axis, 0, 0, tiled=True, axis_ind...]
    ppermute x2 -> x10, starting transfers between devices: 0.96 us -> 11.7 us  [swap(): return lax.ppermute(array, axis, [(i, i ^ bit) for i in range(size)])]
    unnamed x28 -> x11, local copies, waits for them, and re-layouts: 8.03 us -> 0.03 us
    ppermute x2 -> x10, waiting for transfers between devices: 1.54 us -> 7.03 us  [swap(): return lax.ppermute(array, axis, [(i, i ^ bit) for i in range(size)])]
    pallas_call x1, Pallas kernels: 7.8 us -> 10.7 us  [pack(): pl.pallas_call(pack_kernel, out_shape=jax.ShapeDtypeStruct((DEVICES, ROWS...]
    all_to_all x2, waiting for transfers between devices: 2.24 us -> 4.2 us  [the longest x1 2.5 us: front_share(): lax.all_to_all(pieces, 'gy', 0, 0, tiled=True, axis_index_groups=SAME_CORE)]
    pallas_call x3 -> x4, Pallas kernels: 11 us -> 10.9 us  [call(): pl.pallas_call(kernel, out_shape=outs, in_specs=[small if i.dtype == jnp....]
  transfers between devices with their start and end apart: 5 -> 13, of which waited for: 4 -> 7; matrix products, arithmetic and copies ran while one was open for 2% -> 0% of each run, Pallas kernels for 6% -> 5%
where the time goes in v3:
time: 116 us; the launch traced here: 115 us
  waiting for transfers between devices  42.2 us (36%)
  Pallas kernels  38.4 us (33%)
  starting transfers between devices  31.2 us (27%)
  other arithmetic  2.03 us (2%)
    all_to_all x1, waiting for transfers between devices, per_device(): lax.all_to_all(sent, ('gx', 'gy'), split_axis=0, concat_axis=0, tiled=True)  31 us
    pallas_call x1, Pallas kernels, mlp(): pl.pallas_call(mlp_kernel, grid_spec=pltpu.PrefetchScalarGridSpec(num_sca...  16.8 us
    ppermute x10, starting transfers between devices, swap(): return lax.ppermute(array, axis, [(i, i ^ bit) for i in range(size)])  11.7 us
    all_to_all x1, starting transfers between devices, per_device(): lax.all_to_all(sent, ('gx', 'gy'), split_axis=0, concat_axis=0, tiled=True)  11.3 us
    pallas_call x4, Pallas kernels, call(): pl.pallas_call(kernel, out_shape=outs, in_specs=[small if i.dtype == jnp....  10.9 us
    pallas_call x1, Pallas kernels, pack(): pl.pallas_call(pack_kernel, out_shape=jax.ShapeDtypeStruct((DEVICES, ROWS...  10.7 us
    ppermute x10, waiting for transfers between devices, swap(): return lax.ppermute(array, axis, [(i, i ^ bit) for i in range(size)])  7.03 us
    all_to_all x1, starting transfers between devices, front_share(): lax.all_to_all(pieces, 'gy', 0, 0, tiled=True, axis_index_groups=SAME_CORE)  4.14 us
  transfers between devices with their start and end apart: 13, of which 7 were waited for; matrix products, arithmetic and copies ran while one was open for 0% of the time, Pallas kernels for 5%

profile of v3, /device:TPU:0, one launch (start us, length us, event | category | flops | bytes accessed | tf_op | source)
XLA Modules:
  0.0 115.4 jit_solution(7599602321956146879)
XLA Ops:
  0.7 10.7 %pack.1 = bf16[128,72,128]{2,1,0:T(8,128)(2,1)} custom-call(s32[1]{0:T(128)S(6)} %copy.13.cam_ref, bf16[4096,128]{1,0:T(8,128)(2,1)} %feats_hbm.1, s32[32,128]{1,0:T(8,128)} %bitcast.13, s32[32,128]{1,0:T(8,128)} %bitcast.14, f32[6,128]{1,0:T(8,128)} %embed_hbm.1), custom_call_target="tpu_custom_call" | custom-call | flops 8589934592 | bytes 4194304 | tf_op jit(solution)/shard_map/pack/pallas_call | solution.py:160
  11.3 11.3 %all-to-all-start = ((bf16[128,72,128]{2,1,0:T(8,128)(2,1)}), bf16[128,72,128]{2,1,0:T(8,128)(2,1)S(1)}, u32[]{:S(2)}, u32[]{:S(2)}) async-start(bf16[128,72,128]{2,1,0:T(8,128)(2,1)} %pack.1), calls=%async_computation | async-start | bytes 4718592 | tf_op jit(solution)/shard_map/all_to_all | solution.py:400
  22.7 0.1 pad_add_fusion.place_ref
  22.8 31.0 %all-to-all-done.got_ref = bf16[128,72,128]{2,1,0:T(8,128)(2,1)S(1)} async-done(((bf16[128,72,128]{2,1,0:T(8,128)(2,1)}), bf16[128,72,128]{2,1,0:T(8,128)(2,1)S(1)}, u32[]{:S(2)}, u32[]{:S(2)}) %all-to-all-start) | async-done | bytes 2359328 | tf_op jit(solution)/shard_map/all_to_all | solution.py:400
  53.7 5.7 %pool_front.1 = (f32[32,32,128]{2,1,0:T(8,128)S(1)}, f32[32,32,128]{2,1,0:T(8,128)S(1)}, s32[5,64,128]{2,1,0:T(8,128)S(1)}) custom-call(s32[2]{0:T(128)S(1)} %pad_add_fusion.place_ref, bf16[128,72,128]{2,1,0:T(8,128)(2,1)S(1)} %all-to-all-done.got_ref), custom_call_target="tpu_custom_call" | custom-call | flops 8589934592 | bytes 4194304 | tf_op jit(solution)/shard_map/pool_front/pallas_call | solution.py:241
  59.4 1.0 collective-permute-start
  60.4 2.3 %pool_side.1 = (f32[8,32,128]{2,1,0:T(8,128)S(1)}, f32[8,32,128]{2,1,0:T(8,128)S(1)}) custom-call(bf16[128,72,128]{2,1,0:T(8,128)(2,1)S(1)} %all-to-all-done.got_ref, s32[5,64,128]{2,1,0:T(8,128)S(1)} %get-tuple-element.22.labels_ref), custom_call_target="tpu_custom_call" | custom-call | flops 2147483648 | bytes 4194304 | tf_op jit(solution)/shard_map/pool_side/pallas_call | solution.py:241
  62.7 0.0 collective-permute-done
  62.7 0.9 add.20
  63.6 0.8 collective-permute-start.1
  64.4 4.1 %all-to-all-start.1 = ((f32[8,128,128]{2,1,0:T(8,128)}), f32[8,128,128]{2,1,0:T(8,128)}, u32[]{:S(2)}, u32[]{:S(2)}) async-start(f32[8,128,128]{2,1,0:T(8,128)} %bitcast.12), calls=%async_computation.1 | async-start | bytes 1048576 | tf_op jit(solution)/shard_map/all_to_all | solution.py:370
  68.6 0.4 collective-permute-done.1.got_ref
  69.0 2.2 %collective-permute-start.2 = (f32[2,32,128]{2,1,0:T(8,128)S(1)}, f32[2,32,128]{2,1,0:T(8,128)S(1)}, u32[]{:S(2)}, u32[]{:S(2)}) collective-permute-start(f32[2,32,128]{2,1,0:T(8,128)S(1)} %get-tuple-element.29), channel_id=1, source_target_pairs={{0,32},{16,48},{32,0},{48,16},{64,96},{80,112},{96,64},{112,80},{1... | collective-permute-start | bytes 98312 | tf_op jit(solution)/shard_map/ppermute | solution.py:365
  71.2 0.7 collective-permute-start.3
  71.9 0.0 copy-start
  71.9 0.0 copy-start.1
  71.9 0.0 copy-start.2
  71.9 0.0 copy-start.3
  71.9 1.4 %collective-permute-start.4 = (f32[2,32,128]{2,1,0:T(8,128)S(1)}, f32[2,32,128]{2,1,0:T(8,128)S(1)}, u32[]{:S(2)}, u32[]{:S(2)}) collective-permute-start(f32[2,32,128]{2,1,0:T(8,128)S(1)} %get-tuple-element.31), channel_id=1, source_target_pairs={{0,48},{16,32},{32,16},{48,0},{64,112},{80,96},{96,80},{112,64},{1... | collective-permute-start | bytes 98312 | tf_op jit(solution)/shard_map/ppermute | solution.py:365
  73.3 2.9 %pool_top.1.top_ref = f32[64,16,128]{2,1,0:T(8,128)S(1)} custom-call(bf16[128,72,128]{2,1,0:T(8,128)(2,1)S(1)} %all-to-all-done.got_ref, s32[5,64,128]{2,1,0:T(8,128)S(1)} %get-tuple-element.22.labels_ref), custom_call_target="tpu_custom_call" | custom-call | flops 6442450944 | bytes 4194304 | tf_op jit(solution)/shard_map/pool_top/pallas_call | solution.py:241
  76.2 0.0 collective-permute-done.2
  76.2 0.0 collective-permute-done.3
  76.2 0.9 collective-permute-done.4
  77.2 2.5 %all-to-all-done.1 = f32[8,128,128]{2,1,0:T(8,128)} async-done(((f32[8,128,128]{2,1,0:T(8,128)}), f32[8,128,128]{2,1,0:T(8,128)}, u32[]{:S(2)}, u32[]{:S(2)}) %all-to-all-start.1) | async-done | bytes 524320 | tf_op jit(solution)/shard_map/all_to_all | solution.py:370
  79.6 1.1 reduce_sum.9
  80.7 0.7 broadcast_in_dim.2
  81.5 4.0 %all-to-all-start.2 = ((bf16[8,128,128]{2,1,0:T(8,128)(2,1)}), bf16[8,128,128]{2,1,0:T(8,128)(2,1)S(1)}, u32[]{:S(2)}, u32[]{:S(2)}) async-start(bf16[8,128,128]{2,1,0:T(8,128)(2,1)} %broadcast_in_dim.2), calls=%async_computation.2 | async-start | bytes 524288 | tf_op jit(solution)/shard_map/all_to_all | solution.py:376
  85.5 1.5 %collective-permute-start.8 = (bf16[2,32,128]{2,1,0:T(8,128)(2,1)S(1)}, bf16[2,32,128]{2,1,0:T(8,128)(2,1)S(1)}, u32[]{:S(2)}, u32[]{:S(2)}) collective-permute-start(bf16[2,32,128]{2,1,0:T(8,128)(2,1)S(1)} %add_convert_fusion), channel_id=1, source_target_pairs={{0,48},{16,32},{32,16},{48,0},{64,112},{80,96},{96,80},{112,64},{1... | collective-permute-start | bytes 49160 | tf_op jit(solution)/shard_map/ppermute | solution.py:365
  87.0 0.0 collective-permute-start.7
  87.0 3.2 %collective-permute-start.6 = (bf16[2,32,128]{2,1,0:T(8,128)(2,1)S(1)}, bf16[2,32,128]{2,1,0:T(8,128)(2,1)S(1)}, u32[]{:S(2)}, u32[]{:S(2)}) collective-permute-start(bf16[2,32,128]{2,1,0:T(8,128)(2,1)S(1)} %add_convert_fusion), channel_id=1, source_target_pairs={{0,32},{16,48},{32,0},{48,16},{64,96},{80,112},{96,64},{112,80},{1... | collective-permute-start | bytes 49160 | tf_op jit(solution)/shard_map/ppermute | solution.py:365
  90.2 2.0 %collective-permute-done.6 = bf16[2,32,128]{2,1,0:T(8,128)(2,1)S(1)} collective-permute-done((bf16[2,32,128]{2,1,0:T(8,128)(2,1)S(1)}, bf16[2,32,128]{2,1,0:T(8,128)(2,1)S(1)}, u32[]{:S(2)}, u32[]{:S(2)}) %collective-permute-start.6) | collective-permute-done | bytes 16416 | tf_op jit(solution)/shard_map/ppermute | solution.py:365
  92.2 1.7 %all-to-all-done.2 = bf16[8,128,128]{2,1,0:T(8,128)(2,1)S(1)} async-done(((bf16[8,128,128]{2,1,0:T(8,128)(2,1)}), bf16[8,128,128]{2,1,0:T(8,128)(2,1)S(1)}, u32[]{:S(2)}, u32[]{:S(2)}) %all-to-all-start.2) | async-done | bytes 262176 | tf_op jit(solution)/shard_map/all_to_all | solution.py:376
  93.9 0.0 collective-permute-start.5
  93.9 0.0 collective-permute-done.7
  93.9 0.0 collective-permute-done.8
  94.0 0.9 collective-permute-start.9
  94.9 3.6 %collective-permute-done.9.far_ref = bf16[8,32,128]{2,1,0:T(8,128)(2,1)S(1)} collective-permute-done((bf16[8,32,128]{2,1,0:T(8,128)(2,1)S(1)}, bf16[8,32,128]{2,1,0:T(8,128)(2,1)S(1)}, u32[]{:S(2)}, u32[]{:S(2)}) %collective-permute-start.9) | collective-permute-done | bytes 65568 | tf_op jit(solution)/shard_map/ppermute | solution.py:365
  98.5 0.0 collective-permute-done.5.other_ref
  98.6 0.0 copy-done
  98.6 0.0 copy-done.1
  98.6 0.0 copy-done.2
  98.6 0.0 copy-done.3
  98.6 16.8 %voxel_mlp.1 = bf16[64,16,32,128]{3,2,1,0:T(8,128)(2,1)} custom-call(s32[2]{0:T(128)S(1)} %pad_add_fusion.place_ref, f32[64,16,128]{2,1,0:T(8,128)S(1)} %pool_top.1.top_ref, bf16[32,32,128]{2,1,0:T(8,128)(2,1)S(1)} %bitcast.9, bf16[32,32,128]{2,1,0:T(8,128)(2,1)S(1)} %collective-permute-done.5.other_ref, ...), custom_call_target="tpu_custom_call" | custom-call | flops 4294967296 | bytes 9437184 | tf_op jit(solution)/shard_map/voxel_mlp/pallas_call | solution.py:333
  (6 shorter events, 0.1 us)
Async XLA Ops:
  11.3 42.4 %all-to-all-start = ((bf16[128,72,128]{2,1,0:T(8,128)(2,1)}), bf16[128,72,128]{2,1,0:T(8,128)(2,1)S(1)}, u32[]{:S(2)}, u32[]{:S(2)}) async-start(bf16[128,72,128]{2,1,0:T(8,128)(2,1)} %pack.1), calls=%async_computation | async-start | bytes 4718592 | tf_op jit(solution)/shard_map/all_to_all | solution.py:400
  59.4 3.3 %collective-permute-start = (f32[32,32,128]{2,1,0:T(8,128)S(1)}, f32[32,32,128]{2,1,0:T(8,128)S(1)}, u32[]{:S(2)}, u32[]{:S(2)}) collective-permute-start(f32[32,32,128]{2,1,0:T(8,128)S(1)} %get-tuple-element.21), channel_id=1, source_target_pairs={{0,1},{1,0},{2,3},{3,2},{4,5},{5,4},{6,7},{7,6},{8,9},{9,8},{10,11... | collective-permute-start | bytes 1572872 | tf_op jit(solution)/shard_map/ppermute | solution.py:365
  63.6 5.4 %collective-permute-start.1 = (f32[8,32,128]{2,1,0:T(8,128)S(1)}, f32[8,32,128]{2,1,0:T(8,128)S(1)}, u32[]{:S(2)}, u32[]{:S(2)}) collective-permute-start(f32[8,32,128]{2,1,0:T(8,128)S(1)} %get-tuple-element.27), channel_id=1, source_target_pairs={{0,64},{16,80},{32,96},{48,112},{64,0},{80,16},{96,32},{112,48},{1... | collective-permute-start | bytes 393224 | tf_op jit(solution)/shard_map/ppermute | solution.py:365
  64.4 15.2 %all-to-all-start.1 = ((f32[8,128,128]{2,1,0:T(8,128)}), f32[8,128,128]{2,1,0:T(8,128)}, u32[]{:S(2)}, u32[]{:S(2)}) async-start(f32[8,128,128]{2,1,0:T(8,128)} %bitcast.12), calls=%async_computation.1 | async-start | bytes 1048576 | tf_op jit(solution)/shard_map/all_to_all | solution.py:370
  69.0 7.2 %collective-permute-start.2 = (f32[2,32,128]{2,1,0:T(8,128)S(1)}, f32[2,32,128]{2,1,0:T(8,128)S(1)}, u32[]{:S(2)}, u32[]{:S(2)}) collective-permute-start(f32[2,32,128]{2,1,0:T(8,128)S(1)} %get-tuple-element.29), channel_id=1, source_target_pairs={{0,32},{16,48},{32,0},{48,16},{64,96},{80,112},{96,64},{112,80},{1... | collective-permute-start | bytes 98312 | tf_op jit(solution)/shard_map/ppermute | solution.py:365
  71.2 5.0 %collective-permute-start.3 = (f32[2,32,128]{2,1,0:T(8,128)S(1)}, f32[2,32,128]{2,1,0:T(8,128)S(1)}, u32[]{:S(2)}, u32[]{:S(2)}) collective-permute-start(f32[2,32,128]{2,1,0:T(8,128)S(1)} %get-tuple-element.30), channel_id=1, source_target_pairs={{0,16},{16,0},{32,48},{48,32},{64,80},{80,64},{96,112},{112,96},{1... | collective-permute-start | bytes 98312 | tf_op jit(solution)/shard_map/ppermute | solution.py:365
  71.9 26.6 %copy-start = (bf16[128,256]{1,0:T(8,128)(2,1)S(1)}, bf16[128,256]{1,0:T(8,128)(2,1)}, u32[]{:S(2)}) copy-start(bf16[128,256]{1,0:T(8,128)(2,1)} %w_in_ref.1) | copy-start | bytes 196612
  71.9 26.6 %copy-start.1 = (bf16[256,128]{1,0:T(8,128)(2,1)S(1)}, bf16[256,128]{1,0:T(8,128)(2,1)}, u32[]{:S(2)}) copy-start(bf16[256,128]{1,0:T(8,128)(2,1)} %w_out_ref.1) | copy-start | bytes 196612
  71.9 26.6 %copy-start.2 = (f32[256]{0:T(256)S(1)}, f32[256]{0:T(256)}, u32[]{:S(2)}) copy-start(f32[256]{0:T(256)} %param.16) | copy-start | bytes 3076
  71.9 26.6 %copy-start.3 = (f32[128]{0:T(128)S(1)}, f32[128]{0:T(128)}, u32[]{:S(2)}) copy-start(f32[128]{0:T(128)} %param.18) | copy-start | bytes 1540
  71.9 5.2 %collective-permute-start.4 = (f32[2,32,128]{2,1,0:T(8,128)S(1)}, f32[2,32,128]{2,1,0:T(8,128)S(1)}, u32[]{:S(2)}, u32[]{:S(2)}) collective-permute-start(f32[2,32,128]{2,1,0:T(8,128)S(1)} %get-tuple-element.31), channel_id=1, source_target_pairs={{0,48},{16,32},{32,16},{48,0},{64,112},{80,96},{96,80},{112,64},{1... | collective-permute-start | bytes 98312 | tf_op jit(solution)/shard_map/ppermute | solution.py:365
  81.5 12.5 %all-to-all-start.2 = ((bf16[8,128,128]{2,1,0:T(8,128)(2,1)}), bf16[8,128,128]{2,1,0:T(8,128)(2,1)S(1)}, u32[]{:S(2)}, u32[]{:S(2)}) async-start(bf16[8,128,128]{2,1,0:T(8,128)(2,1)} %broadcast_in_dim.2), calls=%async_computation.2 | async-start | bytes 524288 | tf_op jit(solution)/shard_map/all_to_all | solution.py:376
  85.5 8.5 %collective-permute-start.8 = (bf16[2,32,128]{2,1,0:T(8,128)(2,1)S(1)}, bf16[2,32,128]{2,1,0:T(8,128)(2,1)S(1)}, u32[]{:S(2)}, u32[]{:S(2)}) collective-permute-start(bf16[2,32,128]{2,1,0:T(8,128)(2,1)S(1)} %add_convert_fusion), channel_id=1, source_target_pairs={{0,48},{16,32},{32,16},{48,0},{64,112},{80,96},{96,80},{112,64},{1... | collective-permute-start | bytes 49160 | tf_op jit(solution)/shard_map/ppermute | solution.py:365
  87.0 7.0 %collective-permute-start.7 = (bf16[2,32,128]{2,1,0:T(8,128)(2,1)S(1)}, bf16[2,32,128]{2,1,0:T(8,128)(2,1)S(1)}, u32[]{:S(2)}, u32[]{:S(2)}) collective-permute-start(bf16[2,32,128]{2,1,0:T(8,128)(2,1)S(1)} %add_convert_fusion), channel_id=1, source_target_pairs={{0,16},{16,0},{32,48},{48,32},{64,80},{80,64},{96,112},{112,96},{1... | collective-permute-start | bytes 49160 | tf_op jit(solution)/shard_map/ppermute | solution.py:365
  87.0 5.2 %collective-permute-start.6 = (bf16[2,32,128]{2,1,0:T(8,128)(2,1)S(1)}, bf16[2,32,128]{2,1,0:T(8,128)(2,1)S(1)}, u32[]{:S(2)}, u32[]{:S(2)}) collective-permute-start(bf16[2,32,128]{2,1,0:T(8,128)(2,1)S(1)} %add_convert_fusion), channel_id=1, source_target_pairs={{0,32},{16,48},{32,0},{48,16},{64,96},{80,112},{96,64},{112,80},{1... | collective-permute-start | bytes 49160 | tf_op jit(solution)/shard_map/ppermute | solution.py:365
  93.9 4.6 %collective-permute-start.5 = (bf16[32,32,128]{2,1,0:T(8,128)(2,1)S(1)}, bf16[32,32,128]{2,1,0:T(8,128)(2,1)S(1)}, u32[]{:S(2)}, u32[]{:S(2)}) collective-permute-start(bf16[32,32,128]{2,1,0:T(8,128)(2,1)S(1)} %bitcast.8), channel_id=1, source_target_pairs={{0,1},{1,0},{2,3},{3,2},{4,5},{5,4},{6,7},{7,6},{8,9},{9,8},{10,11... | collective-permute-start | bytes 786440 | tf_op jit(solution)/shard_map/ppermute | solution.py:365
  94.0 4.6 %collective-permute-start.9 = (bf16[8,32,128]{2,1,0:T(8,128)(2,1)S(1)}, bf16[8,32,128]{2,1,0:T(8,128)(2,1)S(1)}, u32[]{:S(2)}, u32[]{:S(2)}) collective-permute-start(bf16[8,32,128]{2,1,0:T(8,128)(2,1)S(1)} %constant_dynamic-update-slice_fusion.near_ref), channel_id=1, source_target_pairs={{0,64},{16,80},{32,96},{48,112},{64,0},{80,16},{96,32},{112,48},{1... | collective-permute-start | bytes 196616 | tf_op jit(solution)/shard_map/ppermute | solution.py:365

commit v4 on v3

--- a/solution.py
+++ b/solution.py
@@ -25,6 +25,7 @@
 BF16 = jnp.bfloat16
 VMEM_LIMIT = 24 * 2**20
 PACK_LIMIT = 60 * 2**20
+MLP_LIMIT = 40 * 2**20
 
 
 def iota(shape, axis):
@@ -230,9 +231,8 @@
     split_points(got_ref, labels_ref.at[3], rhs_ref)
     for block in range(2):
         sums = jnp.dot(onehot(labels_ref.at[1], block * 256, 256, PAIRS), rhs_ref[...], preferred_element_type=F32)
-        xs = pl.ds(block * 32, 32)
-        top_ref[xs, 0:8, :] = sums[:, :C].reshape(32, 8, C)
-        top_ref[xs, 8:16, :] = sums[:, C:].reshape(32, 8, C)
+        halves = [sums[:, :C].reshape(32, 8, C), sums[:, C:].reshape(32, 8, C)]
+        top_ref[pl.ds(block * 32, 32)] = jnp.concatenate(halves, axis=1).astype(BF16)
 
 
 def call(kernel, ins, outs, scratch, flops, name):
@@ -245,7 +245,7 @@
         out_specs=[whole] * len(outs),
         scratch_shapes=scratch,
         compiler_params=pltpu.CompilerParams(vmem_limit_bytes=VMEM_LIMIT),
-        cost_estimate=pl.CostEstimate(flops=flops, bytes_accessed=4 * 2**20, transcendentals=0),
+        cost_estimate=pl.CostEstimate(flops=flops, bytes_accessed=flops // 1024, transcendentals=0),
         name=name,
     )(*ins)
 
@@ -282,51 +282,51 @@
     return call(
         pool_top_kernel,
         [got, labels],
-        [jax.ShapeDtypeStruct((BX, BY, C), F32)],
+        [jax.ShapeDtypeStruct((BX, BY, C), BF16)],
         [pltpu.VMEM((SLOTS, 2 * C), BF16)],
-        2 * 8192 * 768 * 256 * 2,
+        1024,
         "pool_top",
     )[0]
 
 
-def gelu(x):
-    half = 0.5 * x
-    return half + half * lax.erf(x * 0.7071067811865476)
-
-
-STEP = 4
+STEP = 16
+HALF_STEPS = BX // STEP // 2
 
 
 def mlp_kernel(
-    place_ref, top_ref, mine_ref, other_ref, near_ref, far_ref, w_in_ref, b_in_ref, w_out_ref, b_out_ref, out_ref, side_ref
+    place_ref, top_ref, mine_ref, other_ref, s0_ref, s1_ref, s2_ref, s3_ref,
+    w_in_ref, b_in_ref, w_out_ref, b_out_ref, out_ref, side_ref, wide_ref, half_ref,
 ):
     @pl.when(pl.program_id(0) == 0)
     def _():
-        for y in range(BY // 2):
-            side_ref[y ^ place_ref[1]] = near_ref[y]
-            side_ref[(y + BY // 2) ^ place_ref[1]] = far_ref[y]
-
-    def work(front_ref):
-        for i in range(STEP):
-            top = top_ref[i].astype(BF16).astype(F32)
-            front = front_ref[i].astype(F32)
-            cell = (top[:, None, :] + front[None, :, :] + side_ref[...].astype(F32)).astype(BF16)
-            cell = cell.reshape(BY * NZ, C)
-            hidden = jnp.dot(cell, w_in_ref[...], preferred_element_type=F32) + b_in_ref[...]
-            hidden = gelu(hidden).astype(BF16)
-            result = jnp.dot(hidden, w_out_ref[...], preferred_element_type=F32)
-            result = result + b_out_ref[...] + cell.astype(F32)
-            out_ref[i] = result.astype(BF16).reshape(BY, NZ, C)
+        for k, rows in enumerate((s0_ref, s1_ref, s2_ref, s3_ref)):
+            for j in range(4):
+                y = k * 2 + j if j < 2 else BY // 2 + k * 2 + j - 2
+                side_ref[y ^ place_ref[1]] = rows[j].astype(F32)
+        bias = b_in_ref[...]
+        high = bias.astype(BF16).astype(F32)
+        middle = (bias - high).astype(BF16).astype(F32)
+        low = bias - high - middle
+        row = iota((C, HID), 0)
+        rest = jnp.where(row == 0, high, jnp.where(row == 1, middle, jnp.where(row == 2, low, 0.0)))
+        wide_ref[0:C, :] = w_in_ref[...]
+        wide_ref[C : 2 * C, :] = rest.astype(BF16)
+        half_ref[...] = (w_out_ref[...].astype(F32) * 0.5).astype(BF16)
 
     mine = pl.program_id(0) < HALF_STEPS
-    pl.when(mine)(lambda: work(mine_ref))
-    pl.when(jnp.logical_not(mine))(lambda: work(other_ref))
-
-
-HALF_STEPS = BX // STEP // 2
-
-
-def mlp(place, top, mine, other, near, far, w_in, b_in, w_out, b_out):
+    ones = jnp.where(iota((BY * NZ, C), 1) < 3, 1.0, 0.0).astype(BF16)
+    for i in range(STEP):
+        top = top_ref[i].astype(F32)
+        front = jnp.where(mine, mine_ref[i].astype(F32), other_ref[i].astype(F32))
+        cell = (top[:, None, :] + front[None, :, :] + side_ref[...]).astype(BF16).reshape(BY * NZ, C)
+        inner = jnp.dot(jnp.concatenate([cell, ones], axis=1), wide_ref[...], preferred_element_type=F32)
+        twice = (inner * (1.0 + lax.erf(inner * 0.7071067811865476))).astype(BF16)
+        result = jnp.dot(twice, half_ref[...], preferred_element_type=F32)
+        result = result + (b_out_ref[...] + cell.astype(F32))
+        out_ref[i] = result.astype(BF16).reshape(BY, NZ, C)
+
+
+def mlp(place, top, mine, other, sides, w_in, b_in, w_out, b_out):
     def same(*shape):
         return pl.BlockSpec(shape, lambda i, h: (0,) * len(shape))
 
@@ -339,23 +339,23 @@
                 pl.BlockSpec((STEP, BY, C), lambda i, h: (i, 0, 0)),
                 pl.BlockSpec((STEP, NZ, C), lambda i, h: (jnp.minimum(i, HALF_STEPS - 1), 0, 0)),
                 pl.BlockSpec((STEP, NZ, C), lambda i, h: (jnp.maximum(i - HALF_STEPS, 0), 0, 0)),
-                same(BY // 2, NZ, C),
-                same(BY // 2, NZ, C),
-                same(C, HID),
-                same(1, HID),
-                same(HID, C),
-                same(1, C),
+            ]
+            + [same(4, NZ, C)] * 4
+            + [same(C, HID), same(1, HID), same(HID, C), same(1, C)],
+            out_specs=pl.BlockSpec((STEP, BY, NZ, C), lambda i, h: (i ^ (h[0] * HALF_STEPS), 0, 0, 0)),
+            scratch_shapes=[
+                pltpu.VMEM((BY, NZ, C), F32),
+                pltpu.VMEM((2 * C, HID), BF16),
+                pltpu.VMEM((HID, C), BF16),
             ],
-            out_specs=pl.BlockSpec((STEP, BY, NZ, C), lambda i, h: (i ^ (h[0] * HALF_STEPS), 0, 0, 0)),
-            scratch_shapes=[pltpu.VMEM((BY, NZ, C), BF16)],
         ),
         out_shape=jax.ShapeDtypeStruct((BX, BY, NZ, C), BF16),
-        compiler_params=pltpu.CompilerParams(vmem_limit_bytes=VMEM_LIMIT),
+        compiler_params=pltpu.CompilerParams(vmem_limit_bytes=MLP_LIMIT),
         cost_estimate=pl.CostEstimate(
             flops=4 * BX * BY * NZ * C * HID, bytes_accessed=9 * 2**20, transcendentals=BX * BY * NZ * HID
         ),
         name="voxel_mlp",
-    )(place, top, mine, other, near, far, w_in, b_in.reshape(1, HID), w_out, b_out.reshape(1, C))
+    )(place, top, mine, other, *sides, w_in, b_in.reshape(1, HID), w_out, b_out.reshape(1, C))
 
 
 SAME_CORE = [list(range(core, N_GY, 2)) for core in range(2)]
@@ -363,30 +363,35 @@
 
 def swap(array, axis, size, bit):
     return lax.ppermute(array, axis, [(i, i ^ bit) for i in range(size)])
+
+
+def spread_kernel(pieces_ref, out_ref):
+    share = jnp.sum(pieces_ref[...], axis=0).astype(BF16)
+    for i in range(8):
+        out_ref[i] = share
 
 
 def front_share(mine):
     pieces = mine.reshape(8, mine.shape[0] * mine.shape[1] // 8, C)
     pieces = lax.all_to_all(pieces, "gy", 0, 0, tiled=True, axis_index_groups=SAME_CORE)
-    return jnp.sum(pieces, axis=0).astype(BF16)
-
-
-def front_gather(share):
-    copies = jnp.broadcast_to(share[None], (8,) + share.shape)
+    return call(spread_kernel, [pieces], [jax.ShapeDtypeStruct(pieces.shape, BF16)], [], 1024, "spread")[0]
+
+
+def front_gather(copies):
     whole = lax.all_to_all(copies, "gy", 0, 0, tiled=True, axis_index_groups=SAME_CORE)
     return whole.reshape(BX // 2, NZ, C)
 
 
 def side_share(keep, send):
     parts = fold(keep, swap(send, "gx", N_GX, 4))
-    return (
+    share = (
         parts[0] + swap(parts[1], "gx", N_GX, 2) + swap(parts[2], "gx", N_GX, 1) + swap(parts[3], "gx", N_GX, 3)
     ).astype(BF16)
+    return jnp.concatenate([share, swap(share, "gx", N_GX, 4)], axis=0)
 
 
 def side_gather(share):
-    near = jnp.concatenate([share] + [swap(share, "gx", N_GX, bit) for bit in (2, 1, 3)], axis=0)
-    return near, swap(near, "gx", N_GX, 4)
+    return [share] + [swap(share, "gx", N_GX, bit) for bit in (2, 1, 3)]
 
 
 def per_device(
@@ -406,9 +411,9 @@
     shares = (front_share(mine), side_share(keep, send), top)
     front, side, top = lax.optimization_barrier(shares)
     mine = front_gather(front)
-    near, far = side_gather(side)
+    mine, *sides = lax.optimization_barrier([mine] + side_gather(side))
     other = swap(mine, "gy", N_GY, 1)
-    return mlp(place, top, mine, other, near, far, w_in, b_in, w_out, b_out)
+    return mlp(place, top, mine, other, sides, w_in, b_in, w_out, b_out)
 
 
 def solution(mesh):

time: 116 us -> 111 us (0.957)
  Pallas kernels: 38.4 us -> 34.2 us
  starting transfers between devices: 31.2 us -> 33.4 us
  waiting for transfers between devices: 42.2 us -> 40.7 us
    pallas_call x1, Pallas kernels: 16.8 us -> 11.9 us  [mlp(): pl.pallas_call(mlp_kernel, grid_spec=pltpu.PrefetchScalarGridSpec(num_sca...]
    all_to_all x1, starting transfers between devices: 4.03 us -> 6.56 us  [front_gather(): lax.all_to_all(copies, 'gy', 0, 0, tiled=True, axis_index_groups=SAME_CORE)]
    all_to_all x1, waiting for transfers between devices: 2.5 us -> 0.01 us  [front_share(): lax.all_to_all(pieces, 'gy', 0, 0, tiled=True, axis_index_groups=SAME_CORE)]
    ppermute x10, waiting for transfers between devices: 7.03 us -> 8.58 us  [swap(): return lax.ppermute(array, axis, [(i, i ^ bit) for i in range(size)])]
    pallas_call x4 -> x5, Pallas kernels: 10.9 us -> 11.6 us  [call(): pl.pallas_call(kernel, out_shape=outs, in_specs=[small if i.dtype == jnp....]
  transfers between devices with their start and end apart: 13 -> 13, of which waited for: 7 -> 10; matrix products, arithmetic and copies ran while one was open for 0% -> 0% of each run, Pallas kernels for 5% -> 5%
where the time goes in v4:
time: 111 us; the launch traced here: 110 us
  waiting for transfers between devices  40.7 us (37%)
  Pallas kernels  34.2 us (31%)
  starting transfers between devices  33.4 us (30%)
    all_to_all x1, waiting for transfers between devices, per_device(): lax.all_to_all(sent, ('gx', 'gy'), split_axis=0, concat_axis=0, tiled=True)  31 us
    pallas_call x1, Pallas kernels, mlp(): pl.pallas_call(mlp_kernel, grid_spec=pltpu.PrefetchScalarGridSpec(num_sca...  11.9 us
    pallas_call x5, Pallas kernels, call(): pl.pallas_call(kernel, out_shape=outs, in_specs=[small if i.dtype == jnp....  11.6 us
    ppermute x10, starting transfers between devices, swap(): return lax.ppermute(array, axis, [(i, i ^ bit) for i in range(size)])  11.6 us
    all_to_all x1, starting transfers between devices, per_device(): lax.all_to_all(sent, ('gx', 'gy'), split_axis=0, concat_axis=0, tiled=True)  11.3 us
    pallas_call x1, Pallas kernels, pack(): pl.pallas_call(pack_kernel, out_shape=jax.ShapeDtypeStruct((DEVICES, ROWS...  10.7 us
    ppermute x10, waiting for transfers between devices, swap(): return lax.ppermute(array, axis, [(i, i ^ bit) for i in range(size)])  8.58 us
    all_to_all x1, starting transfers between devices, front_gather(): lax.all_to_all(copies, 'gy', 0, 0, tiled=True, axis_index_groups=SAME_CORE)  6.56 us
  transfers between devices with their start and end apart: 13, of which 10 were waited for; matrix products, arithmetic and copies ran while one was open for 0% of the time, Pallas kernels for 5%

profile of v4, /device:TPU:0, one launch (start us, length us, event | category | flops | bytes accessed | tf_op | source)
XLA Modules:
  0.0 110.0 jit_solution(9106389644310232153)
XLA Ops:
  0.7 10.7 %pack.1 = bf16[128,72,128]{2,1,0:T(8,128)(2,1)} custom-call(s32[1]{0:T(128)S(6)} %copy.10.cam_ref, bf16[4096,128]{1,0:T(8,128)(2,1)} %feats_hbm.1, s32[32,128]{1,0:T(8,128)} %bitcast.13, s32[32,128]{1,0:T(8,128)} %bitcast.14, f32[6,128]{1,0:T(8,128)} %embed_hbm.1), custom_call_target="tpu_custom_call" | custom-call | flops 8589934592 | bytes 4194304 | tf_op jit(solution)/shard_map/pack/pallas_call | solution.py:161
  11.3 11.3 %all-to-all-start = ((bf16[128,72,128]{2,1,0:T(8,128)(2,1)}), bf16[128,72,128]{2,1,0:T(8,128)(2,1)S(1)}, u32[]{:S(2)}, u32[]{:S(2)}) async-start(bf16[128,72,128]{2,1,0:T(8,128)(2,1)} %pack.1), calls=%async_computation | async-start | bytes 4718592 | tf_op jit(solution)/shard_map/all_to_all | solution.py:405
  22.7 0.1 pad_add_fusion.place_ref
  22.8 31.0 %all-to-all-done.got_ref = bf16[128,72,128]{2,1,0:T(8,128)(2,1)S(1)} async-done(((bf16[128,72,128]{2,1,0:T(8,128)(2,1)}), bf16[128,72,128]{2,1,0:T(8,128)(2,1)S(1)}, u32[]{:S(2)}, u32[]{:S(2)}) %all-to-all-start) | async-done | bytes 2359328 | tf_op jit(solution)/shard_map/all_to_all | solution.py:405
  53.7 5.6 %pool_front.1 = (f32[32,32,128]{2,1,0:T(8,128)S(1)}, f32[32,32,128]{2,1,0:T(8,128)S(1)}, s32[5,64,128]{2,1,0:T(8,128)S(1)}) custom-call(s32[2]{0:T(128)S(1)} %pad_add_fusion.place_ref, bf16[128,72,128]{2,1,0:T(8,128)(2,1)S(1)} %all-to-all-done.got_ref), custom_call_target="tpu_custom_call" | custom-call | flops 8589934592 | bytes 8388608 | tf_op jit(solution)/shard_map/pool_front/pallas_call | solution.py:241
  59.4 1.0 collective-permute-start
  60.3 2.3 %pool_side.1 = (f32[8,32,128]{2,1,0:T(8,128)S(1)}, f32[8,32,128]{2,1,0:T(8,128)S(1)}) custom-call(bf16[128,72,128]{2,1,0:T(8,128)(2,1)S(1)} %all-to-all-done.got_ref, s32[5,64,128]{2,1,0:T(8,128)S(1)} %get-tuple-element.27.labels_ref), custom_call_target="tpu_custom_call" | custom-call | flops 2147483648 | bytes 2097152 | tf_op jit(solution)/shard_map/pool_side/pallas_call | solution.py:241
  62.7 0.0 collective-permute-done
  62.7 0.9 add.20
  63.5 0.8 collective-permute-start.1
  64.4 4.0 %all-to-all-start.1 = ((f32[8,128,128]{2,1,0:T(8,128)}), f32[8,128,128]{2,1,0:T(8,128)S(1)}, u32[]{:S(2)}, u32[]{:S(2)}) async-start(f32[8,128,128]{2,1,0:T(8,128)} %bitcast.12), calls=%async_computation.1 | async-start | bytes 1048576 | tf_op jit(solution)/shard_map/all_to_all | solution.py:376
  68.3 0.0 copy-start
  68.3 0.0 copy-start.2
  68.3 0.0 copy-start.3
  68.4 0.6 collective-permute-done.1.got_ref
  69.0 0.0 copy-start.1
  69.0 2.2 %collective-permute-start.2 = (f32[2,32,128]{2,1,0:T(8,128)S(1)}, f32[2,32,128]{2,1,0:T(8,128)S(1)}, u32[]{:S(2)}, u32[]{:S(2)}) collective-permute-start(f32[2,32,128]{2,1,0:T(8,128)S(1)} %get-tuple-element.34), channel_id=1, source_target_pairs={{0,32},{16,48},{32,0},{48,16},{64,96},{80,112},{96,64},{112,80},{1... | collective-permute-start | bytes 98312 | tf_op jit(solution)/shard_map/ppermute | solution.py:365
  71.1 0.7 collective-permute-start.3
  71.9 1.3 %collective-permute-start.4 = (f32[2,32,128]{2,1,0:T(8,128)S(1)}, f32[2,32,128]{2,1,0:T(8,128)S(1)}, u32[]{:S(2)}, u32[]{:S(2)}) collective-permute-start(f32[2,32,128]{2,1,0:T(8,128)S(1)} %get-tuple-element.36), channel_id=1, source_target_pairs={{0,48},{16,32},{32,16},{48,0},{64,112},{80,96},{96,80},{112,64},{1... | collective-permute-start | bytes 98312 | tf_op jit(solution)/shard_map/ppermute | solution.py:365
  73.1 1.3 %collective-permute-done.2 = f32[2,32,128]{2,1,0:T(8,128)S(1)} collective-permute-done((f32[2,32,128]{2,1,0:T(8,128)S(1)}, f32[2,32,128]{2,1,0:T(8,128)S(1)}, u32[]{:S(2)}, u32[]{:S(2)}) %collective-permute-start.2) | collective-permute-done | bytes 32800 | tf_op jit(solution)/shard_map/ppermute | solution.py:365
  74.5 0.6 collective-permute-done.3
  75.1 1.9 %collective-permute-done.4 = f32[2,32,128]{2,1,0:T(8,128)S(1)} collective-permute-done((f32[2,32,128]{2,1,0:T(8,128)S(1)}, f32[2,32,128]{2,1,0:T(8,128)S(1)}, u32[]{:S(2)}, u32[]{:S(2)}) %collective-permute-start.4) | collective-permute-done | bytes 32800 | tf_op jit(solution)/shard_map/ppermute | solution.py:365
  77.0 0.9 collective-permute-start.5
  77.9 2.9 %pool_top.1.top_ref = bf16[64,16,128]{2,1,0:T(8,128)(2,1)S(1)} custom-call(bf16[128,72,128]{2,1,0:T(8,128)(2,1)S(1)} %all-to-all-done.got_ref, s32[5,64,128]{2,1,0:T(8,128)S(1)} %get-tuple-element.27.labels_ref), custom_call_target="tpu_custom_call" | custom-call | flops 1024 | bytes 1 | tf_op jit(solution)/shard_map/pool_top/pallas_call | solution.py:241
  80.8 0.0 collective-permute-done.5
  80.9 0.0 all-to-all-done.1.pieces_ref
  80.9 0.7 spread.1
  81.6 6.6 %all-to-all-start.2 = ((bf16[8,128,128]{2,1,0:T(8,128)(2,1)}), bf16[8,128,128]{2,1,0:T(8,128)(2,1)S(1)}, u32[]{:S(2)}, u32[]{:S(2)}) async-start(bf16[8,128,128]{2,1,0:T(8,128)(2,1)} %spread.1), calls=%async_computation.2 | async-start | bytes 524288 | tf_op jit(solution)/shard_map/all_to_all | solution.py:381
  88.2 1.9 %collective-permute-start.8 = (bf16[4,32,128]{2,1,0:T(8,128)(2,1)S(1)}, bf16[4,32,128]{2,1,0:T(8,128)(2,1)S(1)}, u32[]{:S(2)}, u32[]{:S(2)}) collective-permute-start(bf16[4,32,128]{2,1,0:T(8,128)(2,1)S(1)} %pad_maximum_fusion.s0_ref), channel_id=1, source_target_pairs={{0,48},{16,32},{32,16},{48,0},{64,112},{80,96},{96,80},{112,64},{1... | collective-permute-start | bytes 98312 | tf_op jit(solution)/shard_map/ppermute | solution.py:365
  90.1 0.0 collective-permute-start.7
  90.1 2.8 %collective-permute-start.6 = (bf16[4,32,128]{2,1,0:T(8,128)(2,1)S(1)}, bf16[4,32,128]{2,1,0:T(8,128)(2,1)S(1)}, u32[]{:S(2)}, u32[]{:S(2)}) collective-permute-start(bf16[4,32,128]{2,1,0:T(8,128)(2,1)S(1)} %pad_maximum_fusion.s0_ref), channel_id=1, source_target_pairs={{0,32},{16,48},{32,0},{48,16},{64,96},{80,112},{96,64},{112,80},{1... | collective-permute-start | bytes 98312 | tf_op jit(solution)/shard_map/ppermute | solution.py:365
  92.9 0.4 collective-permute-done.8.s3_ref
  93.3 0.7 collective-permute-done.7.s2_ref
  94.0 1.5 %collective-permute-done.6.s1_ref = bf16[4,32,128]{2,1,0:T(8,128)(2,1)S(1)} collective-permute-done((bf16[4,32,128]{2,1,0:T(8,128)(2,1)S(1)}, bf16[4,32,128]{2,1,0:T(8,128)(2,1)S(1)}, u32[]{:S(2)}, u32[]{:S(2)}) %collective-permute-start.6) | collective-permute-done | bytes 32800 | tf_op jit(solution)/shard_map/ppermute | solution.py:365
  95.5 1.1 %all-to-all-done.2 = bf16[8,128,128]{2,1,0:T(8,128)(2,1)S(1)} async-done(((bf16[8,128,128]{2,1,0:T(8,128)(2,1)}), bf16[8,128,128]{2,1,0:T(8,128)(2,1)S(1)}, u32[]{:S(2)}, u32[]{:S(2)}) %all-to-all-start.2) | async-done | bytes 262176 | tf_op jit(solution)/shard_map/all_to_all | solution.py:381
  96.6 0.0 collective-permute-start.9
  96.6 1.5 %collective-permute-done.9.other_ref = bf16[32,32,128]{2,1,0:T(8,128)(2,1)S(1)} collective-permute-done((bf16[32,32,128]{2,1,0:T(8,128)(2,1)S(1)}, bf16[32,32,128]{2,1,0:T(8,128)(2,1)S(1)}, u32[]{:S(2)}, u32[]{:S(2)}) %collective-permute-start.9) | collective-permute-done | bytes 262176 | tf_op jit(solution)/shard_map/ppermute | solution.py:365
  98.1 0.0 copy-done
  98.1 0.0 copy-done.2
  98.1 0.0 copy-done.3
  98.2 0.0 copy-done.1
  98.2 11.9 %voxel_mlp.1 = bf16[64,16,32,128]{3,2,1,0:T(8,128)(2,1)} custom-call(s32[2]{0:T(128)S(1)} %pad_add_fusion.place_ref, bf16[64,16,128]{2,1,0:T(8,128)(2,1)S(1)} %pool_top.1.top_ref, bf16[32,32,128]{2,1,0:T(8,128)(2,1)S(1)} %bitcast.9, bf16[32,32,128]{2,1,0:T(8,128)(2,1)S(1)} %collective-permute-done.9.other_ref, ...), custom_call_target="tpu_custom_call" | custom-call | flops 4294967296 | bytes 9437184 | tf_op jit(solution)/shard_map/voxel_mlp/pallas_call | solution.py:333
  (3 shorter events, 0.0 us)
Async XLA Ops:
  11.3 42.4 %all-to-all-start = ((bf16[128,72,128]{2,1,0:T(8,128)(2,1)}), bf16[128,72,128]{2,1,0:T(8,128)(2,1)S(1)}, u32[]{:S(2)}, u32[]{:S(2)}) async-start(bf16[128,72,128]{2,1,0:T(8,128)(2,1)} %pack.1), calls=%async_computation | async-start | bytes 4718592 | tf_op jit(solution)/shard_map/all_to_all | solution.py:405
  59.4 3.3 %collective-permute-start = (f32[32,32,128]{2,1,0:T(8,128)S(1)}, f32[32,32,128]{2,1,0:T(8,128)S(1)}, u32[]{:S(2)}, u32[]{:S(2)}) collective-permute-start(f32[32,32,128]{2,1,0:T(8,128)S(1)} %get-tuple-element.26), channel_id=1, source_target_pairs={{0,1},{1,0},{2,3},{3,2},{4,5},{5,4},{6,7},{7,6},{8,9},{9,8},{10,11... | collective-permute-start | bytes 1572872 | tf_op jit(solution)/shard_map/ppermute | solution.py:365
  63.5 5.4 %collective-permute-start.1 = (f32[8,32,128]{2,1,0:T(8,128)S(1)}, f32[8,32,128]{2,1,0:T(8,128)S(1)}, u32[]{:S(2)}, u32[]{:S(2)}) collective-permute-start(f32[8,32,128]{2,1,0:T(8,128)S(1)} %get-tuple-element.32), channel_id=1, source_target_pairs={{0,64},{16,80},{32,96},{48,112},{64,0},{80,16},{96,32},{112,48},{1... | collective-permute-start | bytes 393224 | tf_op jit(solution)/shard_map/ppermute | solution.py:365
  64.4 16.5 %all-to-all-start.1 = ((f32[8,128,128]{2,1,0:T(8,128)}), f32[8,128,128]{2,1,0:T(8,128)S(1)}, u32[]{:S(2)}, u32[]{:S(2)}) async-start(f32[8,128,128]{2,1,0:T(8,128)} %bitcast.12), calls=%async_computation.1 | async-start | bytes 1048576 | tf_op jit(solution)/shard_map/all_to_all | solution.py:376
  68.3 29.8 %copy-start = (bf16[128,256]{1,0:T(8,128)(2,1)S(1)}, bf16[128,256]{1,0:T(8,128)(2,1)}, u32[]{:S(2)}) copy-start(bf16[128,256]{1,0:T(8,128)(2,1)} %w_in_ref.1) | copy-start | bytes 196612
  68.3 29.8 %copy-start.2 = (f32[256]{0:T(256)S(1)}, f32[256]{0:T(256)}, u32[]{:S(2)}) copy-start(f32[256]{0:T(256)} %param.16) | copy-start | bytes 3076
  68.3 29.8 %copy-start.3 = (f32[128]{0:T(128)S(1)}, f32[128]{0:T(128)}, u32[]{:S(2)}) copy-start(f32[128]{0:T(128)} %param.18) | copy-start | bytes 1540
  69.0 29.2 %copy-start.1 = (bf16[256,128]{1,0:T(8,128)(2,1)S(1)}, bf16[256,128]{1,0:T(8,128)(2,1)}, u32[]{:S(2)}) copy-start(bf16[256,128]{1,0:T(8,128)(2,1)} %w_out_ref.1) | copy-start | bytes 196612
  69.0 5.5 %collective-permute-start.2 = (f32[2,32,128]{2,1,0:T(8,128)S(1)}, f32[2,32,128]{2,1,0:T(8,128)S(1)}, u32[]{:S(2)}, u32[]{:S(2)}) collective-permute-start(f32[2,32,128]{2,1,0:T(8,128)S(1)} %get-tuple-element.34), channel_id=1, source_target_pairs={{0,32},{16,48},{32,0},{48,16},{64,96},{80,112},{96,64},{112,80},{1... | collective-permute-start | bytes 98312 | tf_op jit(solution)/shard_map/ppermute | solution.py:365
  71.1 3.9 %collective-permute-start.3 = (f32[2,32,128]{2,1,0:T(8,128)S(1)}, f32[2,32,128]{2,1,0:T(8,128)S(1)}, u32[]{:S(2)}, u32[]{:S(2)}) collective-permute-start(f32[2,32,128]{2,1,0:T(8,128)S(1)} %get-tuple-element.35), channel_id=1, source_target_pairs={{0,16},{16,0},{32,48},{48,32},{64,80},{80,64},{96,112},{112,96},{1... | collective-permute-start | bytes 98312 | tf_op jit(solution)/shard_map/ppermute | solution.py:365
  71.9 5.1 %collective-permute-start.4 = (f32[2,32,128]{2,1,0:T(8,128)S(1)}, f32[2,32,128]{2,1,0:T(8,128)S(1)}, u32[]{:S(2)}, u32[]{:S(2)}) collective-permute-start(f32[2,32,128]{2,1,0:T(8,128)S(1)} %get-tuple-element.36), channel_id=1, source_target_pairs={{0,48},{16,32},{32,16},{48,0},{64,112},{80,96},{96,80},{112,64},{1... | collective-permute-start | bytes 98312 | tf_op jit(solution)/shard_map/ppermute | solution.py:365
  77.0 3.8 %collective-permute-start.5 = (bf16[2,32,128]{2,1,0:T(8,128)(2,1)S(1)}, bf16[2,32,128]{2,1,0:T(8,128)(2,1)S(1)}, u32[]{:S(2)}, u32[]{:S(2)}) collective-permute-start(bf16[2,32,128]{2,1,0:T(8,128)(2,1)S(1)} %add_convert_fusion), channel_id=1, source_target_pairs={{0,64},{16,80},{32,96},{48,112},{64,0},{80,16},{96,32},{112,48},{1... | collective-permute-start | bytes 49160 | tf_op jit(solution)/shard_map/ppermute | solution.py:365
  81.6 15.0 %all-to-all-start.2 = ((bf16[8,128,128]{2,1,0:T(8,128)(2,1)}), bf16[8,128,128]{2,1,0:T(8,128)(2,1)S(1)}, u32[]{:S(2)}, u32[]{:S(2)}) async-start(bf16[8,128,128]{2,1,0:T(8,128)(2,1)} %spread.1), calls=%async_computation.2 | async-start | bytes 524288 | tf_op jit(solution)/shard_map/all_to_all | solution.py:381
  88.2 5.1 %collective-permute-start.8 = (bf16[4,32,128]{2,1,0:T(8,128)(2,1)S(1)}, bf16[4,32,128]{2,1,0:T(8,128)(2,1)S(1)}, u32[]{:S(2)}, u32[]{:S(2)}) collective-permute-start(bf16[4,32,128]{2,1,0:T(8,128)(2,1)S(1)} %pad_maximum_fusion.s0_ref), channel_id=1, source_target_pairs={{0,48},{16,32},{32,16},{48,0},{64,112},{80,96},{96,80},{112,64},{1... | collective-permute-start | bytes 98312 | tf_op jit(solution)/shard_map/ppermute | solution.py:365
  90.1 3.9 %collective-permute-start.7 = (bf16[4,32,128]{2,1,0:T(8,128)(2,1)S(1)}, bf16[4,32,128]{2,1,0:T(8,128)(2,1)S(1)}, u32[]{:S(2)}, u32[]{:S(2)}) collective-permute-start(bf16[4,32,128]{2,1,0:T(8,128)(2,1)S(1)} %pad_maximum_fusion.s0_ref), channel_id=1, source_target_pairs={{0,16},{16,0},{32,48},{48,32},{64,80},{80,64},{96,112},{112,96},{1... | collective-permute-start | bytes 98312 | tf_op jit(solution)/shard_map/ppermute | solution.py:365
  90.1 5.4 %collective-permute-start.6 = (bf16[4,32,128]{2,1,0:T(8,128)(2,1)S(1)}, bf16[4,32,128]{2,1,0:T(8,128)(2,1)S(1)}, u32[]{:S(2)}, u32[]{:S(2)}) collective-permute-start(bf16[4,32,128]{2,1,0:T(8,128)(2,1)S(1)} %pad_maximum_fusion.s0_ref), channel_id=1, source_target_pairs={{0,32},{16,48},{32,0},{48,16},{64,96},{80,112},{96,64},{112,80},{1... | collective-permute-start | bytes 98312 | tf_op jit(solution)/shard_map/ppermute | solution.py:365
  96.6 1.5 %collective-permute-start.9 = (bf16[32,32,128]{2,1,0:T(8,128)(2,1)S(1)}, bf16[32,32,128]{2,1,0:T(8,128)(2,1)S(1)}, u32[]{:S(2)}, u32[]{:S(2)}) collective-permute-start(bf16[32,32,128]{2,1,0:T(8,128)(2,1)S(1)} %bitcast.8), channel_id=1, source_target_pairs={{0,1},{1,0},{2,3},{3,2},{4,5},{5,4},{6,7},{7,6},{8,9},{9,8},{10,11... | collective-permute-start | bytes 786440 | tf_op jit(solution)/shard_map/ppermute | solution.py:365

commit v5 on v4

--- a/solution.py
+++ b/solution.py
@@ -32,9 +32,13 @@
     return lax.broadcasted_iota(jnp.int32, shape, axis)
 
 
-def columns_of(row):
-    diagonal = jnp.where(iota((128, 128), 0) == iota((128, 128), 1), row, 0.0).astype(BF16)
-    return jnp.dot(diagonal, jnp.ones((128, 128), BF16), preferred_element_type=F32).astype(BF16)
+def columns_of(rows):
+    padding = jnp.zeros((128 - rows.shape[0], 128), F32)
+    return jnp.concatenate([rows.astype(F32), padding], axis=0).T
+
+
+def spread_column(columns, k):
+    return jnp.broadcast_to(columns[:, k : k + 1], (128, 128)).astype(BF16)
 
 
 def split_columns(values, half):
@@ -53,10 +57,15 @@
     )
 
 
+GROUPS = 4
+GROUP = P_DEV // GROUPS
+GROUP_CHUNKS = GROUP // 128
+
+
 def pack_kernel(
     cam_ref, feats_hbm, top_hbm, front_hbm, embed_hbm, out_hbm,
     feats_ref, top_ref, front_ref, embed_ref, out_ref,
-    marks_ref, rank_ref, place_ref, half_ref, rhs_ref, values_ref, sorted_ref, meta_ref, start_ref, start_smem, sems,
+    marks_ref, rank_ref, place_ref, rhs_ref, values_ref, sorted_ref, stage_ref, meta_ref, start_ref, start_smem, sems,
 ):
     loads = [
         pltpu.make_async_copy(source, target, sems.at[i])
@@ -80,39 +89,48 @@
     )
     cells = [cell.astype(F32) for cell in cells]
 
-    for k in range(CHUNKS):
-        marks_ref[:, k * 128 : (k + 1) * 128] = onehot_rows(owner[k : k + 1, :], 0, DEVICES)
-    totals = jnp.dot(marks_ref[...], jnp.ones((P_DEV, 128), BF16), preferred_element_type=F32)
-    below = jnp.where(iota((128, 128), 1) < iota((128, 128), 0), 1.0, 0.0).astype(BF16)
-    starts = jnp.dot(below, totals.astype(BF16), preferred_element_type=F32)
-    start_row = jnp.sum(
-        jnp.where(iota((128, 128), 0) == iota((128, 128), 1), starts, 0.0), axis=0, keepdims=True
-    )
-    start_ref[...] = start_row.astype(jnp.int32)
-    copy = pltpu.make_async_copy(start_ref, start_smem, sems.at[4])
-    copy.start()
-
     before = iota((128, 256), 0) < iota((128, 256), 1)
     later = iota((128, 256), 1) >= 128
     counter = jnp.where(before | later, 1.0, 0.0).astype(BF16)
     seen = jnp.zeros((DEVICES, 128), F32)
-    slot = iota((128, 128), 0) & (CAP - 1)
+    slot = iota((CAP, 128), 0)
+    bounds = [seen]
     for k in range(CHUNKS):
         columns = slice(k * 128, (k + 1) * 128)
         mine = iota((DEVICES, 128), 0) == owner[k : k + 1, :]
-        counts = jnp.dot(marks_ref[:, columns], counter, preferred_element_type=F32)
+        marks = jnp.where(mine, 1.0, 0.0).astype(BF16)
+        marks_ref[:, columns] = marks
+        counts = jnp.dot(marks, counter, preferred_element_type=F32)
         rank = jnp.sum(jnp.where(mine, counts[:, :128] + seen, 0.0), axis=0, keepdims=True)
-        start = jnp.sum(jnp.where(mine, starts, 0.0), axis=0, keepdims=True)
         seen = seen + counts[:, 128:]
-        place_ref[pl.ds(k, 1), :] = rank + start
+        rank_ref[pl.ds(k, 1), :] = rank
         here = slot == rank.astype(jnp.int32)
         for part in range(3):
-            values_ref[part * 128 : (part + 1) * 128, columns] = jnp.where(
+            values_ref[part * CAP : (part + 1) * CAP, columns] = jnp.where(
                 here, cells[part][k : k + 1, :], 0.0
             ).astype(BF16)
+        if (k + 1) % GROUP_CHUNKS == 0:
+            bounds.append(seen)
+
+    below = jnp.where(iota((128, 128), 1) < iota((128, 128), 0), 1.0, 0.0).astype(BF16)
+    diagonal = iota((128, 128), 0) == iota((128, 128), 1)
+    for g in range(GROUPS):
+        count = bounds[g + 1] - bounds[g]
+        starts = jnp.dot(below, count.astype(BF16), preferred_element_type=F32)
+        for row, numbers in ((g, starts), (GROUPS + g, bounds[g])):
+            line = jnp.sum(jnp.where(diagonal, numbers, 0.0), axis=0, keepdims=True)
+            start_ref[pl.ds(row, 1), :] = line.astype(jnp.int32)
+        shift = starts - bounds[g]
+        for k in range(g * GROUP_CHUNKS, (g + 1) * GROUP_CHUNKS):
+            mine = iota((DEVICES, 128), 0) == owner[k : k + 1, :]
+            place_ref[pl.ds(k, 1), :] = rank_ref[pl.ds(k, 1), :] + jnp.sum(
+                jnp.where(mine, shift, 0.0), axis=0, keepdims=True
+            )
+    copy = pltpu.make_async_copy(start_ref, start_smem, sems.at[4])
+    copy.start()
     place = place_ref[...].astype(jnp.int32)
-    half_ref[...] = (place >> 11).astype(F32)
-    place_ref[...] = jnp.where(live, place & 2047, -1).astype(F32)
+    halves = columns_of(place // (GROUP // 2))
+    rank_ref[...] = jnp.where(live, place & (GROUP // 2 - 1), -1).astype(F32)
 
     loads[2].wait()
     loads[3].wait()
@@ -120,34 +138,43 @@
     for k in range(CHUNKS):
         rows = slice(k * 128, (k + 1) * 128)
         features = (feats_ref[rows, :].astype(F32) + camera).astype(BF16)
-        rhs_ref[rows, :] = split_columns(features, columns_of(half_ref[pl.ds(k, 1), :]))
-
-    rank_ref[...] = place_ref[...].astype(jnp.int32)
-    for block in range(8):
-        base = block * 256
-        picked = jnp.dot(onehot(rank_ref, base, 256, CHUNKS), rhs_ref[...], preferred_element_type=F32)
-        sorted_ref[base : base + 256, :] = picked[:, :C]
-        sorted_ref[2048 + base : 2304 + base, :] = picked[:, C:]
-    sorted_ref[P_DEV : P_DEV + CAP, :] = jnp.zeros((CAP, C), F32)
+        rhs_ref[rows, :] = split_columns(features, spread_column(halves, k))
+
+    for g in range(GROUPS):
+        points = rhs_ref[g * GROUP : (g + 1) * GROUP, :]
+        labels = [rank_ref[pl.ds(g * GROUP_CHUNKS + k, 1), :].astype(jnp.int32) for k in range(GROUP_CHUNKS)]
+        for base in range(0, GROUP // 2, 256):
+            picked = jnp.dot(
+                jnp.concatenate([onehot_rows(label, base, 256) for label in labels], axis=1),
+                points,
+                preferred_element_type=F32,
+            )
+            sorted_ref[g, base : base + 256, :] = picked[:, :C]
+            sorted_ref[g, GROUP // 2 + base : GROUP // 2 + base + 256, :] = picked[:, C:]
+        sorted_ref[g, GROUP : GROUP + CAP, :] = jnp.zeros((CAP, C), F32)
 
     meta = lax.dot_general(
         values_ref[...], marks_ref[...], (((1,), (1,)), ((), ())), preferred_element_type=F32
     )
     for part in range(3):
-        meta_ref[pl.ds(part, DEVICES, stride=8), :] = meta[part * 128 : (part + 1) * 128, :].T
+        numbers = meta[part * CAP : (part + 1) * CAP, :]
+        meta_ref[pl.ds(part, DEVICES, stride=8), :] = jnp.concatenate([numbers, numbers], axis=0).T
     for part in range(3, 8):
         meta_ref[pl.ds(part, DEVICES, stride=8), :] = jnp.zeros((DEVICES, 128), F32)
     out_ref[:, CAP:ROWS, :] = meta_ref[...].reshape(DEVICES, 8, 128).astype(BF16)
 
     copy.wait()
-
     stores = []
     for part in range(4):
 
         @pl.loop(0, DEVICES // 4, unroll=8)
         def _(i):
             device = part * (DEVICES // 4) + i
-            out_ref[device, 0:CAP, :] = sorted_ref[pl.ds(start_smem[0, device], CAP), :].astype(BF16)
+            base = device * CAP
+            for g in range(GROUPS):
+                run = sorted_ref[g, pl.ds(start_smem[g, device], CAP), :]
+                stage_ref[pl.ds(base + start_smem[GROUPS + g, device], CAP), :] = run
+            out_ref[device, 0:CAP, :] = stage_ref[pl.ds(base, CAP), :].astype(BF16)
 
         here = pl.ds(part * (DEVICES // 4), DEVICES // 4)
         stores.append(pltpu.make_async_copy(out_ref.at[here], out_hbm.at[here], sems.at[5 + part]))
@@ -170,15 +197,15 @@
             pltpu.VMEM((CAMS, C), F32),
             pltpu.VMEM((DEVICES, ROWS, C), BF16),
             pltpu.VMEM((DEVICES, P_DEV), BF16),
-            pltpu.VMEM((CHUNKS, 128), jnp.int32),
             pltpu.VMEM((CHUNKS, 128), F32),
             pltpu.VMEM((CHUNKS, 128), F32),
             pltpu.VMEM((P_DEV, 2 * C), BF16),
-            pltpu.VMEM((3 * 128, P_DEV), BF16),
-            pltpu.VMEM((P_DEV + CAP, C), F32),
+            pltpu.VMEM((3 * CAP, P_DEV), BF16),
+            pltpu.VMEM((GROUPS, GROUP + CAP, C), F32),
+            pltpu.VMEM((SLOTS + CAP, C), F32),
             pltpu.VMEM((DEVICES * 8, 128), F32),
-            pltpu.VMEM((1, DEVICES), jnp.int32),
-            pltpu.SMEM((1, DEVICES), jnp.int32),
+            pltpu.VMEM((2 * GROUPS, DEVICES), jnp.int32),
+            pltpu.SMEM((2 * GROUPS, DEVICES), jnp.int32),
             pltpu.SemaphoreType.DMA((9,)),
         ],
         compiler_params=pltpu.CompilerParams(vmem_limit_bytes=PACK_LIMIT),
@@ -188,13 +215,13 @@
 
 
 def split_points(got_ref, half_ref, rhs_ref):
+    halves = columns_of(half_ref[...])
     for q in range(PAIRS):
         piece = got_ref[q * 2 : q * 2 + 2, 0:CAP, :].reshape(128, C)
-        half = columns_of(half_ref[pl.ds(q, 1), :].astype(F32))
-        rhs_ref[q * 128 : (q + 1) * 128, :] = split_columns(piece, half)
-
-
-def pool_front_kernel(place_ref, got_ref, mine_ref, other_ref, labels_ref, meta_ref, rhs_ref):
+        rhs_ref[q * 128 : (q + 1) * 128, :] = split_columns(piece, spread_column(halves, q))
+
+
+def pool_front_kernel(place_ref, got_ref, mine_ref, other_ref, labels_ref, rhs_ref, meta_ref):
     meta_ref[...] = got_ref[:, CAP:ROWS, :].astype(F32).reshape(DEVICES * 8, 128)
     first = iota((PAIRS, 128), 1) < CAP
 
@@ -208,7 +235,7 @@
     x = x ^ (place_ref[0] * (BX // 2))
     labels_ref[0] = jnp.where(live, x * 16 + (z & 15), -1)
     labels_ref[1] = jnp.where(live, x * 8 + (y & 7), -1)
-    labels_ref[2] = jnp.where(live, (y ^ place_ref[1]) * 32 + z, -1)
+    labels_ref[2] = jnp.where(live, (y ^ place_ref[1]) * 16 + (z & 15), -1)
     labels_ref[3] = (y >> 3) & 1
     labels_ref[4] = (z >> 4) & 1
     split_points(got_ref, labels_ref.at[4], rhs_ref)
@@ -220,11 +247,12 @@
         out[xs, 16:32, :] = sums[:, C:].reshape(16, 16, C)
 
 
-def pool_side_kernel(got_ref, labels_ref, keep_ref, send_ref):
-    points = got_ref[:, 0:CAP, :].reshape(SLOTS, C)
-    for block, out in enumerate((keep_ref, send_ref)):
-        sums = jnp.dot(onehot(labels_ref.at[2], block * 256, 256, PAIRS), points, preferred_element_type=F32)
-        out[...] = sums.reshape(BY // 2, NZ, C)
+def pool_side_kernel(rhs_ref, labels_ref, keep_ref, send_ref):
+    sums = jnp.dot(onehot(labels_ref.at[2], 0, 256, PAIRS), rhs_ref[...], preferred_element_type=F32)
+    for half, out in enumerate((keep_ref, send_ref)):
+        rows = slice(half * 128, (half + 1) * 128)
+        out[:, 0:16, :] = sums[rows, :C].reshape(BY // 2, 16, C)
+        out[:, 16:32, :] = sums[rows, C:].reshape(BY // 2, 16, C)
 
 
 def pool_top_kernel(got_ref, labels_ref, top_ref, rhs_ref):
@@ -252,19 +280,16 @@
 
 def pool_front(place, got):
     shape = jax.ShapeDtypeStruct((BX // 2, NZ, C), F32)
-    return call(
-        pool_front_kernel,
-        [place, got],
-        [shape, shape, jax.ShapeDtypeStruct((5, PAIRS, 128), jnp.int32)],
-        [pltpu.VMEM((DEVICES * 8, 128), F32), pltpu.VMEM((SLOTS, 2 * C), BF16)],
-        2 * 8192 * 1024 * 256 * 2,
-        "pool_front",
-    )
-
-
-def pool_side(got, labels):
+    labels = jax.ShapeDtypeStruct((5, PAIRS, 128), jnp.int32)
+    points = jax.ShapeDtypeStruct((SLOTS, 2 * C), BF16)
+    scratch = [pltpu.VMEM((DEVICES * 8, 128), F32)]
+    flops = 2 * 8192 * 1024 * 256 * 2
+    return call(pool_front_kernel, [place, got], [shape, shape, labels, points], scratch, flops, "pool_front")
+
+
+def pool_side(points, labels):
     shape = jax.ShapeDtypeStruct((BY // 2, NZ, C), F32)
-    return call(pool_side_kernel, [got, labels], [shape, shape], [], 2 * 8192 * 512 * 256, "pool_side")
+    return call(pool_side_kernel, [points, labels], [shape, shape], [], 2 * 8192 * 512 * 256, "pool_side")
 
 
 def fold_kernel(keep_ref, got_ref, *out_refs):
@@ -403,15 +428,14 @@
     ).astype(jnp.int32)
     sent = pack(camera_of_device, point_feats, top_bin, front_bin, camera_embed)
     got = lax.all_to_all(sent, ("gx", "gy"), split_axis=0, concat_axis=0, tiled=True)
-    mine, other, labels = pool_front(place, got)
-    keep, send = pool_side(got, labels)
+    mine, other, labels, points = pool_front(place, got)
+    keep, send = pool_side(points, labels)
     mine = mine + swap(other, "gy", N_GY, 1)
     mine, keep, send = lax.optimization_barrier((mine, keep, send))
     top = pool_top(got, labels)
-    shares = (front_share(mine), side_share(keep, send), top)
-    front, side, top = lax.optimization_barrier(shares)
+    front, side = lax.optimization_barrier((front_share(mine), side_share(keep, send)))
     mine = front_gather(front)
-    mine, *sides = lax.optimization_barrier([mine] + side_gather(side))
+    mine, top, *sides = lax.optimization_barrier([mine, top] + side_gather(side))
     other = swap(mine, "gy", N_GY, 1)
     return mlp(place, top, mine, other, sides, w_in, b_in, w_out, b_out)
 

time: 111 us -> 108 us (0.973)
  Pallas kernels: 34.2 us -> 29.2 us
    pallas_call x1, Pallas kernels: 10.7 us -> 7.44 us  [pack(): pl.pallas_call(pack_kernel, out_shape=jax.ShapeDtypeStruct((DEVICES, ROWS...]
    pallas_call x5, Pallas kernels: 11.6 us -> 9.92 us  [call(): pl.pallas_call(kernel, out_shape=outs, in_specs=[small if i.dtype == jnp....]
  transfers between devices with their start and end apart: 13 -> 13, of which waited for: 10 -> 9; matrix products, arithmetic and copies ran while one was open for 0% -> 0% of each run, Pallas kernels for 5% -> 4%
where the time goes in v5:
time: 108 us; the launch traced here: 106 us
  waiting for transfers between devices  41.4 us (38%)
  starting transfers between devices  33.9 us (31%)
  Pallas kernels  29.2 us (27%)
    all_to_all x1, waiting for transfers between devices, per_device(): lax.all_to_all(sent, ('gx', 'gy'), split_axis=0, concat_axis=0, tiled=True)  31.1 us
    pallas_call x1, Pallas kernels, mlp(): pl.pallas_call(mlp_kernel, grid_spec=pltpu.PrefetchScalarGridSpec(num_sca...  11.9 us
    ppermute x10, starting transfers between devices, swap(): return lax.ppermute(array, axis, [(i, i ^ bit) for i in range(size)])  11.8 us
    all_to_all x1, starting transfers between devices, per_device(): lax.all_to_all(sent, ('gx', 'gy'), split_axis=0, concat_axis=0, tiled=True)  11.1 us
    pallas_call x5, Pallas kernels, call(): pl.pallas_call(kernel, out_shape=outs, in_specs=[small if i.dtype == jnp....  9.92 us
    ppermute x10, waiting for transfers between devices, swap(): return lax.ppermute(array, axis, [(i, i ^ bit) for i in range(size)])  9.02 us
    pallas_call x1, Pallas kernels, pack(): pl.pallas_call(pack_kernel, out_shape=jax.ShapeDtypeStruct((DEVICES, ROWS...  7.44 us
    all_to_all x1, starting transfers between devices, front_gather(): lax.all_to_all(copies, 'gy', 0, 0, tiled=True, axis_index_groups=SAME_CORE)  6.88 us
  transfers between devices with their start and end apart: 13, of which 9 were waited for; matrix products, arithmetic and copies ran while one was open for 0% of the time, Pallas kernels for 4%

profile of v5, /device:TPU:0, one launch (start us, length us, event | category | flops | bytes accessed | tf_op | source)
XLA Modules:
  0.0 106.3 jit_solution(7262540027757147638)
XLA Ops:
  0.7 7.4 %pack.1 = bf16[128,72,128]{2,1,0:T(8,128)(2,1)} custom-call(s32[1]{0:T(128)S(6)} %copy.10.cam_ref, bf16[4096,128]{1,0:T(8,128)(2,1)} %feats_hbm.1, s32[32,128]{1,0:T(8,128)} %bitcast.13, s32[32,128]{1,0:T(8,128)} %bitcast.14, f32[6,128]{1,0:T(8,128)} %embed_hbm.1), custom_call_target="tpu_custom_call" | custom-call | flops 8589934592 | bytes 4194304 | tf_op jit(solution)/shard_map/pack/pallas_call | solution.py:188
  8.1 11.1 %all-to-all-start = ((bf16[128,72,128]{2,1,0:T(8,128)(2,1)}), bf16[128,72,128]{2,1,0:T(8,128)(2,1)S(1)}, u32[]{:S(2)}, u32[]{:S(2)}) async-start(bf16[128,72,128]{2,1,0:T(8,128)(2,1)} %pack.1), calls=%async_computation | async-start | bytes 4718592 | tf_op jit(solution)/shard_map/all_to_all | solution.py:430
  19.3 0.1 pad_add_fusion.place_ref
  19.3 31.1 %all-to-all-done.got_ref = bf16[128,72,128]{2,1,0:T(8,128)(2,1)S(1)} async-done(((bf16[128,72,128]{2,1,0:T(8,128)(2,1)}), bf16[128,72,128]{2,1,0:T(8,128)(2,1)S(1)}, u32[]{:S(2)}, u32[]{:S(2)}) %all-to-all-start) | async-done | bytes 2359328 | tf_op jit(solution)/shard_map/all_to_all | solution.py:430
  50.5 5.4 %pool_front.1 = (f32[32,32,128]{2,1,0:T(8,128)S(1)}, f32[32,32,128]{2,1,0:T(8,128)S(1)}, s32[5,64,128]{2,1,0:T(8,128)S(1)}, bf16[8192,256]{1,0:T(8,128)(2,1)S(1)}) custom-call(s32[2]{0:T(128)S(1)} %pad_add_fusion.place_ref, bf16[128,72,128]{2,1,0:T(8,128)(2,1)S(1)} %all-to-all-done.got_ref), custom_call_target="tpu_custom_call" | custom-call | flops 8589934592 | bytes 8388608 | tf_op jit(solution)/shard_map/pool_front/pallas_call | solution.py:269
  55.9 1.0 collective-permute-start
  56.9 1.2 %pool_side.1 = (f32[8,32,128]{2,1,0:T(8,128)S(1)}, f32[8,32,128]{2,1,0:T(8,128)S(1)}) custom-call(bf16[8192,256]{1,0:T(8,128)(2,1)S(1)} %get-tuple-element.28.rhs_ref, s32[5,64,128]{2,1,0:T(8,128)S(1)} %get-tuple-element.29.labels_ref), custom_call_target="tpu_custom_call" | custom-call | flops 2147483648 | bytes 2097152 | tf_op jit(solution)/shard_map/pool_side/pallas_call | solution.py:269
  58.1 0.0 copy-start
  58.2 0.0 copy-start.2
  58.2 0.0 copy-start.3
  58.2 0.2 collective-permute-done
  58.4 0.9 add.20
  59.3 0.8 collective-permute-start.1
  60.1 4.1 %all-to-all-start.1 = ((f32[8,128,128]{2,1,0:T(8,128)}), f32[8,128,128]{2,1,0:T(8,128)S(1)}, u32[]{:S(2)}, u32[]{:S(2)}) async-start(f32[8,128,128]{2,1,0:T(8,128)} %bitcast.12), calls=%async_computation.1 | async-start | bytes 1048576 | tf_op jit(solution)/shard_map/all_to_all | solution.py:401
  64.2 0.9 collective-permute-done.1.got_ref
  65.1 0.0 copy-start.1
  65.1 1.8 %collective-permute-start.2 = (f32[2,32,128]{2,1,0:T(8,128)S(1)}, f32[2,32,128]{2,1,0:T(8,128)S(1)}, u32[]{:S(2)}, u32[]{:S(2)}) collective-permute-start(f32[2,32,128]{2,1,0:T(8,128)S(1)} %get-tuple-element.36), channel_id=1, source_target_pairs={{0,32},{16,48},{32,0},{48,16},{64,96},{80,112},{96,64},{112,80},{1... | collective-permute-start | bytes 98312 | tf_op jit(solution)/shard_map/ppermute | solution.py:390
  66.9 0.7 collective-permute-start.3
  67.6 1.6 %collective-permute-start.4 = (f32[2,32,128]{2,1,0:T(8,128)S(1)}, f32[2,32,128]{2,1,0:T(8,128)S(1)}, u32[]{:S(2)}, u32[]{:S(2)}) collective-permute-start(f32[2,32,128]{2,1,0:T(8,128)S(1)} %get-tuple-element.38), channel_id=1, source_target_pairs={{0,48},{16,32},{32,16},{48,0},{64,112},{80,96},{96,80},{112,64},{1... | collective-permute-start | bytes 98312 | tf_op jit(solution)/shard_map/ppermute | solution.py:390
  69.3 1.4 %collective-permute-done.2 = f32[2,32,128]{2,1,0:T(8,128)S(1)} collective-permute-done((f32[2,32,128]{2,1,0:T(8,128)S(1)}, f32[2,32,128]{2,1,0:T(8,128)S(1)}, u32[]{:S(2)}, u32[]{:S(2)}) %collective-permute-start.2) | collective-permute-done | bytes 32800 | tf_op jit(solution)/shard_map/ppermute | solution.py:390
  70.7 0.1 collective-permute-done.3
  70.8 1.9 %collective-permute-done.4 = f32[2,32,128]{2,1,0:T(8,128)S(1)} collective-permute-done((f32[2,32,128]{2,1,0:T(8,128)S(1)}, f32[2,32,128]{2,1,0:T(8,128)S(1)}, u32[]{:S(2)}, u32[]{:S(2)}) %collective-permute-start.4) | collective-permute-done | bytes 32800 | tf_op jit(solution)/shard_map/ppermute | solution.py:390
  72.8 1.1 %collective-permute-start.5 = (bf16[2,32,128]{2,1,0:T(8,128)(2,1)S(1)}, bf16[2,32,128]{2,1,0:T(8,128)(2,1)S(1)}, u32[]{:S(2)}, u32[]{:S(2)}) collective-permute-start(bf16[2,32,128]{2,1,0:T(8,128)(2,1)S(1)} %add_convert_fusion), channel_id=1, source_target_pairs={{0,64},{16,80},{32,96},{48,112},{64,0},{80,16},{96,32},{112,48},{1... | collective-permute-start | bytes 49160 | tf_op jit(solution)/shard_map/ppermute | solution.py:390
  73.9 2.9 %collective-permute-done.5 = bf16[2,32,128]{2,1,0:T(8,128)(2,1)S(1)} collective-permute-done((bf16[2,32,128]{2,1,0:T(8,128)(2,1)S(1)}, bf16[2,32,128]{2,1,0:T(8,128)(2,1)S(1)}, u32[]{:S(2)}, u32[]{:S(2)}) %collective-permute-start.5) | collective-permute-done | bytes 16416 | tf_op jit(solution)/shard_map/ppermute | solution.py:390
  76.8 0.0 all-to-all-done.1.pieces_ref
  76.8 0.7 spread.1
  77.5 6.9 %all-to-all-start.2 = ((bf16[8,128,128]{2,1,0:T(8,128)(2,1)}), bf16[8,128,128]{2,1,0:T(8,128)(2,1)S(1)}, u32[]{:S(2)}, u32[]{:S(2)}) async-start(bf16[8,128,128]{2,1,0:T(8,128)(2,1)} %spread.1), calls=%async_computation.2 | async-start | bytes 524288 | tf_op jit(solution)/shard_map/all_to_all | solution.py:406
  84.4 1.1 %collective-permute-start.8 = (bf16[4,32,128]{2,1,0:T(8,128)(2,1)S(1)}, bf16[4,32,128]{2,1,0:T(8,128)(2,1)S(1)}, u32[]{:S(2)}, u32[]{:S(2)}) collective-permute-start(bf16[4,32,128]{2,1,0:T(8,128)(2,1)S(1)} %pad_maximum_fusion.s0_ref), channel_id=1, source_target_pairs={{0,48},{16,32},{32,16},{48,0},{64,112},{80,96},{96,80},{112,64},{1... | collective-permute-start | bytes 98312 | tf_op jit(solution)/shard_map/ppermute | solution.py:390
  85.5 0.0 collective-permute-start.7
  85.5 3.6 %collective-permute-start.6 = (bf16[4,32,128]{2,1,0:T(8,128)(2,1)S(1)}, bf16[4,32,128]{2,1,0:T(8,128)(2,1)S(1)}, u32[]{:S(2)}, u32[]{:S(2)}) collective-permute-start(bf16[4,32,128]{2,1,0:T(8,128)(2,1)S(1)} %pad_maximum_fusion.s0_ref), channel_id=1, source_target_pairs={{0,32},{16,48},{32,0},{48,16},{64,96},{80,112},{96,64},{112,80},{1... | collective-permute-start | bytes 98312 | tf_op jit(solution)/shard_map/ppermute | solution.py:390
  89.1 2.5 %pool_top.1.top_ref = bf16[64,16,128]{2,1,0:T(8,128)(2,1)S(1)} custom-call(bf16[128,72,128]{2,1,0:T(8,128)(2,1)S(1)} %all-to-all-done.got_ref, s32[5,64,128]{2,1,0:T(8,128)S(1)} %get-tuple-element.29.labels_ref), custom_call_target="tpu_custom_call" | custom-call | flops 1024 | bytes 1 | tf_op jit(solution)/shard_map/pool_top/pallas_call | solution.py:269
  91.6 0.0 collective-permute-done.8.s3_ref
  91.6 0.0 collective-permute-done.7.s2_ref
  91.6 0.0 collective-permute-done.6.s1_ref
  91.6 1.2 %all-to-all-done.2 = bf16[8,128,128]{2,1,0:T(8,128)(2,1)S(1)} async-done(((bf16[8,128,128]{2,1,0:T(8,128)(2,1)}), bf16[8,128,128]{2,1,0:T(8,128)(2,1)S(1)}, u32[]{:S(2)}, u32[]{:S(2)}) %all-to-all-start.2) | async-done | bytes 262176 | tf_op jit(solution)/shard_map/all_to_all | solution.py:406
  92.8 0.0 collective-permute-start.9
  92.8 1.5 %collective-permute-done.9.other_ref = bf16[32,32,128]{2,1,0:T(8,128)(2,1)S(1)} collective-permute-done((bf16[32,32,128]{2,1,0:T(8,128)(2,1)S(1)}, bf16[32,32,128]{2,1,0:T(8,128)(2,1)S(1)}, u32[]{:S(2)}, u32[]{:S(2)}) %collective-permute-start.9) | collective-permute-done | bytes 262176 | tf_op jit(solution)/shard_map/ppermute | solution.py:390
  94.4 0.0 copy-done
  94.4 0.0 copy-done.2
  94.4 0.0 copy-done.3
  94.4 0.0 copy-done.1
  94.4 11.9 %voxel_mlp.1 = bf16[64,16,32,128]{3,2,1,0:T(8,128)(2,1)} custom-call(s32[2]{0:T(128)S(1)} %pad_add_fusion.place_ref, bf16[64,16,128]{2,1,0:T(8,128)(2,1)S(1)} %pool_top.1.top_ref, bf16[32,32,128]{2,1,0:T(8,128)(2,1)S(1)} %bitcast.9, bf16[32,32,128]{2,1,0:T(8,128)(2,1)S(1)} %collective-permute-done.9.other_ref, ...), custom_call_target="tpu_custom_call" | custom-call | flops 4294967296 | bytes 9437184 | tf_op jit(solution)/shard_map/voxel_mlp/pallas_call | solution.py:358
  (3 shorter events, 0.0 us)
Async XLA Ops:
  8.1 42.4 %all-to-all-start = ((bf16[128,72,128]{2,1,0:T(8,128)(2,1)}), bf16[128,72,128]{2,1,0:T(8,128)(2,1)S(1)}, u32[]{:S(2)}, u32[]{:S(2)}) async-start(bf16[128,72,128]{2,1,0:T(8,128)(2,1)} %pack.1), calls=%async_computation | async-start | bytes 4718592 | tf_op jit(solution)/shard_map/all_to_all | solution.py:430
  55.9 2.5 %collective-permute-start = (f32[32,32,128]{2,1,0:T(8,128)S(1)}, f32[32,32,128]{2,1,0:T(8,128)S(1)}, u32[]{:S(2)}, u32[]{:S(2)}) collective-permute-start(f32[32,32,128]{2,1,0:T(8,128)S(1)} %get-tuple-element.27), channel_id=1, source_target_pairs={{0,1},{1,0},{2,3},{3,2},{4,5},{5,4},{6,7},{7,6},{8,9},{9,8},{10,11... | collective-permute-start | bytes 1572872 | tf_op jit(solution)/shard_map/ppermute | solution.py:390
  58.1 36.2 %copy-start = (bf16[128,256]{1,0:T(8,128)(2,1)S(1)}, bf16[128,256]{1,0:T(8,128)(2,1)}, u32[]{:S(2)}) copy-start(bf16[128,256]{1,0:T(8,128)(2,1)} %w_in_ref.1) | copy-start | bytes 196612
  58.2 36.2 %copy-start.2 = (f32[256]{0:T(256)S(1)}, f32[256]{0:T(256)}, u32[]{:S(2)}) copy-start(f32[256]{0:T(256)} %param.16) | copy-start | bytes 3076
  58.2 36.2 %copy-start.3 = (f32[128]{0:T(128)S(1)}, f32[128]{0:T(128)}, u32[]{:S(2)}) copy-start(f32[128]{0:T(128)} %param.18) | copy-start | bytes 1540
  59.3 5.8 %collective-permute-start.1 = (f32[8,32,128]{2,1,0:T(8,128)S(1)}, f32[8,32,128]{2,1,0:T(8,128)S(1)}, u32[]{:S(2)}, u32[]{:S(2)}) collective-permute-start(f32[8,32,128]{2,1,0:T(8,128)S(1)} %get-tuple-element.34), channel_id=1, source_target_pairs={{0,64},{16,80},{32,96},{48,112},{64,0},{80,16},{96,32},{112,48},{1... | collective-permute-start | bytes 393224 | tf_op jit(solution)/shard_map/ppermute | solution.py:390
  60.1 16.6 %all-to-all-start.1 = ((f32[8,128,128]{2,1,0:T(8,128)}), f32[8,128,128]{2,1,0:T(8,128)S(1)}, u32[]{:S(2)}, u32[]{:S(2)}) async-start(f32[8,128,128]{2,1,0:T(8,128)} %bitcast.12), calls=%async_computation.1 | async-start | bytes 1048576 | tf_op jit(solution)/shard_map/all_to_all | solution.py:401
  65.1 29.3 %copy-start.1 = (bf16[256,128]{1,0:T(8,128)(2,1)S(1)}, bf16[256,128]{1,0:T(8,128)(2,1)}, u32[]{:S(2)}) copy-start(bf16[256,128]{1,0:T(8,128)(2,1)} %w_out_ref.1) | copy-start | bytes 196612
  65.1 5.6 %collective-permute-start.2 = (f32[2,32,128]{2,1,0:T(8,128)S(1)}, f32[2,32,128]{2,1,0:T(8,128)S(1)}, u32[]{:S(2)}, u32[]{:S(2)}) collective-permute-start(f32[2,32,128]{2,1,0:T(8,128)S(1)} %get-tuple-element.36), channel_id=1, source_target_pairs={{0,32},{16,48},{32,0},{48,16},{64,96},{80,112},{96,64},{112,80},{1... | collective-permute-start | bytes 98312 | tf_op jit(solution)/shard_map/ppermute | solution.py:390
  66.9 3.9 %collective-permute-start.3 = (f32[2,32,128]{2,1,0:T(8,128)S(1)}, f32[2,32,128]{2,1,0:T(8,128)S(1)}, u32[]{:S(2)}, u32[]{:S(2)}) collective-permute-start(f32[2,32,128]{2,1,0:T(8,128)S(1)} %get-tuple-element.37), channel_id=1, source_target_pairs={{0,16},{16,0},{32,48},{48,32},{64,80},{80,64},{96,112},{112,96},{1... | collective-permute-start | bytes 98312 | tf_op jit(solution)/shard_map/ppermute | solution.py:390
  67.6 5.1 %collective-permute-start.4 = (f32[2,32,128]{2,1,0:T(8,128)S(1)}, f32[2,32,128]{2,1,0:T(8,128)S(1)}, u32[]{:S(2)}, u32[]{:S(2)}) collective-permute-start(f32[2,32,128]{2,1,0:T(8,128)S(1)} %get-tuple-element.38), channel_id=1, source_target_pairs={{0,48},{16,32},{32,16},{48,0},{64,112},{80,96},{96,80},{112,64},{1... | collective-permute-start | bytes 98312 | tf_op jit(solution)/shard_map/ppermute | solution.py:390
  72.8 4.0 %collective-permute-start.5 = (bf16[2,32,128]{2,1,0:T(8,128)(2,1)S(1)}, bf16[2,32,128]{2,1,0:T(8,128)(2,1)S(1)}, u32[]{:S(2)}, u32[]{:S(2)}) collective-permute-start(bf16[2,32,128]{2,1,0:T(8,128)(2,1)S(1)} %add_convert_fusion), channel_id=1, source_target_pairs={{0,64},{16,80},{32,96},{48,112},{64,0},{80,16},{96,32},{112,48},{1... | collective-permute-start | bytes 49160 | tf_op jit(solution)/shard_map/ppermute | solution.py:390
  77.5 15.3 %all-to-all-start.2 = ((bf16[8,128,128]{2,1,0:T(8,128)(2,1)}), bf16[8,128,128]{2,1,0:T(8,128)(2,1)S(1)}, u32[]{:S(2)}, u32[]{:S(2)}) async-start(bf16[8,128,128]{2,1,0:T(8,128)(2,1)} %spread.1), calls=%async_computation.2 | async-start | bytes 524288 | tf_op jit(solution)/shard_map/all_to_all | solution.py:406
  84.4 7.2 %collective-permute-start.8 = (bf16[4,32,128]{2,1,0:T(8,128)(2,1)S(1)}, bf16[4,32,128]{2,1,0:T(8,128)(2,1)S(1)}, u32[]{:S(2)}, u32[]{:S(2)}) collective-permute-start(bf16[4,32,128]{2,1,0:T(8,128)(2,1)S(1)} %pad_maximum_fusion.s0_ref), channel_id=1, source_target_pairs={{0,48},{16,32},{32,16},{48,0},{64,112},{80,96},{96,80},{112,64},{1... | collective-permute-start | bytes 98312 | tf_op jit(solution)/shard_map/ppermute | solution.py:390
  85.5 6.1 %collective-permute-start.7 = (bf16[4,32,128]{2,1,0:T(8,128)(2,1)S(1)}, bf16[4,32,128]{2,1,0:T(8,128)(2,1)S(1)}, u32[]{:S(2)}, u32[]{:S(2)}) collective-permute-start(bf16[4,32,128]{2,1,0:T(8,128)(2,1)S(1)} %pad_maximum_fusion.s0_ref), channel_id=1, source_target_pairs={{0,16},{16,0},{32,48},{48,32},{64,80},{80,64},{96,112},{112,96},{1... | collective-permute-start | bytes 98312 | tf_op jit(solution)/shard_map/ppermute | solution.py:390
  85.5 6.1 %collective-permute-start.6 = (bf16[4,32,128]{2,1,0:T(8,128)(2,1)S(1)}, bf16[4,32,128]{2,1,0:T(8,128)(2,1)S(1)}, u32[]{:S(2)}, u32[]{:S(2)}) collective-permute-start(bf16[4,32,128]{2,1,0:T(8,128)(2,1)S(1)} %pad_maximum_fusion.s0_ref), channel_id=1, source_target_pairs={{0,32},{16,48},{32,0},{48,16},{64,96},{80,112},{96,64},{112,80},{1... | collective-permute-start | bytes 98312 | tf_op jit(solution)/shard_map/ppermute | solution.py:390
  92.8 1.5 %collective-permute-start.9 = (bf16[32,32,128]{2,1,0:T(8,128)(2,1)S(1)}, bf16[32,32,128]{2,1,0:T(8,128)(2,1)S(1)}, u32[]{:S(2)}, u32[]{:S(2)}) collective-permute-start(bf16[32,32,128]{2,1,0:T(8,128)(2,1)S(1)} %bitcast.8), channel_id=1, source_target_pairs={{0,1},{1,0},{2,3},{3,2},{4,5},{5,4},{6,7},{7,6},{8,9},{9,8},{10,11... | collective-permute-start | bytes 786440 | tf_op jit(solution)/shard_map/ppermute | solution.py:390

commit v6 on v5

--- a/solution.py
+++ b/solution.py
@@ -292,17 +292,6 @@
     return call(pool_side_kernel, [points, labels], [shape, shape], [], 2 * 8192 * 512 * 256, "pool_side")
 
 
-def fold_kernel(keep_ref, got_ref, *out_refs):
-    for k, out in enumerate(out_refs):
-        rows = pl.ds(k * 2, 2)
-        out[...] = keep_ref[rows] + got_ref[rows]
-
-
-def fold(keep, got):
-    shape = jax.ShapeDtypeStruct((2, NZ, C), F32)
-    return call(fold_kernel, [keep, got], [shape] * 4, [], 1024, "fold")
-
-
 def pool_top(got, labels):
     return call(
         pool_top_kernel,
@@ -319,15 +308,14 @@
 
 
 def mlp_kernel(
-    place_ref, top_ref, mine_ref, other_ref, s0_ref, s1_ref, s2_ref, s3_ref,
+    place_ref, top_ref, mine_ref, other_ref, near_ref, far_ref,
     w_in_ref, b_in_ref, w_out_ref, b_out_ref, out_ref, side_ref, wide_ref, half_ref,
 ):
     @pl.when(pl.program_id(0) == 0)
     def _():
-        for k, rows in enumerate((s0_ref, s1_ref, s2_ref, s3_ref)):
-            for j in range(4):
-                y = k * 2 + j if j < 2 else BY // 2 + k * 2 + j - 2
-                side_ref[y ^ place_ref[1]] = rows[j].astype(F32)
+        for y in range(BY // 2):
+            side_ref[y ^ place_ref[1]] = near_ref[y].astype(F32)
+            side_ref[(y + BY // 2) ^ place_ref[1]] = far_ref[y].astype(F32)
         bias = b_in_ref[...]
         high = bias.astype(BF16).astype(F32)
         middle = (bias - high).astype(BF16).astype(F32)
@@ -351,7 +339,7 @@
         out_ref[i] = result.astype(BF16).reshape(BY, NZ, C)
 
 
-def mlp(place, top, mine, other, sides, w_in, b_in, w_out, b_out):
+def mlp(place, top, mine, other, near, far, w_in, b_in, w_out, b_out):
     def same(*shape):
         return pl.BlockSpec(shape, lambda i, h: (0,) * len(shape))
 
@@ -365,7 +353,7 @@
                 pl.BlockSpec((STEP, NZ, C), lambda i, h: (jnp.minimum(i, HALF_STEPS - 1), 0, 0)),
                 pl.BlockSpec((STEP, NZ, C), lambda i, h: (jnp.maximum(i - HALF_STEPS, 0), 0, 0)),
             ]
-            + [same(4, NZ, C)] * 4
+            + [same(BY // 2, NZ, C)] * 2
             + [same(C, HID), same(1, HID), same(HID, C), same(1, C)],
             out_specs=pl.BlockSpec((STEP, BY, NZ, C), lambda i, h: (i ^ (h[0] * HALF_STEPS), 0, 0, 0)),
             scratch_shapes=[
@@ -380,7 +368,7 @@
             flops=4 * BX * BY * NZ * C * HID, bytes_accessed=9 * 2**20, transcendentals=BX * BY * NZ * HID
         ),
         name="voxel_mlp",
-    )(place, top, mine, other, *sides, w_in, b_in.reshape(1, HID), w_out, b_out.reshape(1, C))
+    )(place, top, mine, other, near, far, w_in, b_in.reshape(1, HID), w_out, b_out.reshape(1, C))
 
 
 SAME_CORE = [list(range(core, N_GY, 2)) for core in range(2)]
@@ -407,16 +395,18 @@
     return whole.reshape(BX // 2, NZ, C)
 
 
-def side_share(keep, send):
-    parts = fold(keep, swap(send, "gx", N_GX, 4))
-    share = (
-        parts[0] + swap(parts[1], "gx", N_GX, 2) + swap(parts[2], "gx", N_GX, 1) + swap(parts[3], "gx", N_GX, 3)
-    ).astype(BF16)
-    return jnp.concatenate([share, swap(share, "gx", N_GX, 4)], axis=0)
-
-
-def side_gather(share):
-    return [share] + [swap(share, "gx", N_GX, bit) for bit in (2, 1, 3)]
+def sum_kernel(mine_ref, got_ref, out_ref):
+    out_ref[...] = mine_ref[...] + got_ref[...]
+
+
+def pair_sum(mine, got):
+    return call(sum_kernel, [mine, got], [jax.ShapeDtypeStruct(mine.shape, F32)], [], 1024, "pair_sum")[0]
+
+
+def side_near(keep, send):
+    part = pair_sum(keep, swap(send, "gx", N_GX, 4))
+    others = [swap(part, "gx", N_GX, bit) for bit in (2, 1, 3)]
+    return (part + others[0] + others[1] + others[2]).astype(BF16)
 
 
 def per_device(
@@ -424,20 +414,20 @@
 ):
     row = lax.axis_index("gx")
     place = jnp.stack(
-        [lax.axis_index("gy") & 1, (row >> 2 & 1) * 8 + (row & 1) * 4 + (row >> 1 & 1) * 2]
+        [lax.axis_index("gy") & 1, (row >> 2 & 1) * (BY // 2)]
     ).astype(jnp.int32)
     sent = pack(camera_of_device, point_feats, top_bin, front_bin, camera_embed)
     got = lax.all_to_all(sent, ("gx", "gy"), split_axis=0, concat_axis=0, tiled=True)
     mine, other, labels, points = pool_front(place, got)
     keep, send = pool_side(points, labels)
-    mine = mine + swap(other, "gy", N_GY, 1)
+    mine = pair_sum(mine, swap(other, "gy", N_GY, 1))
     mine, keep, send = lax.optimization_barrier((mine, keep, send))
     top = pool_top(got, labels)
-    front, side = lax.optimization_barrier((front_share(mine), side_share(keep, send)))
+    front, near = lax.optimization_barrier((front_share(mine), side_near(keep, send)))
     mine = front_gather(front)
-    mine, top, *sides = lax.optimization_barrier([mine, top] + side_gather(side))
+    mine, top, near, far = lax.optimization_barrier((mine, top, near, swap(near, "gx", N_GX, 4)))
     other = swap(mine, "gy", N_GY, 1)
-    return mlp(place, top, mine, other, sides, w_in, b_in, w_out, b_out)
+    return mlp(place, top, mine, other, near, far, w_in, b_in, w_out, b_out)
 
 
 def solution(mesh):

time: 108 us -> 106 us (0.981)
  starting transfers between devices: 33.9 us -> 29 us
  waiting for transfers between devices: 41.4 us -> 44.2 us
    ppermute x10 -> x7, starting transfers between devices: 11.8 us -> 7.54 us  [swap(): return lax.ppermute(array, axis, [(i, i ^ bit) for i in range(size)])]
    all_to_all x1, waiting for transfers between devices: 1.2 us -> 3.74 us  [front_gather(): lax.all_to_all(copies, 'gy', 0, 0, tiled=True, axis_index_groups=SAME_CORE)]
    pallas_call x5 -> x6, Pallas kernels: 9.92 us -> 10.8 us  [call(): pl.pallas_call(kernel, out_shape=outs, in_specs=[small if i.dtype == jnp....]
    ppermute x10 -> x7, waiting for transfers between devices: 9.02 us -> 9.33 us  [swap(): return lax.ppermute(array, axis, [(i, i ^ bit) for i in range(size)])]
  transfers between devices with their start and end apart: 13 -> 10, of which waited for: 9 -> 9; matrix products, arithmetic and copies ran while one was open for 0% -> 0% of each run, Pallas kernels for 4% -> 4%
where the time goes in v6:
time: 106 us; the launch traced here: 104 us
  waiting for transfers between devices  44.2 us (42%)
  Pallas kernels  30.1 us (28%)
  starting transfers between devices  29 us (27%)
    all_to_all x1, waiting for transfers between devices, per_device(): lax.all_to_all(sent, ('gx', 'gy'), split_axis=0, concat_axis=0, tiled=True)  31.2 us
    pallas_call x1, Pallas kernels, mlp(): pl.pallas_call(mlp_kernel, grid_spec=pltpu.PrefetchScalarGridSpec(num_sca...  11.9 us
    all_to_all x1, starting transfers between devices, per_device(): lax.all_to_all(sent, ('gx', 'gy'), split_axis=0, concat_axis=0, tiled=True)  11.1 us
    pallas_call x6, Pallas kernels, call(): pl.pallas_call(kernel, out_shape=outs, in_specs=[small if i.dtype == jnp....  10.8 us
    ppermute x7, waiting for transfers between devices, swap(): return lax.ppermute(array, axis, [(i, i ^ bit) for i in range(size)])  9.33 us
    ppermute x7, starting transfers between devices, swap(): return lax.ppermute(array, axis, [(i, i ^ bit) for i in range(size)])  7.54 us
    pallas_call x1, Pallas kernels, pack(): pl.pallas_call(pack_kernel, out_shape=jax.ShapeDtypeStruct((DEVICES, ROWS...  7.44 us
    all_to_all x1, starting transfers between devices, front_gather(): lax.all_to_all(copies, 'gy', 0, 0, tiled=True, axis_index_groups=SAME_CORE)  6.21 us
  transfers between devices with their start and end apart: 10, of which 9 were waited for; matrix products, arithmetic and copies ran while one was open for 0% of the time, Pallas kernels for 4%

profile of v6, /device:TPU:0, one launch (start us, length us, event | category | flops | bytes accessed | tf_op | source)
XLA Modules:
  0.0 104.2 jit_solution(13866941316080702857)
XLA Ops:
  0.7 7.4 %pack.1 = bf16[128,72,128]{2,1,0:T(8,128)(2,1)} custom-call(s32[1]{0:T(128)S(6)} %copy.10.cam_ref, bf16[4096,128]{1,0:T(8,128)(2,1)} %feats_hbm.1, s32[32,128]{1,0:T(8,128)} %bitcast.12, s32[32,128]{1,0:T(8,128)} %bitcast.13, f32[6,128]{1,0:T(8,128)} %embed_hbm.1), custom_call_target="tpu_custom_call" | custom-call | flops 8589934592 | bytes 4194304 | tf_op jit(solution)/shard_map/pack/pallas_call | solution.py:188
  8.1 11.1 %all-to-all-start = ((bf16[128,72,128]{2,1,0:T(8,128)(2,1)}), bf16[128,72,128]{2,1,0:T(8,128)(2,1)S(1)}, u32[]{:S(2)}, u32[]{:S(2)}) async-start(bf16[128,72,128]{2,1,0:T(8,128)(2,1)} %pack.1), calls=%async_computation | async-start | bytes 4718592 | tf_op jit(solution)/shard_map/all_to_all | solution.py:420
  19.3 0.1 pad_add_fusion.place_ref
  19.3 31.2 %all-to-all-done.got_ref = bf16[128,72,128]{2,1,0:T(8,128)(2,1)S(1)} async-done(((bf16[128,72,128]{2,1,0:T(8,128)(2,1)}), bf16[128,72,128]{2,1,0:T(8,128)(2,1)S(1)}, u32[]{:S(2)}, u32[]{:S(2)}) %all-to-all-start) | async-done | bytes 2359328 | tf_op jit(solution)/shard_map/all_to_all | solution.py:420
  50.5 5.4 %pool_front.1 = (f32[32,32,128]{2,1,0:T(8,128)S(1)}, f32[32,32,128]{2,1,0:T(8,128)S(1)}, s32[5,64,128]{2,1,0:T(8,128)S(1)}, bf16[8192,256]{1,0:T(8,128)(2,1)S(1)}) custom-call(s32[2]{0:T(128)S(1)} %pad_add_fusion.place_ref, bf16[128,72,128]{2,1,0:T(8,128)(2,1)S(1)} %all-to-all-done.got_ref), custom_call_target="tpu_custom_call" | custom-call | flops 8589934592 | bytes 8388608 | tf_op jit(solution)/shard_map/pool_front/pallas_call | solution.py:269
  55.9 1.0 collective-permute-start
  56.9 1.2 %pool_side.1 = (f32[8,32,128]{2,1,0:T(8,128)S(1)}, f32[8,32,128]{2,1,0:T(8,128)S(1)}) custom-call(bf16[8192,256]{1,0:T(8,128)(2,1)S(1)} %get-tuple-element.22.rhs_ref, s32[5,64,128]{2,1,0:T(8,128)S(1)} %get-tuple-element.23.labels_ref), custom_call_target="tpu_custom_call" | custom-call | flops 2147483648 | bytes 2097152 | tf_op jit(solution)/shard_map/pool_side/pallas_call | solution.py:269
  58.1 0.0 copy-start
  58.1 0.0 copy-start.2
  58.2 0.0 copy-start.3
  58.2 0.2 collective-permute-done.got_ref
  58.4 0.8 pair_sum.2
  59.3 0.8 collective-permute-start.1
  60.1 4.1 %all-to-all-start.1 = ((f32[8,128,128]{2,1,0:T(8,128)}), f32[8,128,128]{2,1,0:T(8,128)S(1)}, u32[]{:S(2)}, u32[]{:S(2)}) async-start(f32[8,128,128]{2,1,0:T(8,128)} %bitcast.4), calls=%async_computation.1 | async-start | bytes 1048576 | tf_op jit(solution)/shard_map/all_to_all | solution.py:389
  64.2 0.9 collective-permute-done.1.got_ref
  65.0 0.0 copy-start.1
  65.1 1.7 %collective-permute-start.4 = (f32[8,32,128]{2,1,0:T(8,128)S(1)}, f32[8,32,128]{2,1,0:T(8,128)S(1)}, u32[]{:S(2)}, u32[]{:S(2)}) collective-permute-start(f32[8,32,128]{2,1,0:T(8,128)S(1)} %pair_sum.3), channel_id=1, source_target_pairs={{0,48},{16,32},{32,16},{48,0},{64,112},{80,96},{96,80},{112,64},{1... | collective-permute-start | bytes 393224 | tf_op jit(solution)/shard_map/ppermute | solution.py:378
  66.7 0.1 collective-permute-start.3
  66.8 3.0 %collective-permute-start.2 = (f32[8,32,128]{2,1,0:T(8,128)S(1)}, f32[8,32,128]{2,1,0:T(8,128)S(1)}, u32[]{:S(2)}, u32[]{:S(2)}) collective-permute-start(f32[8,32,128]{2,1,0:T(8,128)S(1)} %pair_sum.3), channel_id=1, source_target_pairs={{0,32},{16,48},{32,0},{48,16},{64,96},{80,112},{96,64},{112,80},{1... | collective-permute-start | bytes 393224 | tf_op jit(solution)/shard_map/ppermute | solution.py:378
  69.8 2.1 %collective-permute-done.4 = f32[8,32,128]{2,1,0:T(8,128)S(1)} collective-permute-done((f32[8,32,128]{2,1,0:T(8,128)S(1)}, f32[8,32,128]{2,1,0:T(8,128)S(1)}, u32[]{:S(2)}, u32[]{:S(2)}) %collective-permute-start.4) | collective-permute-done | bytes 131104 | tf_op jit(solution)/shard_map/ppermute | solution.py:378
  71.9 0.7 collective-permute-done.3
  72.6 2.7 %collective-permute-done.2 = f32[8,32,128]{2,1,0:T(8,128)S(1)} collective-permute-done((f32[8,32,128]{2,1,0:T(8,128)S(1)}, f32[8,32,128]{2,1,0:T(8,128)S(1)}, u32[]{:S(2)}, u32[]{:S(2)}) %collective-permute-start.2) | collective-permute-done | bytes 131104 | tf_op jit(solution)/shard_map/ppermute | solution.py:378
  75.3 0.0 all-to-all-done.1.pieces_ref
  75.4 0.7 spread.1
  76.1 6.2 %all-to-all-start.2 = ((bf16[8,128,128]{2,1,0:T(8,128)(2,1)}), bf16[8,128,128]{2,1,0:T(8,128)(2,1)S(1)}, u32[]{:S(2)}, u32[]{:S(2)}) async-start(bf16[8,128,128]{2,1,0:T(8,128)(2,1)} %spread.1), calls=%async_computation.2 | async-start | bytes 524288 | tf_op jit(solution)/shard_map/all_to_all | solution.py:394
  82.3 0.9 collective-permute-start.5
  83.3 2.5 %pool_top.1.top_ref = bf16[64,16,128]{2,1,0:T(8,128)(2,1)S(1)} custom-call(bf16[128,72,128]{2,1,0:T(8,128)(2,1)S(1)} %all-to-all-done.got_ref, s32[5,64,128]{2,1,0:T(8,128)S(1)} %get-tuple-element.23.labels_ref), custom_call_target="tpu_custom_call" | custom-call | flops 1024 | bytes 1 | tf_op jit(solution)/shard_map/pool_top/pallas_call | solution.py:269
  85.8 1.2 %collective-permute-done.5.far_ref = bf16[8,32,128]{2,1,0:T(8,128)(2,1)S(1)} collective-permute-done((bf16[8,32,128]{2,1,0:T(8,128)(2,1)S(1)}, bf16[8,32,128]{2,1,0:T(8,128)(2,1)S(1)}, u32[]{:S(2)}, u32[]{:S(2)}) %collective-permute-start.5) | collective-permute-done | bytes 65568 | tf_op jit(solution)/shard_map/ppermute | solution.py:378
  87.0 3.7 %all-to-all-done.2 = bf16[8,128,128]{2,1,0:T(8,128)(2,1)S(1)} async-done(((bf16[8,128,128]{2,1,0:T(8,128)(2,1)}), bf16[8,128,128]{2,1,0:T(8,128)(2,1)S(1)}, u32[]{:S(2)}, u32[]{:S(2)}) %all-to-all-start.2) | async-done | bytes 262176 | tf_op jit(solution)/shard_map/all_to_all | solution.py:394
  90.7 0.0 collective-permute-start.6
  90.7 1.5 %collective-permute-done.6.other_ref = bf16[32,32,128]{2,1,0:T(8,128)(2,1)S(1)} collective-permute-done((bf16[32,32,128]{2,1,0:T(8,128)(2,1)S(1)}, bf16[32,32,128]{2,1,0:T(8,128)(2,1)S(1)}, u32[]{:S(2)}, u32[]{:S(2)}) %collective-permute-start.6) | collective-permute-done | bytes 262176 | tf_op jit(solution)/shard_map/ppermute | solution.py:378
  92.3 0.0 copy-done
  92.3 0.0 copy-done.2
  92.3 0.0 copy-done.3
  92.3 0.0 copy-done.1
  92.3 11.9 %voxel_mlp.1 = bf16[64,16,32,128]{3,2,1,0:T(8,128)(2,1)} custom-call(s32[2]{0:T(128)S(1)} %pad_add_fusion.place_ref, bf16[64,16,128]{2,1,0:T(8,128)(2,1)S(1)} %pool_top.1.top_ref, bf16[32,32,128]{2,1,0:T(8,128)(2,1)S(1)} %bitcast.9, bf16[32,32,128]{2,1,0:T(8,128)(2,1)S(1)} %collective-permute-done.6.other_ref, ...), custom_call_target="tpu_custom_call" | custom-call | flops 4294967296 | bytes 9437184 | tf_op jit(solution)/shard_map/voxel_mlp/pallas_call | solution.py:346
  (2 shorter events, 0.1 us)
Async XLA Ops:
  8.1 42.4 %all-to-all-start = ((bf16[128,72,128]{2,1,0:T(8,128)(2,1)}), bf16[128,72,128]{2,1,0:T(8,128)(2,1)S(1)}, u32[]{:S(2)}, u32[]{:S(2)}) async-start(bf16[128,72,128]{2,1,0:T(8,128)(2,1)} %pack.1), calls=%async_computation | async-start | bytes 4718592 | tf_op jit(solution)/shard_map/all_to_all | solution.py:420
  55.9 2.5 %collective-permute-start = (f32[32,32,128]{2,1,0:T(8,128)S(1)}, f32[32,32,128]{2,1,0:T(8,128)S(1)}, u32[]{:S(2)}, u32[]{:S(2)}) collective-permute-start(f32[32,32,128]{2,1,0:T(8,128)S(1)} %get-tuple-element.21), channel_id=1, source_target_pairs={{0,1},{1,0},{2,3},{3,2},{4,5},{5,4},{6,7},{7,6},{8,9},{9,8},{10,11... | collective-permute-start | bytes 1572872 | tf_op jit(solution)/shard_map/ppermute | solution.py:378
  58.1 34.1 %copy-start = (bf16[128,256]{1,0:T(8,128)(2,1)S(1)}, bf16[128,256]{1,0:T(8,128)(2,1)}, u32[]{:S(2)}) copy-start(bf16[128,256]{1,0:T(8,128)(2,1)} %w_in_ref.1) | copy-start | bytes 196612
  58.1 34.1 %copy-start.2 = (f32[256]{0:T(256)S(1)}, f32[256]{0:T(256)}, u32[]{:S(2)}) copy-start(f32[256]{0:T(256)} %param.16) | copy-start | bytes 3076
  58.2 34.1 %copy-start.3 = (f32[128]{0:T(128)S(1)}, f32[128]{0:T(128)}, u32[]{:S(2)}) copy-start(f32[128]{0:T(128)} %param.18) | copy-start | bytes 1540
  59.3 5.8 %collective-permute-start.1 = (f32[8,32,128]{2,1,0:T(8,128)S(1)}, f32[8,32,128]{2,1,0:T(8,128)S(1)}, u32[]{:S(2)}, u32[]{:S(2)}) collective-permute-start(f32[8,32,128]{2,1,0:T(8,128)S(1)} %get-tuple-element.28), channel_id=1, source_target_pairs={{0,64},{16,80},{32,96},{48,112},{64,0},{80,16},{96,32},{112,48},{1... | collective-permute-start | bytes 393224 | tf_op jit(solution)/shard_map/ppermute | solution.py:378
  60.1 15.2 %all-to-all-start.1 = ((f32[8,128,128]{2,1,0:T(8,128)}), f32[8,128,128]{2,1,0:T(8,128)S(1)}, u32[]{:S(2)}, u32[]{:S(2)}) async-start(f32[8,128,128]{2,1,0:T(8,128)} %bitcast.4), calls=%async_computation.1 | async-start | bytes 1048576 | tf_op jit(solution)/shard_map/all_to_all | solution.py:389
  65.0 27.3 %copy-start.1 = (bf16[256,128]{1,0:T(8,128)(2,1)S(1)}, bf16[256,128]{1,0:T(8,128)(2,1)}, u32[]{:S(2)}) copy-start(bf16[256,128]{1,0:T(8,128)(2,1)} %w_out_ref.1) | copy-start | bytes 196612
  65.1 6.8 %collective-permute-start.4 = (f32[8,32,128]{2,1,0:T(8,128)S(1)}, f32[8,32,128]{2,1,0:T(8,128)S(1)}, u32[]{:S(2)}, u32[]{:S(2)}) collective-permute-start(f32[8,32,128]{2,1,0:T(8,128)S(1)} %pair_sum.3), channel_id=1, source_target_pairs={{0,48},{16,32},{32,16},{48,0},{64,112},{80,96},{96,80},{112,64},{1... | collective-permute-start | bytes 393224 | tf_op jit(solution)/shard_map/ppermute | solution.py:378
  66.7 5.8 %collective-permute-start.3 = (f32[8,32,128]{2,1,0:T(8,128)S(1)}, f32[8,32,128]{2,1,0:T(8,128)S(1)}, u32[]{:S(2)}, u32[]{:S(2)}) collective-permute-start(f32[8,32,128]{2,1,0:T(8,128)S(1)} %pair_sum.3), channel_id=1, source_target_pairs={{0,16},{16,0},{32,48},{48,32},{64,80},{80,64},{96,112},{112,96},{1... | collective-permute-start | bytes 393224 | tf_op jit(solution)/shard_map/ppermute | solution.py:378
  66.8 8.5 %collective-permute-start.2 = (f32[8,32,128]{2,1,0:T(8,128)S(1)}, f32[8,32,128]{2,1,0:T(8,128)S(1)}, u32[]{:S(2)}, u32[]{:S(2)}) collective-permute-start(f32[8,32,128]{2,1,0:T(8,128)S(1)} %pair_sum.3), channel_id=1, source_target_pairs={{0,32},{16,48},{32,0},{48,16},{64,96},{80,112},{96,64},{112,80},{1... | collective-permute-start | bytes 393224 | tf_op jit(solution)/shard_map/ppermute | solution.py:378
  76.1 14.6 %all-to-all-start.2 = ((bf16[8,128,128]{2,1,0:T(8,128)(2,1)}), bf16[8,128,128]{2,1,0:T(8,128)(2,1)S(1)}, u32[]{:S(2)}, u32[]{:S(2)}) async-start(bf16[8,128,128]{2,1,0:T(8,128)(2,1)} %spread.1), calls=%async_computation.2 | async-start | bytes 524288 | tf_op jit(solution)/shard_map/all_to_all | solution.py:394
  82.3 4.7 %collective-permute-start.5 = (bf16[8,32,128]{2,1,0:T(8,128)(2,1)S(1)}, bf16[8,32,128]{2,1,0:T(8,128)(2,1)S(1)}, u32[]{:S(2)}, u32[]{:S(2)}) collective-permute-start(bf16[8,32,128]{2,1,0:T(8,128)(2,1)S(1)} %add_convert_fusion.near_ref), channel_id=1, source_target_pairs={{0,64},{16,80},{32,96},{48,112},{64,0},{80,16},{96,32},{112,48},{1... | collective-permute-start | bytes 196616 | tf_op jit(solution)/shard_map/ppermute | solution.py:378
  90.7 1.5 %collective-permute-start.6 = (bf16[32,32,128]{2,1,0:T(8,128)(2,1)S(1)}, bf16[32,32,128]{2,1,0:T(8,128)(2,1)S(1)}, u32[]{:S(2)}, u32[]{:S(2)}) collective-permute-start(bf16[32,32,128]{2,1,0:T(8,128)(2,1)S(1)} %bitcast.8), channel_id=1, source_target_pairs={{0,1},{1,0},{2,3},{3,2},{4,5},{5,4},{6,7},{7,6},{8,9},{9,8},{10,11... | collective-permute-start | bytes 786440 | tf_op jit(solution)/shard_map/ppermute | solution.py:378

commit v7 on v6

--- a/solution.py
+++ b/solution.py
@@ -303,65 +303,63 @@
     )[0]
 
 
-STEP = 16
-HALF_STEPS = BX // STEP // 2
+PIECE = 4
+PIECES = BX // PIECE
 
 
 def mlp_kernel(
-    place_ref, top_ref, mine_ref, other_ref, near_ref, far_ref,
-    w_in_ref, b_in_ref, w_out_ref, b_out_ref, out_ref, side_ref, wide_ref, half_ref,
+    place_ref, top_ref, mine_ref, other_ref, near_ref, far_ref, w_in_ref, b_in_ref, w_out_ref, b_out_ref, out_hbm,
+    side_ref, wide_ref, half_ref, out_ref, sems,
 ):
-    @pl.when(pl.program_id(0) == 0)
-    def _():
-        for y in range(BY // 2):
-            side_ref[y ^ place_ref[1]] = near_ref[y].astype(F32)
-            side_ref[(y + BY // 2) ^ place_ref[1]] = far_ref[y].astype(F32)
-        bias = b_in_ref[...]
-        high = bias.astype(BF16).astype(F32)
-        middle = (bias - high).astype(BF16).astype(F32)
-        low = bias - high - middle
-        row = iota((C, HID), 0)
-        rest = jnp.where(row == 0, high, jnp.where(row == 1, middle, jnp.where(row == 2, low, 0.0)))
-        wide_ref[0:C, :] = w_in_ref[...]
-        wide_ref[C : 2 * C, :] = rest.astype(BF16)
-        half_ref[...] = (w_out_ref[...].astype(F32) * 0.5).astype(BF16)
-
-    mine = pl.program_id(0) < HALF_STEPS
+    for y in range(BY // 2):
+        side_ref[y ^ place_ref[1]] = near_ref[y].astype(F32)
+        side_ref[(y + BY // 2) ^ place_ref[1]] = far_ref[y].astype(F32)
+    bias = b_in_ref[...]
+    high = bias.astype(BF16).astype(F32)
+    middle = (bias - high).astype(BF16).astype(F32)
+    low = bias - high - middle
+    row = iota((C, HID), 0)
+    rest = jnp.where(row == 0, high, jnp.where(row == 1, middle, jnp.where(row == 2, low, 0.0)))
+    wide_ref[0:C, :] = w_in_ref[...]
+    wide_ref[C : 2 * C, :] = rest.astype(BF16)
+    half_ref[...] = (w_out_ref[...].astype(F32) * 0.5).astype(BF16)
+
+    def store(piece):
+        return pltpu.make_async_copy(
+            out_ref.at[pl.ds(piece * PIECE, PIECE)],
+            out_hbm.at[pl.ds((piece ^ (place_ref[0] * (PIECES // 2))) * PIECE, PIECE)],
+            sems.at[piece],
+        )
+
     ones = jnp.where(iota((BY * NZ, C), 1) < 3, 1.0, 0.0).astype(BF16)
-    for i in range(STEP):
+    for i in range(BX):
         top = top_ref[i].astype(F32)
-        front = jnp.where(mine, mine_ref[i].astype(F32), other_ref[i].astype(F32))
+        front = (mine_ref[i] if i < BX // 2 else other_ref[i - BX // 2]).astype(F32)
         cell = (top[:, None, :] + front[None, :, :] + side_ref[...]).astype(BF16).reshape(BY * NZ, C)
         inner = jnp.dot(jnp.concatenate([cell, ones], axis=1), wide_ref[...], preferred_element_type=F32)
         twice = (inner * (1.0 + lax.erf(inner * 0.7071067811865476))).astype(BF16)
         result = jnp.dot(twice, half_ref[...], preferred_element_type=F32)
         result = result + (b_out_ref[...] + cell.astype(F32))
         out_ref[i] = result.astype(BF16).reshape(BY, NZ, C)
+        if i % PIECE == PIECE - 1:
+            store(i // PIECE).start()
+    for piece in range(PIECES):
+        store(piece).wait()
 
 
 def mlp(place, top, mine, other, near, far, w_in, b_in, w_out, b_out):
-    def same(*shape):
-        return pl.BlockSpec(shape, lambda i, h: (0,) * len(shape))
-
+    whole = pl.BlockSpec(memory_space=pltpu.VMEM)
     return pl.pallas_call(
         mlp_kernel,
-        grid_spec=pltpu.PrefetchScalarGridSpec(
-            num_scalar_prefetch=1,
-            grid=(BX // STEP,),
-            in_specs=[
-                pl.BlockSpec((STEP, BY, C), lambda i, h: (i, 0, 0)),
-                pl.BlockSpec((STEP, NZ, C), lambda i, h: (jnp.minimum(i, HALF_STEPS - 1), 0, 0)),
-                pl.BlockSpec((STEP, NZ, C), lambda i, h: (jnp.maximum(i - HALF_STEPS, 0), 0, 0)),
-            ]
-            + [same(BY // 2, NZ, C)] * 2
-            + [same(C, HID), same(1, HID), same(HID, C), same(1, C)],
-            out_specs=pl.BlockSpec((STEP, BY, NZ, C), lambda i, h: (i ^ (h[0] * HALF_STEPS), 0, 0, 0)),
-            scratch_shapes=[
-                pltpu.VMEM((BY, NZ, C), F32),
-                pltpu.VMEM((2 * C, HID), BF16),
-                pltpu.VMEM((HID, C), BF16),
-            ],
-        ),
+        in_specs=[pl.BlockSpec(memory_space=pltpu.SMEM)] + [whole] * 9,
+        out_specs=pl.BlockSpec(memory_space=pl.ANY),
+        scratch_shapes=[
+            pltpu.VMEM((BY, NZ, C), F32),
+            pltpu.VMEM((2 * C, HID), BF16),
+            pltpu.VMEM((HID, C), BF16),
+            pltpu.VMEM((BX, BY, NZ, C), BF16),
+            pltpu.SemaphoreType.DMA((PIECES,)),
+        ],
         out_shape=jax.ShapeDtypeStruct((BX, BY, NZ, C), BF16),
         compiler_params=pltpu.CompilerParams(vmem_limit_bytes=MLP_LIMIT),
         cost_estimate=pl.CostEstimate(

time: 106 us -> 104 us (0.981)
  Pallas kernels: 30.1 us -> 28.7 us
    pallas_call x1, Pallas kernels: 11.9 us -> 10.5 us  [mlp(): pl.pallas_call(mlp_kernel, in_specs=[pl.BlockSpec(memory_space=pltpu.SMEM...]
where the time goes in v7:
time: 104 us; the launch traced here: 103 us
  waiting for transfers between devices  44.2 us (42%)
  starting transfers between devices  29 us (28%)
  Pallas kernels  28.7 us (28%)
    all_to_all x1, waiting for transfers between devices, per_device(): lax.all_to_all(sent, ('gx', 'gy'), split_axis=0, concat_axis=0, tiled=True)  31.2 us
    all_to_all x1, starting transfers between devices, per_device(): lax.all_to_all(sent, ('gx', 'gy'), split_axis=0, concat_axis=0, tiled=True)  11.2 us
    pallas_call x6, Pallas kernels, call(): pl.pallas_call(kernel, out_shape=outs, in_specs=[small if i.dtype == jnp....  10.8 us
    pallas_call x1, Pallas kernels, mlp(): pl.pallas_call(mlp_kernel, in_specs=[pl.BlockSpec(memory_space=pltpu.SMEM...  10.5 us
    ppermute x7, waiting for transfers between devices, swap(): return lax.ppermute(array, axis, [(i, i ^ bit) for i in range(size)])  9.33 us
    ppermute x7, starting transfers between devices, swap(): return lax.ppermute(array, axis, [(i, i ^ bit) for i in range(size)])  7.53 us
    pallas_call x1, Pallas kernels, pack(): pl.pallas_call(pack_kernel, out_shape=jax.ShapeDtypeStruct((DEVICES, ROWS...  7.44 us
    all_to_all x1, starting transfers between devices, front_gather(): lax.all_to_all(copies, 'gy', 0, 0, tiled=True, axis_index_groups=SAME_CORE)  6.21 us
  transfers between devices with their start and end apart: 10, of which 9 were waited for; matrix products, arithmetic and copies ran while one was open for 0% of the time, Pallas kernels for 4%

profile of v7, /device:TPU:0, one launch (start us, length us, event | category | flops | bytes accessed | tf_op | source)
XLA Modules:
  0.0 103.0 jit_solution(15783265838251562225)
XLA Ops:
  0.7 7.4 %pack.1 = bf16[128,72,128]{2,1,0:T(8,128)(2,1)} custom-call(s32[1]{0:T(128)S(6)} %copy.10.cam_ref, bf16[4096,128]{1,0:T(8,128)(2,1)} %feats_hbm.1, s32[32,128]{1,0:T(8,128)} %bitcast.12, s32[32,128]{1,0:T(8,128)} %bitcast.13, f32[6,128]{1,0:T(8,128)} %embed_hbm.1), custom_call_target="tpu_custom_call" | custom-call | flops 8589934592 | bytes 4194304 | tf_op jit(solution)/shard_map/pack/pallas_call | solution.py:188
  8.1 11.2 %all-to-all-start = ((bf16[128,72,128]{2,1,0:T(8,128)(2,1)}), bf16[128,72,128]{2,1,0:T(8,128)(2,1)S(1)}, u32[]{:S(2)}, u32[]{:S(2)}) async-start(bf16[128,72,128]{2,1,0:T(8,128)(2,1)} %pack.1), calls=%async_computation | async-start | bytes 4718592 | tf_op jit(solution)/shard_map/all_to_all | solution.py:418
  19.3 0.1 pad_add_fusion.place_ref
  19.3 31.2 %all-to-all-done.got_ref = bf16[128,72,128]{2,1,0:T(8,128)(2,1)S(1)} async-done(((bf16[128,72,128]{2,1,0:T(8,128)(2,1)}), bf16[128,72,128]{2,1,0:T(8,128)(2,1)S(1)}, u32[]{:S(2)}, u32[]{:S(2)}) %all-to-all-start) | async-done | bytes 2359328 | tf_op jit(solution)/shard_map/all_to_all | solution.py:418
  50.5 5.4 %pool_front.1 = (f32[32,32,128]{2,1,0:T(8,128)S(1)}, f32[32,32,128]{2,1,0:T(8,128)S(1)}, s32[5,64,128]{2,1,0:T(8,128)S(1)}, bf16[8192,256]{1,0:T(8,128)(2,1)S(1)}) custom-call(s32[2]{0:T(128)S(1)} %pad_add_fusion.place_ref, bf16[128,72,128]{2,1,0:T(8,128)(2,1)S(1)} %all-to-all-done.got_ref), custom_call_target="tpu_custom_call" | custom-call | flops 8589934592 | bytes 8388608 | tf_op jit(solution)/shard_map/pool_front/pallas_call | solution.py:269
  55.9 1.0 collective-permute-start
  56.9 1.2 %pool_side.1 = (f32[8,32,128]{2,1,0:T(8,128)S(1)}, f32[8,32,128]{2,1,0:T(8,128)S(1)}) custom-call(bf16[8192,256]{1,0:T(8,128)(2,1)S(1)} %get-tuple-element.22.rhs_ref, s32[5,64,128]{2,1,0:T(8,128)S(1)} %get-tuple-element.23.labels_ref), custom_call_target="tpu_custom_call" | custom-call | flops 2147483648 | bytes 2097152 | tf_op jit(solution)/shard_map/pool_side/pallas_call | solution.py:269
  58.1 0.0 copy-start
  58.2 0.0 copy-start.2
  58.2 0.0 copy-start.3
  58.2 0.2 collective-permute-done.got_ref
  58.4 0.8 pair_sum.2
  59.3 0.8 collective-permute-start.1
  60.1 4.1 %all-to-all-start.1 = ((f32[8,128,128]{2,1,0:T(8,128)}), f32[8,128,128]{2,1,0:T(8,128)S(1)}, u32[]{:S(2)}, u32[]{:S(2)}) async-start(f32[8,128,128]{2,1,0:T(8,128)} %bitcast.4), calls=%async_computation.1 | async-start | bytes 1048576 | tf_op jit(solution)/shard_map/all_to_all | solution.py:387
  64.2 0.9 collective-permute-done.1.got_ref
  65.1 0.0 copy-start.1
  65.1 1.7 %collective-permute-start.4 = (f32[8,32,128]{2,1,0:T(8,128)S(1)}, f32[8,32,128]{2,1,0:T(8,128)S(1)}, u32[]{:S(2)}, u32[]{:S(2)}) collective-permute-start(f32[8,32,128]{2,1,0:T(8,128)S(1)} %pair_sum.3), channel_id=1, source_target_pairs={{0,48},{16,32},{32,16},{48,0},{64,112},{80,96},{96,80},{112,64},{1... | collective-permute-start | bytes 393224 | tf_op jit(solution)/shard_map/ppermute | solution.py:376
  66.7 0.1 collective-permute-start.3
  66.8 3.0 %collective-permute-start.2 = (f32[8,32,128]{2,1,0:T(8,128)S(1)}, f32[8,32,128]{2,1,0:T(8,128)S(1)}, u32[]{:S(2)}, u32[]{:S(2)}) collective-permute-start(f32[8,32,128]{2,1,0:T(8,128)S(1)} %pair_sum.3), channel_id=1, source_target_pairs={{0,32},{16,48},{32,0},{48,16},{64,96},{80,112},{96,64},{112,80},{1... | collective-permute-start | bytes 393224 | tf_op jit(solution)/shard_map/ppermute | solution.py:376
  69.9 2.1 %collective-permute-done.4 = f32[8,32,128]{2,1,0:T(8,128)S(1)} collective-permute-done((f32[8,32,128]{2,1,0:T(8,128)S(1)}, f32[8,32,128]{2,1,0:T(8,128)S(1)}, u32[]{:S(2)}, u32[]{:S(2)}) %collective-permute-start.4) | collective-permute-done | bytes 131104 | tf_op jit(solution)/shard_map/ppermute | solution.py:376
  71.9 0.7 collective-permute-done.3
  72.6 2.7 %collective-permute-done.2 = f32[8,32,128]{2,1,0:T(8,128)S(1)} collective-permute-done((f32[8,32,128]{2,1,0:T(8,128)S(1)}, f32[8,32,128]{2,1,0:T(8,128)S(1)}, u32[]{:S(2)}, u32[]{:S(2)}) %collective-permute-start.2) | collective-permute-done | bytes 131104 | tf_op jit(solution)/shard_map/ppermute | solution.py:376
  75.4 0.0 all-to-all-done.1.pieces_ref
  75.4 0.7 spread.1
  76.1 6.2 %all-to-all-start.2 = ((bf16[8,128,128]{2,1,0:T(8,128)(2,1)}), bf16[8,128,128]{2,1,0:T(8,128)(2,1)S(1)}, u32[]{:S(2)}, u32[]{:S(2)}) async-start(bf16[8,128,128]{2,1,0:T(8,128)(2,1)} %spread.1), calls=%async_computation.2 | async-start | bytes 524288 | tf_op jit(solution)/shard_map/all_to_all | solution.py:392
  82.3 0.9 collective-permute-start.5
  83.3 2.5 %pool_top.1.top_ref = bf16[64,16,128]{2,1,0:T(8,128)(2,1)S(1)} custom-call(bf16[128,72,128]{2,1,0:T(8,128)(2,1)S(1)} %all-to-all-done.got_ref, s32[5,64,128]{2,1,0:T(8,128)S(1)} %get-tuple-element.23.labels_ref), custom_call_target="tpu_custom_call" | custom-call | flops 1024 | bytes 1 | tf_op jit(solution)/shard_map/pool_top/pallas_call | solution.py:269
  85.8 1.2 %collective-permute-done.5.far_ref = bf16[8,32,128]{2,1,0:T(8,128)(2,1)S(1)} collective-permute-done((bf16[8,32,128]{2,1,0:T(8,128)(2,1)S(1)}, bf16[8,32,128]{2,1,0:T(8,128)(2,1)S(1)}, u32[]{:S(2)}, u32[]{:S(2)}) %collective-permute-start.5) | collective-permute-done | bytes 65568 | tf_op jit(solution)/shard_map/ppermute | solution.py:376
  87.0 3.7 %all-to-all-done.2 = bf16[8,128,128]{2,1,0:T(8,128)(2,1)S(1)} async-done(((bf16[8,128,128]{2,1,0:T(8,128)(2,1)}), bf16[8,128,128]{2,1,0:T(8,128)(2,1)S(1)}, u32[]{:S(2)}, u32[]{:S(2)}) %all-to-all-start.2) | async-done | bytes 262176 | tf_op jit(solution)/shard_map/all_to_all | solution.py:392
  90.8 0.0 collective-permute-start.6
  90.8 1.5 %collective-permute-done.6.other_ref = bf16[32,32,128]{2,1,0:T(8,128)(2,1)S(1)} collective-permute-done((bf16[32,32,128]{2,1,0:T(8,128)(2,1)S(1)}, bf16[32,32,128]{2,1,0:T(8,128)(2,1)S(1)}, u32[]{:S(2)}, u32[]{:S(2)}) %collective-permute-start.6) | collective-permute-done | bytes 262176 | tf_op jit(solution)/shard_map/ppermute | solution.py:376
  92.3 0.0 copy-done
  92.3 0.0 copy-done.2
  92.3 0.0 copy-done.3
  92.3 0.0 copy-done.1
  92.3 10.5 %voxel_mlp.1 = bf16[64,16,32,128]{3,2,1,0:T(8,128)(2,1)} custom-call(s32[2]{0:T(128)S(1)} %pad_add_fusion.place_ref, bf16[64,16,128]{2,1,0:T(8,128)(2,1)S(1)} %pool_top.1.top_ref, bf16[32,32,128]{2,1,0:T(8,128)(2,1)S(1)} %bitcast.9, bf16[32,32,128]{2,1,0:T(8,128)(2,1)S(1)} %collective-permute-done.6.other_ref, ...), custom_call_target="tpu_custom_call" | custom-call | flops 4294967296 | bytes 9437184 | tf_op jit(solution)/shard_map/voxel_mlp/pallas_call | solution.py:352
  (2 shorter events, 0.1 us)
Async XLA Ops:
  8.1 42.4 %all-to-all-start = ((bf16[128,72,128]{2,1,0:T(8,128)(2,1)}), bf16[128,72,128]{2,1,0:T(8,128)(2,1)S(1)}, u32[]{:S(2)}, u32[]{:S(2)}) async-start(bf16[128,72,128]{2,1,0:T(8,128)(2,1)} %pack.1), calls=%async_computation | async-start | bytes 4718592 | tf_op jit(solution)/shard_map/all_to_all | solution.py:418
  55.9 2.5 %collective-permute-start = (f32[32,32,128]{2,1,0:T(8,128)S(1)}, f32[32,32,128]{2,1,0:T(8,128)S(1)}, u32[]{:S(2)}, u32[]{:S(2)}) collective-permute-start(f32[32,32,128]{2,1,0:T(8,128)S(1)} %get-tuple-element.21), channel_id=1, source_target_pairs={{0,1},{1,0},{2,3},{3,2},{4,5},{5,4},{6,7},{7,6},{8,9},{9,8},{10,11... | collective-permute-start | bytes 1572872 | tf_op jit(solution)/shard_map/ppermute | solution.py:376
  58.1 34.1 %copy-start = (bf16[128,256]{1,0:T(8,128)(2,1)S(1)}, bf16[128,256]{1,0:T(8,128)(2,1)}, u32[]{:S(2)}) copy-start(bf16[128,256]{1,0:T(8,128)(2,1)} %w_in_ref.1) | copy-start | bytes 196612
  58.2 34.1 %copy-start.2 = (f32[256]{0:T(256)S(1)}, f32[256]{0:T(256)}, u32[]{:S(2)}) copy-start(f32[256]{0:T(256)} %param.16) | copy-start | bytes 3076
  58.2 34.1 %copy-start.3 = (f32[128]{0:T(128)S(1)}, f32[128]{0:T(128)}, u32[]{:S(2)}) copy-start(f32[128]{0:T(128)} %param.18) | copy-start | bytes 1540
  59.3 5.8 %collective-permute-start.1 = (f32[8,32,128]{2,1,0:T(8,128)S(1)}, f32[8,32,128]{2,1,0:T(8,128)S(1)}, u32[]{:S(2)}, u32[]{:S(2)}) collective-permute-start(f32[8,32,128]{2,1,0:T(8,128)S(1)} %get-tuple-element.28), channel_id=1, source_target_pairs={{0,64},{16,80},{32,96},{48,112},{64,0},{80,16},{96,32},{112,48},{1... | collective-permute-start | bytes 393224 | tf_op jit(solution)/shard_map/ppermute | solution.py:376
  60.1 15.2 %all-to-all-start.1 = ((f32[8,128,128]{2,1,0:T(8,128)}), f32[8,128,128]{2,1,0:T(8,128)S(1)}, u32[]{:S(2)}, u32[]{:S(2)}) async-start(f32[8,128,128]{2,1,0:T(8,128)} %bitcast.4), calls=%async_computation.1 | async-start | bytes 1048576 | tf_op jit(solution)/shard_map/all_to_all | solution.py:387
  65.1 27.3 %copy-start.1 = (bf16[256,128]{1,0:T(8,128)(2,1)S(1)}, bf16[256,128]{1,0:T(8,128)(2,1)}, u32[]{:S(2)}) copy-start(bf16[256,128]{1,0:T(8,128)(2,1)} %w_out_ref.1) | copy-start | bytes 196612
  65.1 6.8 %collective-permute-start.4 = (f32[8,32,128]{2,1,0:T(8,128)S(1)}, f32[8,32,128]{2,1,0:T(8,128)S(1)}, u32[]{:S(2)}, u32[]{:S(2)}) collective-permute-start(f32[8,32,128]{2,1,0:T(8,128)S(1)} %pair_sum.3), channel_id=1, source_target_pairs={{0,48},{16,32},{32,16},{48,0},{64,112},{80,96},{96,80},{112,64},{1... | collective-permute-start | bytes 393224 | tf_op jit(solution)/shard_map/ppermute | solution.py:376
  66.7 5.8 %collective-permute-start.3 = (f32[8,32,128]{2,1,0:T(8,128)S(1)}, f32[8,32,128]{2,1,0:T(8,128)S(1)}, u32[]{:S(2)}, u32[]{:S(2)}) collective-permute-start(f32[8,32,128]{2,1,0:T(8,128)S(1)} %pair_sum.3), channel_id=1, source_target_pairs={{0,16},{16,0},{32,48},{48,32},{64,80},{80,64},{96,112},{112,96},{1... | collective-permute-start | bytes 393224 | tf_op jit(solution)/shard_map/ppermute | solution.py:376
  66.8 8.5 %collective-permute-start.2 = (f32[8,32,128]{2,1,0:T(8,128)S(1)}, f32[8,32,128]{2,1,0:T(8,128)S(1)}, u32[]{:S(2)}, u32[]{:S(2)}) collective-permute-start(f32[8,32,128]{2,1,0:T(8,128)S(1)} %pair_sum.3), channel_id=1, source_target_pairs={{0,32},{16,48},{32,0},{48,16},{64,96},{80,112},{96,64},{112,80},{1... | collective-permute-start | bytes 393224 | tf_op jit(solution)/shard_map/ppermute | solution.py:376
  76.1 14.6 %all-to-all-start.2 = ((bf16[8,128,128]{2,1,0:T(8,128)(2,1)}), bf16[8,128,128]{2,1,0:T(8,128)(2,1)S(1)}, u32[]{:S(2)}, u32[]{:S(2)}) async-start(bf16[8,128,128]{2,1,0:T(8,128)(2,1)} %spread.1), calls=%async_computation.2 | async-start | bytes 524288 | tf_op jit(solution)/shard_map/all_to_all | solution.py:392
  82.3 4.7 %collective-permute-start.5 = (bf16[8,32,128]{2,1,0:T(8,128)(2,1)S(1)}, bf16[8,32,128]{2,1,0:T(8,128)(2,1)S(1)}, u32[]{:S(2)}, u32[]{:S(2)}) collective-permute-start(bf16[8,32,128]{2,1,0:T(8,128)(2,1)S(1)} %add_convert_fusion.near_ref), channel_id=1, source_target_pairs={{0,64},{16,80},{32,96},{48,112},{64,0},{80,16},{96,32},{112,48},{1... | collective-permute-start | bytes 196616 | tf_op jit(solution)/shard_map/ppermute | solution.py:376
  90.8 1.5 %collective-permute-start.6 = (bf16[32,32,128]{2,1,0:T(8,128)(2,1)S(1)}, bf16[32,32,128]{2,1,0:T(8,128)(2,1)S(1)}, u32[]{:S(2)}, u32[]{:S(2)}) collective-permute-start(bf16[32,32,128]{2,1,0:T(8,128)(2,1)S(1)} %bitcast.8), channel_id=1, source_target_pairs={{0,1},{1,0},{2,3},{3,2},{4,5},{5,4},{6,7},{7,6},{8,9},{9,8},{10,11... | collective-permute-start | bytes 786440 | tf_op jit(solution)/shard_map/ppermute | solution.py:376

commit v8 on v7

--- a/solution.py
+++ b/solution.py
@@ -418,8 +418,8 @@
     got = lax.all_to_all(sent, ("gx", "gy"), split_axis=0, concat_axis=0, tiled=True)
     mine, other, labels, points = pool_front(place, got)
     keep, send = pool_side(points, labels)
-    mine = pair_sum(mine, swap(other, "gy", N_GY, 1))
-    mine, keep, send = lax.optimization_barrier((mine, keep, send))
+    mine, other, keep, send = lax.optimization_barrier((mine, swap(other, "gy", N_GY, 1), keep, send))
+    mine = pair_sum(mine, other)
     top = pool_top(got, labels)
     front, near = lax.optimization_barrier((front_share(mine), side_near(keep, send)))
     mine = front_gather(front)

time: 104 us -> 104 us (level)
  no operation moved by 1% of the time
where the time goes in v8:
time: 104 us; the launch traced here: 103 us
  waiting for transfers between devices  44.1 us (42%)
  starting transfers between devices  29.1 us (28%)
  Pallas kernels  28.7 us (28%)
    all_to_all x1, waiting for transfers between devices, per_device(): lax.all_to_all(sent, ('gx', 'gy'), split_axis=0, concat_axis=0, tiled=True)  31.2 us
    all_to_all x1, starting transfers between devices, per_device(): lax.all_to_all(sent, ('gx', 'gy'), split_axis=0, concat_axis=0, tiled=True)  11.2 us
    pallas_call x6, Pallas kernels, call(): pl.pallas_call(kernel, out_shape=outs, in_specs=[small if i.dtype == jnp....  10.8 us
    pallas_call x1, Pallas kernels, mlp(): pl.pallas_call(mlp_kernel, in_specs=[pl.BlockSpec(memory_space=pltpu.SMEM...  10.5 us
    ppermute x7, waiting for transfers between devices, swap(): return lax.ppermute(array, axis, [(i, i ^ bit) for i in range(size)])  8.62 us
    ppermute x7, starting transfers between devices, swap(): return lax.ppermute(array, axis, [(i, i ^ bit) for i in range(size)])  7.54 us
    pallas_call x1, Pallas kernels, pack(): pl.pallas_call(pack_kernel, out_shape=jax.ShapeDtypeStruct((DEVICES, ROWS...  7.44 us
    all_to_all x1, starting transfers between devices, front_gather(): lax.all_to_all(copies, 'gy', 0, 0, tiled=True, axis_index_groups=SAME_CORE)  6.37 us
  transfers between devices with their start and end apart: 10, of which 9 were waited for; matrix products, arithmetic and copies ran while one was open for 0% of the time, Pallas kernels for 4%

profile of v8, /device:TPU:0, one launch (start us, length us, event | category | flops | bytes accessed | tf_op | source)
XLA Modules:
  0.0 103.0 jit_solution(9329467800288996231)
XLA Ops:
  0.7 7.4 %pack.1 = bf16[128,72,128]{2,1,0:T(8,128)(2,1)} custom-call(s32[1]{0:T(128)S(6)} %copy.10.cam_ref, bf16[4096,128]{1,0:T(8,128)(2,1)} %feats_hbm.1, s32[32,128]{1,0:T(8,128)} %bitcast.12, s32[32,128]{1,0:T(8,128)} %bitcast.13, f32[6,128]{1,0:T(8,128)} %embed_hbm.1), custom_call_target="tpu_custom_call" | custom-call | flops 8589934592 | bytes 4194304 | tf_op jit(solution)/shard_map/pack/pallas_call | solution.py:188
  8.1 11.2 %all-to-all-start = ((bf16[128,72,128]{2,1,0:T(8,128)(2,1)}), bf16[128,72,128]{2,1,0:T(8,128)(2,1)S(1)}, u32[]{:S(2)}, u32[]{:S(2)}) async-start(bf16[128,72,128]{2,1,0:T(8,128)(2,1)} %pack.1), calls=%async_computation | async-start | bytes 4718592 | tf_op jit(solution)/shard_map/all_to_all | solution.py:418
  19.3 0.1 pad_add_fusion.place_ref
  19.3 31.2 %all-to-all-done.got_ref = bf16[128,72,128]{2,1,0:T(8,128)(2,1)S(1)} async-done(((bf16[128,72,128]{2,1,0:T(8,128)(2,1)}), bf16[128,72,128]{2,1,0:T(8,128)(2,1)S(1)}, u32[]{:S(2)}, u32[]{:S(2)}) %all-to-all-start) | async-done | bytes 2359328 | tf_op jit(solution)/shard_map/all_to_all | solution.py:418
  50.5 5.4 %pool_front.1 = (f32[32,32,128]{2,1,0:T(8,128)S(1)}, f32[32,32,128]{2,1,0:T(8,128)S(1)}, s32[5,64,128]{2,1,0:T(8,128)S(1)}, bf16[8192,256]{1,0:T(8,128)(2,1)S(1)}) custom-call(s32[2]{0:T(128)S(1)} %pad_add_fusion.place_ref, bf16[128,72,128]{2,1,0:T(8,128)(2,1)S(1)} %all-to-all-done.got_ref), custom_call_target="tpu_custom_call" | custom-call | flops 8589934592 | bytes 8388608 | tf_op jit(solution)/shard_map/pool_front/pallas_call | solution.py:269
  55.9 1.0 collective-permute-start
  56.9 1.2 %pool_side.1 = (f32[8,32,128]{2,1,0:T(8,128)S(1)}, f32[8,32,128]{2,1,0:T(8,128)S(1)}) custom-call(bf16[8192,256]{1,0:T(8,128)(2,1)S(1)} %get-tuple-element.23.rhs_ref, s32[5,64,128]{2,1,0:T(8,128)S(1)} %get-tuple-element.24.labels_ref), custom_call_target="tpu_custom_call" | custom-call | flops 2147483648 | bytes 2097152 | tf_op jit(solution)/shard_map/pool_side/pallas_call | solution.py:269
  58.1 0.0 copy-start
  58.2 0.0 copy-start.2
  58.2 0.0 copy-start.3
  58.2 0.2 collective-permute-done.got_ref
  58.4 0.8 collective-permute-start.1
  59.3 0.8 pair_sum.2
  60.1 4.1 %all-to-all-start.1 = ((f32[8,128,128]{2,1,0:T(8,128)}), f32[8,128,128]{2,1,0:T(8,128)S(1)}, u32[]{:S(2)}, u32[]{:S(2)}) async-start(f32[8,128,128]{2,1,0:T(8,128)} %bitcast.4), calls=%async_computation.1 | async-start | bytes 1048576 | tf_op jit(solution)/shard_map/all_to_all | solution.py:387
  64.2 0.0 collective-permute-done.1.got_ref
  64.2 0.0 copy-start.1
  64.2 2.2 %collective-permute-start.4 = (f32[8,32,128]{2,1,0:T(8,128)S(1)}, f32[8,32,128]{2,1,0:T(8,128)S(1)}, u32[]{:S(2)}, u32[]{:S(2)}) collective-permute-start(f32[8,32,128]{2,1,0:T(8,128)S(1)} %pair_sum.3), channel_id=1, source_target_pairs={{0,48},{16,32},{32,16},{48,0},{64,112},{80,96},{96,80},{112,64},{1... | collective-permute-start | bytes 393224 | tf_op jit(solution)/shard_map/ppermute | solution.py:376
  66.4 0.0 collective-permute-start.3
  66.4 2.6 %collective-permute-start.2 = (f32[8,32,128]{2,1,0:T(8,128)S(1)}, f32[8,32,128]{2,1,0:T(8,128)S(1)}, u32[]{:S(2)}, u32[]{:S(2)}) collective-permute-start(f32[8,32,128]{2,1,0:T(8,128)S(1)} %pair_sum.3), channel_id=1, source_target_pairs={{0,32},{16,48},{32,0},{48,16},{64,96},{80,112},{96,64},{112,80},{1... | collective-permute-start | bytes 393224 | tf_op jit(solution)/shard_map/ppermute | solution.py:376
  69.0 2.0 %collective-permute-done.4 = f32[8,32,128]{2,1,0:T(8,128)S(1)} collective-permute-done((f32[8,32,128]{2,1,0:T(8,128)S(1)}, f32[8,32,128]{2,1,0:T(8,128)S(1)}, u32[]{:S(2)}, u32[]{:S(2)}) %collective-permute-start.4) | collective-permute-done | bytes 131104 | tf_op jit(solution)/shard_map/ppermute | solution.py:376
  71.1 1.5 %collective-permute-done.3 = f32[8,32,128]{2,1,0:T(8,128)S(1)} collective-permute-done((f32[8,32,128]{2,1,0:T(8,128)S(1)}, f32[8,32,128]{2,1,0:T(8,128)S(1)}, u32[]{:S(2)}, u32[]{:S(2)}) %collective-permute-start.3) | collective-permute-done | bytes 131104 | tf_op jit(solution)/shard_map/ppermute | solution.py:376
  72.5 2.1 %collective-permute-done.2 = f32[8,32,128]{2,1,0:T(8,128)S(1)} collective-permute-done((f32[8,32,128]{2,1,0:T(8,128)S(1)}, f32[8,32,128]{2,1,0:T(8,128)S(1)}, u32[]{:S(2)}, u32[]{:S(2)}) %collective-permute-start.2) | collective-permute-done | bytes 131104 | tf_op jit(solution)/shard_map/ppermute | solution.py:376
  74.6 0.6 all-to-all-done.1.pieces_ref
  75.2 0.7 spread.1
  75.9 6.4 %all-to-all-start.2 = ((bf16[8,128,128]{2,1,0:T(8,128)(2,1)}), bf16[8,128,128]{2,1,0:T(8,128)(2,1)S(1)}, u32[]{:S(2)}, u32[]{:S(2)}) async-start(bf16[8,128,128]{2,1,0:T(8,128)(2,1)} %spread.1), calls=%async_computation.2 | async-start | bytes 524288 | tf_op jit(solution)/shard_map/all_to_all | solution.py:392
  82.3 0.9 collective-permute-start.5
  83.3 2.5 %pool_top.1.top_ref = bf16[64,16,128]{2,1,0:T(8,128)(2,1)S(1)} custom-call(bf16[128,72,128]{2,1,0:T(8,128)(2,1)S(1)} %all-to-all-done.got_ref, s32[5,64,128]{2,1,0:T(8,128)S(1)} %get-tuple-element.24.labels_ref), custom_call_target="tpu_custom_call" | custom-call | flops 1024 | bytes 1 | tf_op jit(solution)/shard_map/pool_top/pallas_call | solution.py:269
  85.8 1.2 %collective-permute-done.5.far_ref = bf16[8,32,128]{2,1,0:T(8,128)(2,1)S(1)} collective-permute-done((bf16[8,32,128]{2,1,0:T(8,128)(2,1)S(1)}, bf16[8,32,128]{2,1,0:T(8,128)(2,1)S(1)}, u32[]{:S(2)}, u32[]{:S(2)}) %collective-permute-start.5) | collective-permute-done | bytes 65568 | tf_op jit(solution)/shard_map/ppermute | solution.py:376
  87.0 3.7 %all-to-all-done.2 = bf16[8,128,128]{2,1,0:T(8,128)(2,1)S(1)} async-done(((bf16[8,128,128]{2,1,0:T(8,128)(2,1)}), bf16[8,128,128]{2,1,0:T(8,128)(2,1)S(1)}, u32[]{:S(2)}, u32[]{:S(2)}) %all-to-all-start.2) | async-done | bytes 262176 | tf_op jit(solution)/shard_map/all_to_all | solution.py:392
  90.8 0.0 collective-permute-start.6
  90.8 1.5 %collective-permute-done.6.other_ref = bf16[32,32,128]{2,1,0:T(8,128)(2,1)S(1)} collective-permute-done((bf16[32,32,128]{2,1,0:T(8,128)(2,1)S(1)}, bf16[32,32,128]{2,1,0:T(8,128)(2,1)S(1)}, u32[]{:S(2)}, u32[]{:S(2)}) %collective-permute-start.6) | collective-permute-done | bytes 262176 | tf_op jit(solution)/shard_map/ppermute | solution.py:376
  92.3 0.0 copy-done
  92.3 0.0 copy-done.2
  92.3 0.0 copy-done.3
  92.3 0.0 copy-done.1
  92.3 10.5 %voxel_mlp.1 = bf16[64,16,32,128]{3,2,1,0:T(8,128)(2,1)} custom-call(s32[2]{0:T(128)S(1)} %pad_add_fusion.place_ref, bf16[64,16,128]{2,1,0:T(8,128)(2,1)S(1)} %pool_top.1.top_ref, bf16[32,32,128]{2,1,0:T(8,128)(2,1)S(1)} %bitcast.9, bf16[32,32,128]{2,1,0:T(8,128)(2,1)S(1)} %collective-permute-done.6.other_ref, ...), custom_call_target="tpu_custom_call" | custom-call | flops 4294967296 | bytes 9437184 | tf_op jit(solution)/shard_map/voxel_mlp/pallas_call | solution.py:352
  (2 shorter events, 0.1 us)
Async XLA Ops:
  8.1 42.4 %all-to-all-start = ((bf16[128,72,128]{2,1,0:T(8,128)(2,1)}), bf16[128,72,128]{2,1,0:T(8,128)(2,1)S(1)}, u32[]{:S(2)}, u32[]{:S(2)}) async-start(bf16[128,72,128]{2,1,0:T(8,128)(2,1)} %pack.1), calls=%async_computation | async-start | bytes 4718592 | tf_op jit(solution)/shard_map/all_to_all | solution.py:418
  55.9 2.5 %collective-permute-start = (f32[32,32,128]{2,1,0:T(8,128)S(1)}, f32[32,32,128]{2,1,0:T(8,128)S(1)}, u32[]{:S(2)}, u32[]{:S(2)}) collective-permute-start(f32[32,32,128]{2,1,0:T(8,128)S(1)} %get-tuple-element.22), channel_id=1, source_target_pairs={{0,1},{1,0},{2,3},{3,2},{4,5},{5,4},{6,7},{7,6},{8,9},{9,8},{10,11... | collective-permute-start | bytes 1572872 | tf_op jit(solution)/shard_map/ppermute | solution.py:376
  58.1 34.1 %copy-start = (bf16[128,256]{1,0:T(8,128)(2,1)S(1)}, bf16[128,256]{1,0:T(8,128)(2,1)}, u32[]{:S(2)}) copy-start(bf16[128,256]{1,0:T(8,128)(2,1)} %w_in_ref.1) | copy-start | bytes 196612
  58.2 34.1 %copy-start.2 = (f32[256]{0:T(256)S(1)}, f32[256]{0:T(256)}, u32[]{:S(2)}) copy-start(f32[256]{0:T(256)} %param.16) | copy-start | bytes 3076
  58.2 34.1 %copy-start.3 = (f32[128]{0:T(128)S(1)}, f32[128]{0:T(128)}, u32[]{:S(2)}) copy-start(f32[128]{0:T(128)} %param.18) | copy-start | bytes 1540
  58.4 5.8 %collective-permute-start.1 = (f32[8,32,128]{2,1,0:T(8,128)S(1)}, f32[8,32,128]{2,1,0:T(8,128)S(1)}, u32[]{:S(2)}, u32[]{:S(2)}) collective-permute-start(f32[8,32,128]{2,1,0:T(8,128)S(1)} %get-tuple-element.30), channel_id=1, source_target_pairs={{0,64},{16,80},{32,96},{48,112},{64,0},{80,16},{96,32},{112,48},{1... | collective-permute-start | bytes 393224 | tf_op jit(solution)/shard_map/ppermute | solution.py:376
  60.1 15.1 %all-to-all-start.1 = ((f32[8,128,128]{2,1,0:T(8,128)}), f32[8,128,128]{2,1,0:T(8,128)S(1)}, u32[]{:S(2)}, u32[]{:S(2)}) async-start(f32[8,128,128]{2,1,0:T(8,128)} %bitcast.4), calls=%async_computation.1 | async-start | bytes 1048576 | tf_op jit(solution)/shard_map/all_to_all | solution.py:387
  64.2 28.1 %copy-start.1 = (bf16[256,128]{1,0:T(8,128)(2,1)S(1)}, bf16[256,128]{1,0:T(8,128)(2,1)}, u32[]{:S(2)}) copy-start(bf16[256,128]{1,0:T(8,128)(2,1)} %w_out_ref.1) | copy-start | bytes 196612
  64.2 6.8 %collective-permute-start.4 = (f32[8,32,128]{2,1,0:T(8,128)S(1)}, f32[8,32,128]{2,1,0:T(8,128)S(1)}, u32[]{:S(2)}, u32[]{:S(2)}) collective-permute-start(f32[8,32,128]{2,1,0:T(8,128)S(1)} %pair_sum.3), channel_id=1, source_target_pairs={{0,48},{16,32},{32,16},{48,0},{64,112},{80,96},{96,80},{112,64},{1... | collective-permute-start | bytes 393224 | tf_op jit(solution)/shard_map/ppermute | solution.py:376
  66.4 6.1 %collective-permute-start.3 = (f32[8,32,128]{2,1,0:T(8,128)S(1)}, f32[8,32,128]{2,1,0:T(8,128)S(1)}, u32[]{:S(2)}, u32[]{:S(2)}) collective-permute-start(f32[8,32,128]{2,1,0:T(8,128)S(1)} %pair_sum.3), channel_id=1, source_target_pairs={{0,16},{16,0},{32,48},{48,32},{64,80},{80,64},{96,112},{112,96},{1... | collective-permute-start | bytes 393224 | tf_op jit(solution)/shard_map/ppermute | solution.py:376
  66.4 8.2 %collective-permute-start.2 = (f32[8,32,128]{2,1,0:T(8,128)S(1)}, f32[8,32,128]{2,1,0:T(8,128)S(1)}, u32[]{:S(2)}, u32[]{:S(2)}) collective-permute-start(f32[8,32,128]{2,1,0:T(8,128)S(1)} %pair_sum.3), channel_id=1, source_target_pairs={{0,32},{16,48},{32,0},{48,16},{64,96},{80,112},{96,64},{112,80},{1... | collective-permute-start | bytes 393224 | tf_op jit(solution)/shard_map/ppermute | solution.py:376
  75.9 14.8 %all-to-all-start.2 = ((bf16[8,128,128]{2,1,0:T(8,128)(2,1)}), bf16[8,128,128]{2,1,0:T(8,128)(2,1)S(1)}, u32[]{:S(2)}, u32[]{:S(2)}) async-start(bf16[8,128,128]{2,1,0:T(8,128)(2,1)} %spread.1), calls=%async_computation.2 | async-start | bytes 524288 | tf_op jit(solution)/shard_map/all_to_all | solution.py:392
  82.3 4.7 %collective-permute-start.5 = (bf16[8,32,128]{2,1,0:T(8,128)(2,1)S(1)}, bf16[8,32,128]{2,1,0:T(8,128)(2,1)S(1)}, u32[]{:S(2)}, u32[]{:S(2)}) collective-permute-start(bf16[8,32,128]{2,1,0:T(8,128)(2,1)S(1)} %add_convert_fusion.near_ref), channel_id=1, source_target_pairs={{0,64},{16,80},{32,96},{48,112},{64,0},{80,16},{96,32},{112,48},{1... | collective-permute-start | bytes 196616 | tf_op jit(solution)/shard_map/ppermute | solution.py:376
  90.8 1.5 %collective-permute-start.6 = (bf16[32,32,128]{2,1,0:T(8,128)(2,1)S(1)}, bf16[32,32,128]{2,1,0:T(8,128)(2,1)S(1)}, u32[]{:S(2)}, u32[]{:S(2)}) collective-permute-start(bf16[32,32,128]{2,1,0:T(8,128)(2,1)S(1)} %bitcast.8), channel_id=1, source_target_pairs={{0,1},{1,0},{2,3},{3,2},{4,5},{5,4},{6,7},{7,6},{8,9},{9,8},{10,11... | collective-permute-start | bytes 786440 | tf_op jit(solution)/shard_map/ppermute | solution.py:376
